TPU v7x, 32 devices: a whole 2x2x4 slice. The times are simulated.
32 devices in a mesh: gx: 8 (over y, x, core), gy: 4 (over z).
Axes of the slice: x: 2, y: 2, z: 4, core: 2. Of those that a mesh axis runs over, the one named last changes fastest.
Arguments:
- pressure: float32 [128, 24576], P('gx', 'gy'), may hold values from -6 to 6
- previous: float32 [128, 24576], P('gx', 'gy'), may hold values from -6 to 6
- velocity: bfloat16 [128, 24576], P('gx', 'gy'), may hold values from 0.039794922 to 0.19921875
- tucker_core: bfloat16 [3, 384, 12288], P(None, 'gx', 'gy'), may hold values from -6 to 6
- first_factor: bfloat16 [128, 384], P('gx'), may hold values from -0.3125 to 0.3125
- second_factor: bfloat16 [384, 384], P('gy'), may hold values from -0.3125 to 0.3125
- depth_factor: bfloat16 [64, 32], replicated, may hold values from -1 to 1
Outputs:
- image: float32 [128, 24576], P('gx', 'gy')
All inputs are finite; a program needn't handle non-finite values.
Results may differ from a plain program's by a relative error of at most 0.00035.
Values may be sent and summed in bfloat16 or wider, within the bound.
No kernel may reach another device: no remote copies, remote signals or barrier semaphores. Data moves between devices by JAX's collectives and lax.ppermute only.
A program may use at most 192 MiB of HBM per device.

v0:
```python
import jax
import jax.numpy as jnp
from jax import lax
from jax.sharding import PartitionSpec as P

STENCIL = (-205.0 / 72.0, 8.0 / 5.0, -1.0 / 5.0, 8.0 / 315.0, -1.0 / 560.0)
HIGH = lax.Precision.HIGHEST


def with_halo(cells, sides, width):
    for axis, dim in sides:
        count = lax.axis_size(axis)
        ends = count - 1
        head = lax.slice_in_dim(cells, 0, width, axis=dim)
        tail = lax.slice_in_dim(cells, cells.shape[dim] - width, cells.shape[dim], axis=dim)
        cells = jnp.concatenate(
            [
                lax.ppermute(tail, axis, [(i, (i + 1) % count) for i in range(ends)]),
                cells,
                lax.ppermute(head, axis, [((i + 1) % count, i) for i in range(ends)]),
            ],
            axis=dim,
        )
    return cells


def laplace(field, depth_cells):
    lines, flat = field.shape
    margin = 4 * depth_cells
    wide_rows = with_halo(field, (("gx", 0),), 4)
    wide_cols = with_halo(field, (("gy", 1),), margin)
    level = lax.broadcasted_iota(jnp.int32, (1, flat), 1) % depth_cells
    blank = jnp.zeros_like(field)
    total = 3.0 * STENCIL[0] * field
    for reach in range(1, 5):
        near = wide_rows[4 + reach : 4 + reach + lines] + wide_rows[4 - reach : 4 - reach + lines]
        lift = reach * depth_cells
        near = (
            near
            + wide_cols[:, margin + lift : margin + lift + flat]
            + wide_cols[:, margin - lift : margin - lift + flat]
        )
        deeper = jnp.concatenate([field[:, reach:], blank[:, :reach]], axis=1)
        higher = jnp.concatenate([blank[:, :reach], field[:, : flat - reach]], axis=1)
        near = (
            near
            + jnp.where(level + reach < depth_cells, deeper, 0.0)
            + jnp.where(level >= reach, higher, 0.0)
        )
        total = total + STENCIL[reach] * near
    return total


def expand(blocks, first_factor, second_factor, depth_factor):
    count, rows_first, rows_second, rank_depth = blocks.shape
    cells_x = first_factor.shape[0]
    cells_y = second_factor.shape[0]
    columns = first_factor
    partial_value = jnp.einsum(
        "xr,srnc->sxnc",
        columns,
        lax.all_gather(blocks, "gx", axis=1, tiled=True),
        preferred_element_type=jnp.float32,
    )
    columns = second_factor.astype(jnp.float32)
    mixed = jnp.einsum(
        "yn,sxnc->sxyc",
        columns,
        lax.all_gather(partial_value, "gy", axis=2, tiled=True),
        precision=HIGH,
    )
    field = jnp.einsum("sxyc,zc->sxyz", mixed, depth_factor.astype(jnp.float32), precision=HIGH)
    return field.reshape(count, cells_x, cells_y * depth_factor.shape[0])


def body(pressure, previous, velocity, tucker_core, first_factor, second_factor, depth_factor):
    depth_cells = depth_factor.shape[0]
    rank_depth = depth_factor.shape[1]
    steps_all = tucker_core.shape[0]
    local_second = tucker_core.shape[2] // rank_depth
    core_blocks = tucker_core.reshape(steps_all, tucker_core.shape[1], local_second, rank_depth)
    speed = velocity.astype(jnp.float32)
    group = 1
    current = pressure
    before = previous
    image = jnp.zeros(pressure.shape, jnp.float32)
    sources = None
    for section in range(steps_all):
        sources = expand(
            core_blocks[section : section + group], first_factor, second_factor, depth_factor
        )
        following = 2.0 * current - before + speed * laplace(current, depth_cells)
        image = image + sources[section % group] * following
        before = current
        current = following
    return image


def solution(mesh):
    placed = (
        P("gx", "gy"),
        P("gx", "gy"),
        P("gx", "gy"),
        P(None, "gx", "gy"),
        P("gx", None),
        P("gy", None),
        P(),
    )
    return jax.shard_map(body, mesh=mesh, in_specs=placed, out_specs=P("gx", "gy"), check_vma=False)
```

profile of v0, /device:TPU:0, one launch (start us, length us, event | category | flops | bytes accessed | tf_op | source)
XLA Modules:
  0.0 281.0 jit_solution(1032410224676475917)
XLA Ops:
  6.5 1.2 fusion.151
  7.8 0.9 slice.349
  8.7 1.1 copy.40
  9.9 0.9 slice.379
  10.8 1.1 copy.45
  12.0 0.6 fusion.169
  12.6 4.9 %collective-permute-start.3 = (f32[16,256]{1,0:T(8,128)}, f32[16,256]{1,0:T(8,128)S(1)}, u32[]{:S(2)}, u32[]{:S(2)}) collective-permute-start(f32[16,256]{1,0:T(8,128)} %get-tuple-element.46), channel_id=1, source_target_pairs={{0,1},{1,2},{2,3},{4,5},{5,6},{6,7},{8,9},{9,10},{10,11},{12,13},{... | collective-permute-start | bytes 49160 | tf_op jit(solution)/shard_map/ppermute | solution.py:18
  17.6 1.3 collective-permute-start
  18.9 1.3 collective-permute-start.2
  20.2 3.0 %collective-permute-start.1 = (f32[4,6144]{1,0:T(4,128)S(1)}, f32[4,6144]{1,0:T(4,128)S(1)}, u32[]{:S(2)}, u32[]{:S(2)}) collective-permute-start(f32[4,6144]{1,0:T(4,128)S(1)} %get-tuple-element.41), channel_id=1, source_target_pairs={{0,4},{4,8},{8,12},{12,16},{16,20},{20,24},{24,28},{1,5},{5,9},{9,... | collective-permute-start | bytes 294920 | tf_op jit(solution)/shard_map/ppermute | solution.py:18
  23.2 0.9 slice.319
  24.1 1.1 copy.35
  26.8 1.2 fusion.18
  28.6 1.3 collective-permute-start.4
  29.9 3.6 %collective-permute-start.5 = (f32[4,6144]{1,0:T(4,128)S(1)}, f32[4,6144]{1,0:T(4,128)S(1)}, u32[]{:S(2)}, u32[]{:S(2)}) collective-permute-start(f32[4,6144]{1,0:T(4,128)S(1)} %get-tuple-element.29), channel_id=1, source_target_pairs={{0,4},{4,8},{8,12},{12,16},{16,20},{20,24},{24,28},{1,5},{5,9},{9,... | collective-permute-start | bytes 294920 | tf_op jit(solution)/shard_map/ppermute | solution.py:18
  33.5 1.3 collective-permute-start.6
  34.8 5.2 %collective-permute-start.7 = (f32[16,256]{1,0:T(8,128)S(1)}, f32[16,256]{1,0:T(8,128)S(1)}, u32[]{:S(2)}, u32[]{:S(2)}) collective-permute-start(f32[16,256]{1,0:T(8,128)S(1)} %get-tuple-element.31), channel_id=1, source_target_pairs={{0,1},{1,2},{2,3},{4,5},{5,6},{6,7},{8,9},{9,10},{10,11},{12,13},{... | collective-permute-start | bytes 49160 | tf_op jit(solution)/shard_map/ppermute | solution.py:18
  40.2 1.2 collective-permute-done.7
  41.4 1.9 fusion.19
  43.6 1.0 fusion.154
  44.6 0.7 fusion.156
  45.3 0.6 fusion.157
  45.9 1.3 collective-permute-start.8
  47.2 4.1 %collective-permute-start.9 = (f32[4,6144]{1,0:T(4,128)}, f32[4,6144]{1,0:T(4,128)}, u32[]{:S(2)}, u32[]{:S(2)}) collective-permute-start(f32[4,6144]{1,0:T(4,128)} %get-tuple-element.17), channel_id=1, source_target_pairs={{0,4},{4,8},{8,12},{12,16},{16,20},{20,24},{24,28},{1,5},{5,9},{9,... | collective-permute-start | bytes 294920 | tf_op jit(solution)/shard_map/ppermute | solution.py:18
  51.3 1.3 collective-permute-start.10
  52.6 4.9 %collective-permute-start.11 = (f32[16,256]{1,0:T(8,128)S(1)}, f32[16,256]{1,0:T(8,128)S(1)}, u32[]{:S(2)}, u32[]{:S(2)}) collective-permute-start(f32[16,256]{1,0:T(8,128)S(1)} %get-tuple-element.19), channel_id=1, source_target_pairs={{0,1},{1,2},{2,3},{4,5},{5,6},{6,7},{8,9},{9,10},{10,11},{12,13},{... | collective-permute-start | bytes 49160 | tf_op jit(solution)/shard_map/ppermute | solution.py:18
  57.5 1.0 fusion.155
  58.5 1.0 fusion.152
  59.5 5.4 %copy.41 = bf16[1,384,96,32]{1,3,2,0:T(8,128)(2,1)} copy(bf16[1,384,96,32]{2,3,0,1:T(8,128)(2,1)} %all-gather.6.cloned.1.call-done) | data formatting | bytes 4718592 | tf_op jit(solution)/shard_map/all_gather | solution.py:62
  65.0 3.8 %fusion.9 = f32[1,16,96,32]{3,1,0,2:T(8,128)S(1)} fusion(bf16[1,384,96,32]{1,3,2,0:T(8,128)(2,1)} %copy.41, bf16[16,384]{1,0:T(8,128)(2,1)S(1)} %copy-done.6), kind=kOutput, calls=%fused_computation.7 | convolution fusion | flops 37748736 | bytes 2568192 | tf_op jit(solution)/shard_map/xr,srnc->sxnc/dot_general | solution.py:59
  68.8 56.4 %all_gather.21 = f32[1,16,384,32]{3,1,0,2:T(8,128)} all-gather(f32[1,16,96,32]{3,1,0,2:T(8,128)S(1)} %fusion.9), channel_id=1, replica_groups=mesh['gx'=8,'gy'=4] {'gy'}, dimensions={2}, use_global_device_ids=true | all-gather | bytes 983040 | tf_op jit(solution)/shard_map/all_gather | solution.py:69
  125.1 2.3 copy.43
  127.5 5.3 %copy.46 = bf16[1,384,96,32]{1,3,2,0:T(8,128)(2,1)} copy(bf16[1,384,96,32]{2,3,0,1:T(8,128)(2,1)} %all-gather.8.cloned.1.call-done) | data formatting | bytes 4718592 | tf_op jit(solution)/shard_map/all_gather | solution.py:62
  132.8 3.8 %fusion.12 = f32[1,16,96,32]{3,1,0,2:T(8,128)S(1)} fusion(bf16[1,384,96,32]{1,3,2,0:T(8,128)(2,1)} %copy.46, bf16[16,384]{1,0:T(8,128)(2,1)S(1)} %copy-done.6), kind=kOutput, calls=%fused_computation.8 | convolution fusion | flops 37748736 | bytes 2568192 | tf_op jit(solution)/shard_map/xr,srnc->sxnc/dot_general | solution.py:59
  136.6 54.5 %all_gather.23 = f32[1,16,384,32]{3,1,0,2:T(8,128)} all-gather(f32[1,16,96,32]{3,1,0,2:T(8,128)S(1)} %fusion.12), channel_id=1, replica_groups=mesh['gx'=8,'gy'=4] {'gy'}, dimensions={2}, use_global_device_ids=true | all-gather | bytes 983040 | tf_op jit(solution)/shard_map/all_gather | solution.py:69
  191.1 2.3 copy.48
  194.0 0.8 fusion.147
  195.3 0.8 fusion.145
  196.1 5.4 %copy.36 = bf16[1,384,96,32]{1,3,2,0:T(8,128)(2,1)} copy(bf16[1,384,96,32]{2,3,0,1:T(8,128)(2,1)} %all-gather.4.cloned.1.call-done) | data formatting | bytes 4718592 | tf_op jit(solution)/shard_map/all_gather | solution.py:62
  201.5 3.8 %fusion.6 = f32[1,16,96,32]{3,1,0,2:T(8,128)S(1)} fusion(bf16[1,384,96,32]{1,3,2,0:T(8,128)(2,1)} %copy.36, bf16[16,384]{1,0:T(8,128)(2,1)S(1)} %copy-done.6), kind=kOutput, calls=%fused_computation.6 | convolution fusion | flops 37748736 | bytes 2568192 | tf_op jit(solution)/shard_map/xr,srnc->sxnc/dot_general | solution.py:59
  205.3 55.0 %all_gather.19 = f32[1,16,384,32]{3,1,0,2:T(8,128)} all-gather(f32[1,16,96,32]{3,1,0,2:T(8,128)S(1)} %fusion.6), channel_id=1, replica_groups=mesh['gx'=8,'gy'=4] {'gy'}, dimensions={2}, use_global_device_ids=true | all-gather | bytes 983040 | tf_op jit(solution)/shard_map/all_gather | solution.py:69
  260.2 3.1 %copy.38 = f32[1,16,384,32]{2,3,1,0:T(8,128)} copy(f32[1,16,384,32]{3,1,0,2:T(8,128)} %all_gather.19) | data formatting | bytes 1572864 | tf_op jit(solution)/shard_map/all_gather | solution.py:69
  263.3 1.6 convolution_bitcast_fusion.2
  264.9 1.7 fusion.149
  266.6 1.0 squeeze_reshape.10
  267.7 1.0 squeeze_reshape.11
  268.7 1.4 squeeze_reshape.9
  270.2 4.3 %fusion.22 = f32[16,6144]{1,0:T(8,128)} fusion(f32[16,6144]{1,0:T(8,128)} %squeeze_reshape.11, bf16[16,6144]{1,0:T(8,128)(2,1)S(1)} %copy-done.2, f32[16,6144]{1,0:T(8,128)S(1)} %fusion.19, f32[16,256]{1,0:T(8,128)S(1)} %collective-permute-done.11, f32[16,256]{1,0:T(8,128)S(1)} %collective-permute-done.10, f32[4,6144]{1,0:T(4,128)} %collective-permute-done.9, ...), kind=kLoop, calls=%fused_computation.64 | loop fusion | flops 6193152 | bytes 5978880 | tf_op jit(solution)/shard_map/add | solution.py:93
  (58 shorter events, 3.6 us)
Async XLA Ops:
  6.5 186.9 %copy-start = (bf16[96,384]{1,0:T(8,128)(2,1)S(1)}, bf16[96,384]{1,0:T(8,128)(2,1)}, u32[]{:S(2)}) copy-start(bf16[96,384]{1,0:T(8,128)(2,1)} %param.12) | copy-start | bytes 221188
  6.5 53.0 %all-gather.6.cloned.1.call-start = ((), (), s32[]{:S(2)}) async-start(), calls=%async_computation.1 | async-start | bytes 3538944 | tf_op jit(solution)/shard_map/all_gather | solution.py:62
  8.7 3.3 %copy-start.1 = (f32[16,6144]{1,0:T(8,128)S(1)}, f32[16,6144]{1,0:T(8,128)}, u32[]{:S(2)}) copy-start(f32[16,6144]{1,0:T(8,128)} %param.7) | copy-start | bytes 1179652
  9.8 117.6 %all-gather.8.cloned.1.call-start = ((), (), s32[]{:S(2)}) async-start(), calls=%async_computation.2 | async-start | bytes 3538944 | tf_op jit(solution)/shard_map/all_gather | solution.py:62
  11.9 184.2 %all-gather.4.cloned.1.call-start = ((), (), s32[]{:S(2)}) async-start(), calls=%async_computation | async-start | bytes 3538944 | tf_op jit(solution)/shard_map/all_gather | solution.py:62
  12.6 13.5 %collective-permute-start.3 = (f32[16,256]{1,0:T(8,128)}, f32[16,256]{1,0:T(8,128)S(1)}, u32[]{:S(2)}, u32[]{:S(2)}) collective-permute-start(f32[16,256]{1,0:T(8,128)} %get-tuple-element.46), channel_id=1, source_target_pairs={{0,1},{1,2},{2,3},{4,5},{5,6},{6,7},{8,9},{9,10},{10,11},{12,13},{... | collective-permute-start | bytes 49160 | tf_op jit(solution)/shard_map/ppermute | solution.py:18
  17.6 8.6 %collective-permute-start = (f32[4,6144]{1,0:T(4,128)S(1)}, f32[4,6144]{1,0:T(4,128)S(1)}, u32[]{:S(2)}, u32[]{:S(2)}) collective-permute-start(f32[4,6144]{1,0:T(4,128)S(1)} %get-tuple-element.40), channel_id=1, source_target_pairs={{4,0},{8,4},{12,8},{16,12},{20,16},{24,20},{28,24},{5,1},{9,5},{13... | collective-permute-start | bytes 294920 | tf_op jit(solution)/shard_map/ppermute | solution.py:20
  18.9 7.3 %collective-permute-start.2 = (f32[16,256]{1,0:T(8,128)S(1)}, f32[16,256]{1,0:T(8,128)S(1)}, u32[]{:S(2)}, u32[]{:S(2)}) collective-permute-start(f32[16,256]{1,0:T(8,128)S(1)} %get-tuple-element.45), channel_id=1, source_target_pairs={{1,0},{2,1},{3,2},{5,4},{6,5},{7,6},{9,8},{10,9},{11,10},{13,12},{... | collective-permute-start | bytes 49160 | tf_op jit(solution)/shard_map/ppermute | solution.py:20
  20.2 6.1 %collective-permute-start.1 = (f32[4,6144]{1,0:T(4,128)S(1)}, f32[4,6144]{1,0:T(4,128)S(1)}, u32[]{:S(2)}, u32[]{:S(2)}) collective-permute-start(f32[4,6144]{1,0:T(4,128)S(1)} %get-tuple-element.41), channel_id=1, source_target_pairs={{0,4},{4,8},{8,12},{12,16},{16,20},{20,24},{24,28},{1,5},{5,9},{9,... | collective-permute-start | bytes 294920 | tf_op jit(solution)/shard_map/ppermute | solution.py:18
  25.7 0.9 copy-start.2
  25.7 1.1 copy-start.5
  28.6 12.9 %collective-permute-start.4 = (f32[4,6144]{1,0:T(4,128)S(1)}, f32[4,6144]{1,0:T(4,128)S(1)}, u32[]{:S(2)}, u32[]{:S(2)}) collective-permute-start(f32[4,6144]{1,0:T(4,128)S(1)} %get-tuple-element.28), channel_id=1, source_target_pairs={{4,0},{8,4},{12,8},{16,12},{20,16},{24,20},{28,24},{5,1},{9,5},{13... | collective-permute-start | bytes 294920 | tf_op jit(solution)/shard_map/ppermute | solution.py:20
  29.9 11.6 %collective-permute-start.5 = (f32[4,6144]{1,0:T(4,128)S(1)}, f32[4,6144]{1,0:T(4,128)S(1)}, u32[]{:S(2)}, u32[]{:S(2)}) collective-permute-start(f32[4,6144]{1,0:T(4,128)S(1)} %get-tuple-element.29), channel_id=1, source_target_pairs={{0,4},{4,8},{8,12},{12,16},{16,20},{20,24},{24,28},{1,5},{5,9},{9,... | collective-permute-start | bytes 294920 | tf_op jit(solution)/shard_map/ppermute | solution.py:18
  33.5 6.7 %collective-permute-start.6 = (f32[16,256]{1,0:T(8,128)S(1)}, f32[16,256]{1,0:T(8,128)S(1)}, u32[]{:S(2)}, u32[]{:S(2)}) collective-permute-start(f32[16,256]{1,0:T(8,128)S(1)} %get-tuple-element.30), channel_id=1, source_target_pairs={{1,0},{2,1},{3,2},{5,4},{6,5},{7,6},{9,8},{10,9},{11,10},{13,12},{... | collective-permute-start | bytes 49160 | tf_op jit(solution)/shard_map/ppermute | solution.py:20
  34.8 6.6 %collective-permute-start.7 = (f32[16,256]{1,0:T(8,128)S(1)}, f32[16,256]{1,0:T(8,128)S(1)}, u32[]{:S(2)}, u32[]{:S(2)}) collective-permute-start(f32[16,256]{1,0:T(8,128)S(1)} %get-tuple-element.31), channel_id=1, source_target_pairs={{0,1},{1,2},{2,3},{4,5},{5,6},{6,7},{8,9},{9,10},{10,11},{12,13},{... | collective-permute-start | bytes 49160 | tf_op jit(solution)/shard_map/ppermute | solution.py:18
  45.9 224.2 %collective-permute-start.8 = (f32[4,6144]{1,0:T(4,128)}, f32[4,6144]{1,0:T(4,128)}, u32[]{:S(2)}, u32[]{:S(2)}) collective-permute-start(f32[4,6144]{1,0:T(4,128)} %get-tuple-element.16), channel_id=1, source_target_pairs={{4,0},{8,4},{12,8},{16,12},{20,16},{24,20},{28,24},{5,1},{9,5},{13... | collective-permute-start | bytes 294920 | tf_op jit(solution)/shard_map/ppermute | solution.py:20
  47.2 222.9 %collective-permute-start.9 = (f32[4,6144]{1,0:T(4,128)}, f32[4,6144]{1,0:T(4,128)}, u32[]{:S(2)}, u32[]{:S(2)}) collective-permute-start(f32[4,6144]{1,0:T(4,128)} %get-tuple-element.17), channel_id=1, source_target_pairs={{0,4},{4,8},{8,12},{12,16},{16,20},{20,24},{24,28},{1,5},{5,9},{9,... | collective-permute-start | bytes 294920 | tf_op jit(solution)/shard_map/ppermute | solution.py:18
  51.3 218.9 %collective-permute-start.10 = (f32[16,256]{1,0:T(8,128)}, f32[16,256]{1,0:T(8,128)S(1)}, u32[]{:S(2)}, u32[]{:S(2)}) collective-permute-start(f32[16,256]{1,0:T(8,128)} %get-tuple-element.18), channel_id=1, source_target_pairs={{1,0},{2,1},{3,2},{5,4},{6,5},{7,6},{9,8},{10,9},{11,10},{13,12},{... | collective-permute-start | bytes 49160 | tf_op jit(solution)/shard_map/ppermute | solution.py:20
  52.6 217.6 %collective-permute-start.11 = (f32[16,256]{1,0:T(8,128)S(1)}, f32[16,256]{1,0:T(8,128)S(1)}, u32[]{:S(2)}, u32[]{:S(2)}) collective-permute-start(f32[16,256]{1,0:T(8,128)S(1)} %get-tuple-element.19), channel_id=1, source_target_pairs={{0,1},{1,2},{2,3},{4,5},{5,6},{6,7},{8,9},{9,10},{10,11},{12,13},{... | collective-permute-start | bytes 49160 | tf_op jit(solution)/shard_map/ppermute | solution.py:18
  59.5 5.4 %copy-start.6 = (bf16[16,384]{1,0:T(8,128)(2,1)S(1)}, bf16[16,384]{1,0:T(8,128)(2,1)}, u32[]{:S(2)}) copy-start(bf16[16,384]{1,0:T(8,128)(2,1)} %param.11) | copy-start | bytes 36868
  191.1 2.9 %copy-start.7 = (bf16[64,32]{0,1:T(8,128)(2,1)S(1)}, bf16[64,32]{0,1:T(8,128)(2,1)}, u32[]{:S(2)}) copy-start(bf16[64,32]{0,1:T(8,128)(2,1)} %param.13) | copy-start | bytes 12292
  267.7 2.5 copy-start.3
  267.7 2.5 copy-start.4
Sparse Core Ops, SparseCore 0:
  10.0 36.8 all-gather.5
  48.7 32.6 all-gather.7
  83.3 32.3 all-gather.3
where the time goes:
time: 282 us; the launch traced here: 281 us
  blocking collectives  166 us (59%)
  local copies, waits for them, and re-layouts  41.9 us (15%)
  starting transfers between devices  33.6 us (12%)
  matrix products  17.3 us (6%)
  between operations  13.5 us (5%)
  other arithmetic  7.48 us (3%)
    all_gather x3, blocking collectives, expand(): lax.all_gather(partial_value, 'gy', axis=2, tiled=True)  166 us
    ppermute x6, starting transfers between devices, with_halo(): lax.ppermute(tail, axis, [(i, (i + 1) % count) for i in range(ends)])  25.8 us
    all_gather x3, local copies, waits for them, and re-layouts, expand(): lax.all_gather(blocks, 'gx', axis=1, tiled=True)  16.1 us
    dot_general x3, matrix products, expand(): jnp.einsum('xr,srnc->sxnc', columns, lax.all_gather(blocks, 'gx', axis=1,...  11.4 us
    all_gather x3, local copies, waits for them, and re-layouts, expand(): lax.all_gather(partial_value, 'gy', axis=2, tiled=True)  7.76 us
    ppermute x6, starting transfers between devices, with_halo(): lax.ppermute(head, axis, [((i + 1) % count, i) for i in range(ends)])  7.73 us
    slice x7, local copies, waits for them, and re-layouts, body(): core_blocks[section:section + group]  7.27 us
  transfers between devices with their start and end apart: 15, of which 1 were waited for; matrix products, arithmetic and copies ran while one was open for 21% of the time, Pallas kernels for 0%

commit v1 on v0

v1 whole, which is shorter than its diff:
```python
import functools

import jax
import jax.numpy as jnp
from jax import lax
from jax.experimental import pallas as pl
from jax.experimental.pallas import tpu as pltpu
from jax.sharding import PartitionSpec as P

STENCIL = (-205.0 / 72.0, 8.0 / 5.0, -1.0 / 5.0, 8.0 / 315.0, -1.0 / 560.0)
F32 = jnp.float32
BF16 = jnp.bfloat16
LANES = 128
TOP = 2.0**7.75
VMEM_BYTES = 48 * 1024 * 1024


def encode(values):
    peak = jnp.max(jnp.abs(values), axis=1, keepdims=True)
    scale = (jnp.maximum(peak, 1e-30) * (1.0 + 2.0**-7)).astype(BF16).astype(F32)
    ratio = values * (TOP / scale)
    power = ratio * ratio
    power = power * power
    power = power * power
    power = power * power
    return jnp.where(ratio < 0.0, -power, power).astype(BF16), scale


def decode(codes, unit):
    codes = codes.astype(F32)
    size = jnp.maximum(jnp.abs(codes), 2.0**-126)
    for _ in range(4):
        size = lax.rsqrt(size)
    size = size * unit
    return jnp.where(codes < 0.0, -size, jnp.where(codes > 0.0, size, 0.0))


def put_codes(ref, row, values, flat):
    rows = values.shape[0]
    codes, scale = encode(values)
    ref[row : row + rows, :flat] = codes
    ref[row : row + rows, flat : flat + LANES] = jnp.broadcast_to(scale, (rows, LANES)).astype(BF16)


def units(ref, row, rows, lane):
    return ref[row : row + rows, lane : lane + LANES].astype(F32) * (1.0 / TOP)


def split(values):
    upper = values.astype(BF16)
    return upper, (values - upper.astype(F32)).astype(BF16)


def dot(left, right):
    return jnp.dot(left, right, preferred_element_type=F32)


def swap_groups(tiles, depth):
    group = lax.broadcasted_iota(jnp.int32, (1, LANES), 1) // depth
    low_half, even = group < 2, group % 2 == 0

    def exchange(left, right, distance, keep):
        return (
            jnp.where(keep, left, pltpu.roll(right, distance, 1)),
            jnp.where(keep, pltpu.roll(left, LANES - distance, 1), right),
        )

    first, third = exchange(tiles[0], tiles[2], 2 * depth, low_half)
    second, fourth = exchange(tiles[1], tiles[3], 2 * depth, low_half)
    first, second = exchange(first, second, depth, even)
    third, fourth = exchange(third, fourth, depth, even)
    return first, second, third, fourth


def pieces(rows):
    return [(start, 16) for start in range(0, rows, 16)] if rows % 16 == 0 else [(0, rows)]


def project_kernel(chips, parts, core, other, *rest):
    factors, outs, (partial,) = rest[:chips], rest[chips:-1], rest[-1:]
    steps, rank, flat = core.shape
    lines = partial.shape[1]
    cells = lines // steps
    place = lax.axis_index("gx")
    factor = jnp.concatenate([ref[...] for ref in factors], axis=0)
    offset = lax.broadcasted_iota(jnp.int32, (factor.shape[1], rank), 0) - lax.broadcasted_iota(
        jnp.int32, (factor.shape[1], rank), 1
    )
    own_rows, other_rows = [
        dot(factor, jnp.where(offset == owner * rank, 1.0, 0.0).astype(BF16)).astype(BF16)
        for owner in (place, place + 1 - 2 * (place % 2))
    ]
    share = flat // parts
    width = 512 if share % 512 == 0 else 256
    for part in range(parts):
        mine, sends = outs[part * chips], outs[part * chips + 1 : (part + 1) * chips]
        for step in range(steps):
            for low in range(0, share, width):
                lanes = slice(part * share + low, part * share + low + width)
                value = dot(own_rows, core[step, :, lanes]) + dot(other_rows, other[step, :, lanes])
                mine[step * cells : (step + 1) * cells, low : low + width] = value[:cells]
                for distance in range(1, chips):
                    partial[distance - 1, step * cells : (step + 1) * cells, low : low + width] = value[
                        distance * cells : (distance + 1) * cells
                    ]
        for distance in range(1, chips):
            for start, count in pieces(lines):
                put_codes(sends[distance - 1], start, partial[distance - 1, start : start + count, :], share)


def gather_kernel(depth, steps, mine, *rest):
    received, (codes, spread, turned) = rest[:-3], rest[-3:]
    lines, flat = mine.shape
    cells = lines // steps
    quads = LANES // depth
    groups = flat // LANES
    pad = spread.shape[0] // lines
    for start, count in pieces(lines):
        scales = [units(ref, start, count, flat) for ref in received]
        for group in range(groups):
            lanes = slice(group * LANES, (group + 1) * LANES)
            value = mine[start : start + count, lanes]
            for ref, unit in zip(received, scales):
                value = value + decode(ref[start : start + count, lanes], unit)
            for row in range(0, count, 8):
                spread[pl.ds((start + row) * pad + group, 8, stride=pad), :] = value[row : row + 8]
    rest_x = cells // quads
    for line in range(steps * rest_x):
        base = line // rest_x * cells + line % rest_x
        for top in range(0, groups, 8):
            count = min(8, groups - top)
            tiles = [
                spread[(base + i * rest_x) * pad + top : (base + i * rest_x) * pad + top + 8, :] for i in range(quads)
            ]
            for j, tile in enumerate(swap_groups(tiles, depth)):
                turned[j * groups + top : j * groups + top + count, line * LANES : (line + 1) * LANES] = tile[:count]
    for start, count in pieces(turned.shape[0]):
        put_codes(codes, start, turned[start : start + count, :], turned.shape[1])


def contract_second(part, parts, depth, second, blocks, upper, lower, total, earlier):
    count_y, rows, flat = upper.shape
    quads = LANES // depth
    ranks = second.shape[1]
    place = lax.axis_index("gy")
    width = 512 if flat % 512 == 0 else 256
    for distance, block in enumerate(blocks):
        owner = jnp.bitwise_xor(place, distance)
        for start, count in pieces(rows):
            unit = units(block, start, count, flat)
            for low in range(0, flat, LANES):
                high, rest_of = split(decode(block[start : start + count, low : low + LANES], unit))
                upper[owner, start : start + count, low : low + LANES] = high
                lower[owner, start : start + count, low : low + LANES] = rest_of
    shape = (ranks, count_y * rows)
    column = lax.broadcasted_iota(jnp.int32, shape, 1)
    inside = column % rows
    groups = rows // quads
    rank = column // rows * (rows * parts) + part * rows + inside % groups * quads + inside // groups
    chosen = jnp.where(lax.broadcasted_iota(jnp.int32, shape, 0) == rank, 1.0, 0.0).astype(BF16)
    columns = dot(second[...], chosen).astype(BF16)
    together = count_y if rows % 16 == 0 else 1
    for low in range(0, flat, width):
        value = None if earlier is None else earlier[:, low : low + width]
        for first in range(0, count_y, together):
            left = columns[:, first * rows : (first + together) * rows]
            for ref in (upper, lower):
                right = ref[first : first + together, :, low : low + width].reshape(together * rows, width)
                value = dot(left, right) if value is None else value + dot(left, right)
        total[:, low : low + width] = value


def early_kernel(part, parts, depth, second, *rest):
    blocks, (total, upper, lower) = rest[:-3], rest[-3:]
    contract_second(part, parts, depth, second, blocks, upper, lower, total, None)


def image_kernel(part, parts, depth, steps, second, depth_factor, waves, *rest):
    rest, (image, upper, lower, mixed, spread) = rest[:-5], rest[-5:]
    earlier, blocks = (rest[0], rest[1:]) if part > 0 else (None, rest)
    contract_second(part, parts, depth, second, blocks, upper, lower, mixed, earlier)
    flat = mixed.shape[1]
    cells = image.shape[0]
    levels = depth_factor.shape[0]
    quads = LANES // depth
    groups = flat // LANES
    pad = spread.shape[0] // mixed.shape[0]
    for row in range(0, mixed.shape[0], 8):
        for group in range(groups):
            spread[pl.ds(row * pad + group, 8, stride=pad), :] = mixed[
                row : row + 8, group * LANES : (group + 1) * LANES
            ]
    square = jnp.concatenate([depth_factor[...].astype(F32)] * quads, axis=1)
    square = jnp.concatenate([square] * quads, axis=0)
    shape = square.shape
    same = lax.broadcasted_iota(jnp.int32, shape, 0) // levels == lax.broadcasted_iota(jnp.int32, shape, 1) // depth
    square = jnp.where(same, square, 0.0).astype(BF16)
    tiles = quads * levels // LANES
    contract = (((1,), (1,)), ((), ()))
    rest_x = cells // quads
    for quad in range(mixed.shape[0] // quads):
        turned = [
            swap_groups(
                [spread[(quad * quads + j) * pad + top : (quad * quads + j) * pad + top + 8, :] for j in range(quads)],
                depth,
            )
            for top in range(0, pad, 8)
        ]
        high, rest_of = split(jnp.concatenate([piece[i] for i in range(quads) for piece in turned], axis=0))
        source = lax.dot_general(high, square, contract, preferred_element_type=F32) + lax.dot_general(
            rest_of, square, contract, preferred_element_type=F32
        )
        for tile in range(tiles):
            at = quad * tiles + tile
            total = None
            for step in range(steps):
                value = jnp.concatenate(
                    [
                        source[i * pad + step * rest_x : i * pad + (step + 1) * rest_x, tile * LANES : (tile + 1) * LANES]
                        for i in range(quads)
                    ],
                    axis=0,
                )
                value = value * waves[at, step * cells : (step + 1) * cells, :]
                total = value if total is None else total + value
            image[:, at * LANES : (at + 1) * LANES] = total


def pack_kernel(pressure, previous, velocity, own, up, down):
    cells, flat = pressure.shape
    span = up.shape[1] - LANES
    put_codes(own, 0, pressure[...], flat)
    put_codes(own, cells, previous[...], flat)
    own[2 * cells :, :flat] = velocity[...]
    own[2 * cells :, flat:] = jnp.zeros((cells, LANES), BF16)
    up[:, :span] = own[:, flat - span : flat]
    down[:, :span] = own[:, :span]
    up[:, span:] = own[:, flat:]
    down[:, span:] = own[:, flat:]


def edge_kernel(own, low, high, ahead, behind):
    flat = own.shape[1] - LANES
    span = low.shape[1] - LANES
    near = span * 2 // 3
    cells = own.shape[0] // 3
    half = cells // 2
    scales = 2 * near + flat
    spans = [
        (low, slice(span - near, span), slice(0, near)),
        (own, slice(0, flat), slice(near, near + flat)),
        (high, slice(0, near), slice(near + flat, scales)),
        (low, slice(span, span + LANES), slice(scales, scales + LANES)),
        (own, slice(flat, flat + LANES), slice(scales + LANES, scales + 2 * LANES)),
        (high, slice(span, span + LANES), slice(scales + 2 * LANES, scales + 3 * LANES)),
    ]
    for ref, rows in ((ahead, slice(half, cells)), (behind, slice(0, half))):
        for part, lanes, into in spans:
            ref[:cells, into] = part[:cells, lanes]
            prior = part[cells : 2 * cells, lanes].astype(F32)[rows]
            speed = part[2 * cells :, lanes].astype(F32)[rows]
            ref[cells:, into] = jnp.concatenate([prior, speed], axis=0).astype(BF16)


def wave_kernel(levels, pressure, previous, velocity, left, right, low, high, waves, first, second, third, prior, speed):
    cells, flat = pressure.shape
    half = cells // 2
    span = low.shape[1] - LANES
    near = span * 2 // 3
    steps = waves.shape[1] // cells
    edge, inner, own_tiles = span // LANES, near // LANES, flat // LANES

    for tile in range(own_tiles):
        lane = tile * LANES
        first[edge + tile, cells : 2 * cells, :] = pressure[:, lane : lane + LANES]
        prior[inner + tile, half : half + cells, :] = previous[:, lane : lane + LANES]
        speed[inner + tile, half : half + cells, :] = velocity[:, lane : lane + LANES].astype(F32)
    wide = own_tiles + 2 * inner
    for part, top, side in ((left, 0, 0), (right, 2 * cells, half + cells)):
        scales = [units(part, 0, 2 * cells, (wide + k) * LANES) for k in range(3)]
        for tile in range(wide):
            lanes = slice(tile * LANES, (tile + 1) * LANES)
            unit = scales[0 if tile < inner else 1 if tile < inner + own_tiles else 2]
            first[edge - inner + tile, top : top + cells, :] = decode(part[:cells, lanes], unit[:cells])
            both = part[cells:, lanes].astype(F32)
            prior[tile, side : side + half, :] = decode(both[:half], unit[cells : cells + half])
            speed[tile, side : side + half, :] = both[half:]
        for tile in list(range(edge - inner)) + list(range(edge + own_tiles + inner, 2 * edge + own_tiles)):
            first[tile, top : top + cells, :] = jnp.zeros((cells, LANES), F32)
    for part, start, cut, begin in ((low, 0, edge - inner, 0), (high, edge + own_tiles, 0, inner + own_tiles)):
        unit = units(part, 0, 3 * cells, span)
        for tile in range(edge):
            lanes = slice(tile * LANES, (tile + 1) * LANES)
            first[start + tile, cells : 2 * cells, :] = decode(part[:cells, lanes], unit[:cells])
            if cut <= tile < cut + inner:
                prior[begin + tile - cut, half : half + cells, :] = decode(
                    part[cells : 2 * cells, lanes], unit[cells : 2 * cells]
                )
                speed[begin + tile - cut, half : half + cells, :] = part[2 * cells :, lanes].astype(F32)

    line = lax.broadcasted_iota(jnp.int32, (LANES, LANES), 0)
    column = lax.broadcasted_iota(jnp.int32, (LANES, LANES), 1)
    gap = jnp.abs(line - column)
    band = jnp.zeros((LANES, LANES), F32)
    for reach in range(5):
        band = jnp.where(gap == reach, STENCIL[reach] * (3.0 if reach == 0 else 1.0), band)
    band = jnp.where(line // levels == column // levels, band, 0.0)
    band_upper, band_lower = split(band)
    bands = jnp.concatenate([band_upper, band_upper, band_lower], axis=0)
    front = lax.broadcasted_iota(jnp.int32, (1, LANES), 1) < levels
    count = 4

    def advance(now, before, shift, tile_shift, later, out_row, top, rows, tile):
        tiles = [now[tile + step, top : top + rows, :] for step in range(-2, count + 2)]
        rolled = [pltpu.roll(value, levels, 1) for value in tiles]
        tall = jnp.concatenate(tiles[2 : 2 + count], axis=0)
        upper, lower = split(tall)
        deep = dot(jnp.concatenate([upper, lower, upper], axis=1), bands)
        for step in range(count):
            at = step + 2
            total = deep[step * rows : (step + 1) * rows]
            sides = [
                jnp.where(front, rolled[at] + rolled[at - 1], rolled[at + 1] + rolled[at]),
                tiles[at + 1] + tiles[at - 1],
                jnp.where(front, rolled[at + 1] + rolled[at - 2], rolled[at + 2] + rolled[at - 1]),
                tiles[at + 2] + tiles[at - 2],
            ]
            for reach in range(1, 5):
                value = sides[reach - 1] + now[tile + step, top + reach : top + reach + rows, :]
                value = value + now[tile + step, top - reach : top - reach + rows, :]
                total = total + STENCIL[reach] * value
            rate = speed[tile + step - (edge - inner), top - half : top - half + rows, :]
            past = before[tile + step - tile_shift, top - shift : top - shift + rows, :]
            following = 2.0 * tiles[at] - past + rate * total
            if later is None:
                waves[tile + step - edge, out_row : out_row + rows, :] = following
            else:
                later[tile + step, top : top + rows, :] = following

    chain = [(first, prior, half, edge - inner, second), (second, first, 0, 0, third), (third, second, 0, 0, None)]
    for step in range(steps):
        now, before, shift, tile_shift, later = chain[step]
        margin = (steps - 1 - step) * (edge // steps)
        tops = (cells - half, 2 * cells - half) if later is not None else (cells,)

        def loop(block, carry):
            for top in tops:
                advance(now, before, shift, tile_shift, later, step * cells, top, cells, edge - margin + count * block)
            return carry

        lax.fori_loop(0, (own_tiles + 2 * margin) // count, loop, 0)
        if later is not None:
            for tile in range(own_tiles):
                waves[tile, step * cells : (step + 1) * cells, :] = later[edge + tile, cells : 2 * cells, :]


def call(kernel, outs, scratch, flops, *args):
    moved = sum(arg.size * arg.dtype.itemsize for arg in args)
    moved += sum(out.size * jnp.dtype(out.dtype).itemsize for out in outs)
    return pl.pallas_call(
        kernel,
        out_shape=outs,
        scratch_shapes=scratch,
        cost_estimate=pl.CostEstimate(flops=flops, bytes_accessed=moved, transcendentals=0),
        compiler_params=pltpu.CompilerParams(vmem_limit_bytes=VMEM_BYTES),
    )(*args)


def shape_of(*shape, dtype=F32):
    return jax.ShapeDtypeStruct(shape, dtype)


def body(pressure, previous, velocity, tucker_core, first_factor, second_factor, depth_factor):
    cells, flat = pressure.shape
    levels, depth = depth_factor.shape
    steps, rank, core_flat = tucker_core.shape
    local_second = core_flat // depth
    lines = steps * cells
    count_x, count_y = lax.axis_size("gx"), lax.axis_size("gy")
    chips = count_x // 2
    span = 4 * steps * levels
    near = span * 2 // 3
    parts = 2 if local_second % 32 == 0 else 1
    rows = local_second // parts
    share = core_flat // parts
    groups_pad = (share // LANES + 7) // 8 * 8
    lines_pad = (lines * depth // LANES + 7) // 8 * 8

    across = [[(i, 2 * ((i // 2) ^ distance) + i % 2) for i in range(count_x)] for distance in range(1, chips)]
    factors = [first_factor] + [lax.ppermute(first_factor, "gx", route) for route in across]
    other = lax.ppermute(tucker_core, "gx", [(i, i + 1 - 2 * (i % 2)) for i in range(count_x)])

    outs = call(
        functools.partial(project_kernel, chips, parts),
        ([shape_of(lines, share)] + [shape_of(lines, share + LANES, dtype=BF16)] * (chips - 1)) * parts,
        [pltpu.VMEM((chips - 1, lines, share), F32)],
        4 * lines * chips * rank * core_flat,
        tucker_core,
        other,
        *factors,
    )
    outs = [outs[part * chips : (part + 1) * chips] for part in range(parts)]
    received = [[lax.ppermute(send, "gx", route) for send, route in zip(outs[0][1:], across)]]

    pressure_later, _ = lax.optimization_barrier((pressure, outs[0][0]))
    own, up, down = call(
        pack_kernel,
        [shape_of(3 * cells, flat + LANES, dtype=BF16)] + [shape_of(3 * cells, span + LANES, dtype=BF16)] * 2,
        [],
        10 * cells * flat,
        pressure_later,
        previous,
        velocity,
    )
    low = lax.ppermute(up, "gy", [(i, i + 1) for i in range(count_y - 1)])
    high = lax.ppermute(down, "gy", [(i + 1, i) for i in range(count_y - 1)])
    mixed, blocks = [], []
    for part in range(parts):
        if part + 1 < parts:
            received[part], sends = lax.optimization_barrier((received[part], outs[part + 1][1:]))
            received.append([lax.ppermute(send, "gx", route) for send, route in zip(sends, across)])
        if part > 0:
            received[part], blocks[1:3] = lax.optimization_barrier((received[part], blocks[1:3]))
            mixed = call(
                functools.partial(early_kernel, part - 1, parts, depth),
                [shape_of(second_factor.shape[0], lines * depth)],
                [pltpu.VMEM((count_y, rows, lines * depth), BF16)] * 2,
                4 * second_factor.shape[0] * count_y * rows * lines * depth,
                second_factor,
                *blocks,
            )
        (codes,) = call(
            functools.partial(gather_kernel, depth, steps),
            [shape_of(rows, lines * depth + LANES, dtype=BF16)],
            [pltpu.VMEM((lines * groups_pad, LANES), F32), pltpu.VMEM((rows, lines * depth), F32)],
            30 * chips * lines * share,
            outs[part][0],
            *received[part],
        )
        if part == 0:
            codes, low, high = lax.optimization_barrier((codes, low, high))
            ahead, behind = call(
                edge_kernel,
                [shape_of(2 * cells, flat + 2 * near + 3 * LANES, dtype=BF16)] * 2,
                [],
                1000,
                own,
                low,
                high,
            )
        if part == parts - 1:
            codes, ahead, behind = lax.optimization_barrier((codes, ahead, behind))
        blocks = [codes] + [
            lax.ppermute(codes, "gy", [(i, i ^ distance) for i in range(count_y)]) for distance in range(1, count_y)
        ]

    left = lax.ppermute(ahead, "gx", [(i, i + 1) for i in range(count_x - 1)])
    right = lax.ppermute(behind, "gx", [(i + 1, i) for i in range(count_x - 1)])
    (waves,) = call(
        functools.partial(wave_kernel, levels),
        [shape_of(flat // LANES, lines, LANES)],
        [pltpu.VMEM(((flat + 2 * span) // LANES, 3 * cells, LANES), F32)] * 3
        + [pltpu.VMEM(((flat + 2 * near) // LANES, 2 * cells, LANES), F32)] * 2,
        150 * lines * flat,
        pressure,
        previous,
        velocity,
        left,
        right,
        low,
        high,
    )
    cells_y = second_factor.shape[0]
    (image,) = call(
        functools.partial(image_kernel, parts - 1, parts, depth, steps),
        [shape_of(cells, flat)],
        [pltpu.VMEM((count_y, rows, lines * depth), BF16)] * 2
        + [pltpu.VMEM((cells_y, lines * depth), F32), pltpu.VMEM((cells_y * lines_pad, LANES), F32)],
        4 * cells_y * count_y * rows * lines * depth,
        second_factor,
        depth_factor,
        waves,
        *mixed,
        *blocks,
    )
    return image


def solution(mesh):
    placed = (
        P("gx", "gy"),
        P("gx", "gy"),
        P("gx", "gy"),
        P(None, "gx", "gy"),
        P("gx", None),
        P("gy", None),
        P(),
    )
    return jax.shard_map(body, mesh=mesh, in_specs=placed, out_specs=P("gx", "gy"), check_vma=False)
```

time: 282 us -> 67.2 us (0.24)
  the two profiles are of different devices: /device:TPU:0 before, /device:TPU:12 now
where the time goes in v1:
time: 67.2 us; the launch traced here: 66.9 us
  starting transfers between devices  32.3 us (48%)
  Pallas kernels  17 us (25%)
  waiting for transfers between devices  15.5 us (23%)
  local copies, waits for them, and re-layouts  1.99 us (3%)
    pallas_call x8, Pallas kernels, call(): pl.pallas_call(kernel, out_shape=outs, scratch_shapes=scratch, cost_estim...  17 us
    ppermute x6, waiting for transfers between devices, body(): lax.ppermute(codes, 'gy', [(i, i ^ distance) for i in range(count_y)])  12.1 us
    ppermute x6, starting transfers between devices, body(): lax.ppermute(codes, 'gy', [(i, i ^ distance) for i in range(count_y)])  9.29 us
    ppermute x6, starting transfers between devices, body(): lax.ppermute(send, 'gx', route)  7.11 us
    ppermute x1, starting transfers between devices, body(): right = lax.ppermute(behind, 'gx', [(i + 1, i) for i in range(count_x - 1)])  4.54 us
    ppermute x3, starting transfers between devices, body(): lax.ppermute(first_factor, 'gx', route)  3.55 us
    ppermute x1, starting transfers between devices, body(): low = lax.ppermute(up, 'gy', [(i, i + 1) for i in range(count_y - 1)])  3.49 us
    ppermute x3, waiting for transfers between devices, body(): lax.ppermute(first_factor, 'gx', route)  3.31 us
  transfers between devices with their start and end apart: 20, of which 6 were waited for; matrix products, arithmetic and copies ran while one was open for 0% of the time, Pallas kernels for 17%

profile of v1, /device:TPU:12, one launch (start us, length us, event | category | flops | bytes accessed | tf_op | source)
XLA Modules:
  0.0 66.9 jit_solution(17900111811303005923)
XLA Ops:
  0.0 0.0 collective-permute-start
  0.0 1.6 %collective-permute-start.1 = (bf16[16,384]{1,0:T(8,128)(2,1)}, bf16[16,384]{1,0:T(8,128)(2,1)S(1)}, u32[]{:S(2)}, u32[]{:S(2)}) collective-permute-start(bf16[16,384]{1,0:T(8,128)(2,1)} %rest_0_.1), channel_id=1, source_target_pairs={{0,8},{4,12},{8,0},{12,4},{16,24},{20,28},{24,16},{28,20},{1,9},{5... | collective-permute-start | bytes 36872 | tf_op jit(solution)/shard_map/ppermute | solution.py:390
  1.6 0.5 collective-permute-start.2
  2.1 1.5 %collective-permute-start.3 = (bf16[16,384]{1,0:T(8,128)(2,1)}, bf16[16,384]{1,0:T(8,128)(2,1)S(1)}, u32[]{:S(2)}, u32[]{:S(2)}) collective-permute-start(bf16[16,384]{1,0:T(8,128)(2,1)} %rest_0_.1), channel_id=1, source_target_pairs={{0,24},{4,28},{8,16},{12,20},{16,8},{20,12},{24,0},{28,4},{1,25},{... | collective-permute-start | bytes 36872 | tf_op jit(solution)/shard_map/ppermute | solution.py:390
  3.6 0.4 collective-permute-done.1.rest_1_
  4.0 1.5 %collective-permute-done.2.rest_2_ = bf16[16,384]{1,0:T(8,128)(2,1)S(1)} collective-permute-done((bf16[16,384]{1,0:T(8,128)(2,1)}, bf16[16,384]{1,0:T(8,128)(2,1)S(1)}, u32[]{:S(2)}, u32[]{:S(2)}) %collective-permute-start.2) | collective-permute-done | bytes 12320 | tf_op jit(solution)/shard_map/ppermute | solution.py:390
  5.5 1.4 %collective-permute-done.3.rest_3_ = bf16[16,384]{1,0:T(8,128)(2,1)S(1)} collective-permute-done((bf16[16,384]{1,0:T(8,128)(2,1)}, bf16[16,384]{1,0:T(8,128)(2,1)S(1)}, u32[]{:S(2)}, u32[]{:S(2)}) %collective-permute-start.3) | collective-permute-done | bytes 12320 | tf_op jit(solution)/shard_map/ppermute | solution.py:390
  6.9 0.0 collective-permute-done.other
  6.9 1.2 %copy-done.2 = bf16[3,48,3072]{2,1,0:T(8,128)(2,1)S(1)} copy-done((bf16[3,48,3072]{2,1,0:T(8,128)(2,1)S(1)}, bf16[3,48,3072]{2,1,0:T(8,128)(2,1)}, u32[]{:S(2)}) %copy-start.2) | copy-done | bytes 884760
  8.1 0.7 %copy-done.5 = bf16[16,384]{1,0:T(8,128)(2,1)S(1)} copy-done((bf16[16,384]{1,0:T(8,128)(2,1)S(1)}, bf16[16,384]{1,0:T(8,128)(2,1)}, u32[]{:S(2)}) %copy-start.5) | copy-done | bytes 12312
  8.8 1.4 %shard_map.73 = (f32[48,1536]{1,0:T(8,128)S(1)}, bf16[48,1664]{1,0:T(8,128)(2,1)S(1)}, bf16[48,1664]{1,0:T(8,128)(2,1)S(1)}, bf16[48,1664]{1,0:T(8,128)(2,1)S(1)...) custom-call(bf16[3,48,3072]{2,1,0:T(8,128)(2,1)S(1)} %copy-done.2, ...), custom_call_target="tpu_custom_call" | custom-call | flops 113246208 | bytes 3366912 | tf_op jit(solution)/shard_map/pallas_call | solution.py:360
  10.2 0.6 collective-permute-start.4
  10.8 1.5 %collective-permute-start.5 = (bf16[48,1664]{1,0:T(8,128)(2,1)S(1)}, bf16[48,1664]{1,0:T(8,128)(2,1)S(1)}, u32[]{:S(2)}, u32[]{:S(2)}) collective-permute-start(bf16[48,1664]{1,0:T(8,128)(2,1)S(1)} %get-tuple-element.38), channel_id=1, source_target_pairs={{0,16},{4,20},{8,24},{12,28},{16,0},{20,4},{24,8},{28,12},{1,17},{... | collective-permute-start | bytes 479240 | tf_op jit(solution)/shard_map/ppermute | solution.py:403
  12.3 1.4 %collective-permute-start.6 = (bf16[48,1664]{1,0:T(8,128)(2,1)S(1)}, bf16[48,1664]{1,0:T(8,128)(2,1)S(1)}, u32[]{:S(2)}, u32[]{:S(2)}) collective-permute-start(bf16[48,1664]{1,0:T(8,128)(2,1)S(1)} %get-tuple-element.39), channel_id=1, source_target_pairs={{0,24},{4,28},{8,16},{12,20},{16,8},{20,12},{24,0},{28,4},{1,25},{... | collective-permute-start | bytes 479240 | tf_op jit(solution)/shard_map/ppermute | solution.py:403
  13.7 0.5 shard_map.75
  14.2 3.5 %collective-permute-start.10 = (bf16[48,896]{1,0:T(8,128)(2,1)S(1)}, bf16[48,896]{1,0:T(8,128)(2,1)S(1)}, u32[]{:S(2)}, u32[]{:S(2)}) collective-permute-start(bf16[48,896]{1,0:T(8,128)(2,1)S(1)} %get-tuple-element.51), channel_id=1, source_target_pairs={{0,1},{1,2},{2,3},{4,5},{5,6},{6,7},{8,9},{9,10},{10,11},{12,13},{... | collective-permute-start | bytes 258056 | tf_op jit(solution)/shard_map/ppermute | solution.py:415
  17.7 2.4 %collective-permute-start.11 = (bf16[48,896]{1,0:T(8,128)(2,1)S(1)}, bf16[48,896]{1,0:T(8,128)(2,1)S(1)}, u32[]{:S(2)}, u32[]{:S(2)}) collective-permute-start(bf16[48,896]{1,0:T(8,128)(2,1)S(1)} %get-tuple-element.52), channel_id=1, source_target_pairs={{1,0},{2,1},{3,2},{5,4},{6,5},{7,6},{9,8},{10,9},{11,10},{13,12},{... | collective-permute-start | bytes 258056 | tf_op jit(solution)/shard_map/ppermute | solution.py:416
  20.1 0.0 collective-permute-done.4.rest_0_
  20.1 0.0 collective-permute-done.5.rest_1_
  20.1 0.0 collective-permute-done.6.rest_2_
  20.1 0.0 copy-start.6
  20.1 0.0 copy-start.4
  20.1 0.7 %collective-permute-start.7 = (bf16[48,1664]{1,0:T(8,128)(2,1)S(1)}, bf16[48,1664]{1,0:T(8,128)(2,1)S(1)}, u32[]{:S(2)}, u32[]{:S(2)}) collective-permute-start(bf16[48,1664]{1,0:T(8,128)(2,1)S(1)} %get-tuple-element.43), channel_id=1, source_target_pairs={{0,8},{4,12},{8,0},{12,4},{16,24},{20,28},{24,16},{28,20},{1,9},{5... | collective-permute-start | bytes 479240 | tf_op jit(solution)/shard_map/ppermute | solution.py:421
  20.8 1.4 %collective-permute-start.8 = (bf16[48,1664]{1,0:T(8,128)(2,1)S(1)}, bf16[48,1664]{1,0:T(8,128)(2,1)S(1)}, u32[]{:S(2)}, u32[]{:S(2)}) collective-permute-start(bf16[48,1664]{1,0:T(8,128)(2,1)S(1)} %get-tuple-element.44), channel_id=1, source_target_pairs={{0,16},{4,20},{8,24},{12,28},{16,0},{20,4},{24,8},{28,12},{1,17},{... | collective-permute-start | bytes 479240 | tf_op jit(solution)/shard_map/ppermute | solution.py:421
  22.2 1.4 %collective-permute-start.9 = (bf16[48,1664]{1,0:T(8,128)(2,1)S(1)}, bf16[48,1664]{1,0:T(8,128)(2,1)S(1)}, u32[]{:S(2)}, u32[]{:S(2)}) collective-permute-start(bf16[48,1664]{1,0:T(8,128)(2,1)S(1)} %get-tuple-element.45), channel_id=1, source_target_pairs={{0,24},{4,28},{8,16},{12,20},{16,8},{20,12},{24,0},{28,4},{1,25},{... | collective-permute-start | bytes 479240 | tf_op jit(solution)/shard_map/ppermute | solution.py:421
  23.7 0.8 %shard_map.74.rest_0_ = bf16[48,1664]{1,0:T(8,128)(2,1)S(1)} custom-call(f32[48,1536]{1,0:T(8,128)S(1)} %get-tuple-element.46.mine, bf16[48,1664]{1,0:T(8,128)(2,1)S(1)} %collective-permute-done.4.rest_0_, bf16[48,1664]{1,0:T(8,128)(2,1)S(1)} %collective-permute-done.5.rest_1_, bf16[48,1664]{1,0:T(8,128)(2,1)S(1)} %collective-permute-done.6.rest_2_), custom_call_target="tpu_custom_call" | custom-call | flops 8847360 | bytes 933888 | tf_op jit(solution)/shard_map/pallas_call | solution.py:360
  24.5 0.0 collective-permute-done.10.low
  24.5 0.0 collective-permute-done.11.high
  24.5 0.6 collective-permute-start.12
  25.2 2.5 %collective-permute-start.13 = (bf16[48,1664]{1,0:T(8,128)(2,1)S(1)}, bf16[48,1664]{1,0:T(8,128)(2,1)S(1)}, u32[]{:S(2)}, u32[]{:S(2)}) collective-permute-start(bf16[48,1664]{1,0:T(8,128)(2,1)S(1)} %shard_map.74.rest_0_), channel_id=1, source_target_pairs={{0,2},{1,3},{2,0},{3,1},{4,6},{5,7},{6,4},{7,5},{8,10},{9,11},{10,... | collective-permute-start | bytes 479240 | tf_op jit(solution)/shard_map/ppermute | solution.py:454
  27.7 1.0 %shard_map.77 = (bf16[32,7552]{1,0:T(8,128)(2,1)}, bf16[32,7552]{1,0:T(8,128)(2,1)}) custom-call(bf16[48,6272]{1,0:T(8,128)(2,1)S(1)} %get-tuple-element.57.own, bf16[48,896]{1,0:T(8,128)(2,1)S(1)} %collective-permute-done.10.low, bf16[48,896]{1,0:T(8,128)(2,1)S(1)} %collective-permute-done.11.high), custom_call_target="tpu_custom_call" | custom-call | flops 1000 | bytes 1740800 | tf_op jit(solution)/shard_map/pallas_call | solution.py:360
  28.7 0.0 collective-permute-done.7.rest_0_
  28.7 0.0 collective-permute-done.8.rest_1_
  28.7 1.2 %collective-permute-done.12.rest_1_ = bf16[48,1664]{1,0:T(8,128)(2,1)S(1)} collective-permute-done((bf16[48,1664]{1,0:T(8,128)(2,1)S(1)}, bf16[48,1664]{1,0:T(8,128)(2,1)S(1)}, u32[]{:S(2)}, u32[]{:S(2)}) %collective-permute-start.12) | collective-permute-done | bytes 159776 | tf_op jit(solution)/shard_map/ppermute | solution.py:454
  29.9 2.8 %collective-permute-done.13.rest_2_ = bf16[48,1664]{1,0:T(8,128)(2,1)S(1)} collective-permute-done((bf16[48,1664]{1,0:T(8,128)(2,1)S(1)}, bf16[48,1664]{1,0:T(8,128)(2,1)S(1)}, u32[]{:S(2)}, u32[]{:S(2)}) %collective-permute-start.13) | collective-permute-done | bytes 159776 | tf_op jit(solution)/shard_map/ppermute | solution.py:454
  32.7 0.8 %shard_map.76.rest_1_ = bf16[48,1664]{1,0:T(8,128)(2,1)S(1)} custom-call(f32[48,1536]{1,0:T(8,128)S(1)} %get-tuple-element.36.mine, bf16[48,1664]{1,0:T(8,128)(2,1)S(1)} %collective-permute-done.7.rest_0_, bf16[48,1664]{1,0:T(8,128)(2,1)S(1)} %collective-permute-done.8.rest_1_, bf16[48,1664]{1,0:T(8,128)(2,1)S(1)} %collective-permute-done.9.rest_2_), custom_call_target="tpu_custom_call" | custom-call | flops 8847360 | bytes 933888 | tf_op jit(solution)/shard_map/pallas_call | solution.py:360
  33.6 1.9 %collective-permute-start.14 = (bf16[32,7552]{1,0:T(8,128)(2,1)}, bf16[32,7552]{1,0:T(8,128)(2,1)S(1)}, u32[]{:S(2)}, u32[]{:S(2)}) collective-permute-start(bf16[32,7552]{1,0:T(8,128)(2,1)} %get-tuple-element.62), channel_id=1, source_target_pairs={{0,4},{4,8},{8,12},{12,16},{16,20},{20,24},{24,28},{1,5},{5,9},{9,... | collective-permute-start | bytes 1449992 | tf_op jit(solution)/shard_map/ppermute | solution.py:457
  35.5 4.5 %collective-permute-start.15 = (bf16[32,7552]{1,0:T(8,128)(2,1)}, bf16[32,7552]{1,0:T(8,128)(2,1)S(1)}, u32[]{:S(2)}, u32[]{:S(2)}) collective-permute-start(bf16[32,7552]{1,0:T(8,128)(2,1)} %get-tuple-element.63), channel_id=1, source_target_pairs={{4,0},{8,4},{12,8},{16,12},{20,16},{24,20},{28,24},{5,1},{9,5},{13... | collective-permute-start | bytes 1449992 | tf_op jit(solution)/shard_map/ppermute | solution.py:458
  40.0 1.4 %collective-permute-start.16 = (bf16[48,1664]{1,0:T(8,128)(2,1)S(1)}, bf16[48,1664]{1,0:T(8,128)(2,1)S(1)}, u32[]{:S(2)}, u32[]{:S(2)}) collective-permute-start(bf16[48,1664]{1,0:T(8,128)(2,1)S(1)} %shard_map.74.rest_0_), channel_id=1, source_target_pairs={{0,3},{1,2},{2,1},{3,0},{4,7},{5,6},{6,5},{7,4},{8,11},{9,10},{10,... | collective-permute-start | bytes 479240 | tf_op jit(solution)/shard_map/ppermute | solution.py:454
  41.4 3.0 %collective-permute-start.17 = (bf16[48,1664]{1,0:T(8,128)(2,1)S(1)}, bf16[48,1664]{1,0:T(8,128)(2,1)S(1)}, u32[]{:S(2)}, u32[]{:S(2)}) collective-permute-start(bf16[48,1664]{1,0:T(8,128)(2,1)S(1)} %shard_map.76.rest_1_), channel_id=1, source_target_pairs={{0,1},{1,0},{2,3},{3,2},{4,5},{5,4},{6,7},{7,6},{8,9},{9,8},{10,11... | collective-permute-start | bytes 479240 | tf_op jit(solution)/shard_map/ppermute | solution.py:454
  44.4 0.0 collective-permute-start.18
  44.4 8.1 %collective-permute-done.16.rest_3_ = bf16[48,1664]{1,0:T(8,128)(2,1)S(1)} collective-permute-done((bf16[48,1664]{1,0:T(8,128)(2,1)S(1)}, bf16[48,1664]{1,0:T(8,128)(2,1)S(1)}, u32[]{:S(2)}, u32[]{:S(2)}) %collective-permute-start.16) | collective-permute-done | bytes 159776 | tf_op jit(solution)/shard_map/ppermute | solution.py:454
  52.6 1.8 %collective-permute-start.19 = (bf16[48,1664]{1,0:T(8,128)(2,1)S(1)}, bf16[48,1664]{1,0:T(8,128)(2,1)S(1)}, u32[]{:S(2)}, u32[]{:S(2)}) collective-permute-start(bf16[48,1664]{1,0:T(8,128)(2,1)S(1)} %shard_map.76.rest_1_), channel_id=1, source_target_pairs={{0,3},{1,2},{2,1},{3,0},{4,7},{5,6},{6,5},{7,4},{8,11},{9,10},{10,... | collective-permute-start | bytes 479240 | tf_op jit(solution)/shard_map/ppermute | solution.py:454
  54.3 0.1 copy.8.depth_factor
  54.4 1.1 %shard_map.79.rest_0_ = f32[96,1536]{1,0:T(8,128)S(1)} custom-call(bf16[96,384]{1,0:T(8,128)(2,1)S(1)} %copy-done.4, bf16[48,1664]{1,0:T(8,128)(2,1)S(1)} %shard_map.74.rest_0_, bf16[48,1664]{1,0:T(8,128)(2,1)S(1)} %collective-permute-done.12.rest_1_, bf16[48,1664]{1,0:T(8,128)(2,1)S(1)} %collective-permute-done.13.rest_2_, ...), custom_call_target="tpu_custom_call" | custom-call | flops 113246208 | bytes 1302528 | tf_op jit(solution)/shard_map/pallas_call | solution.py:360
  55.6 7.9 %shard_map.78.waves = f32[48,48,128]{2,1,0:T(8,128)S(1)} custom-call(f32[16,6144]{1,0:T(8,128)S(1)} %copy-done, f32[16,6144]{1,0:T(8,128)S(1)} %copy-done.1, bf16[16,6144]{1,0:T(8,128)(2,1)S(1)} %copy-done.3, bf16[32,7552]{1,0:T(8,128)(2,1)S(1)} %collective-permute-done.14.left, bf16[32,7552]{1,0:T(8,128)(2,1)S(1)} %collective-permute-done.15.right, ...), custom_call_target="tpu_custom_call" | custom-call | flops 44236800 | bytes 3301376 | tf_op jit(solution)/shard_map/pallas_call | solution.py:360
  63.5 0.0 collective-permute-done.18.rest_3_
  63.5 3.4 %shard_map.80 = f32[16,6144]{1,0:T(8,128)} custom-call(bf16[96,384]{1,0:T(8,128)(2,1)S(1)} %copy-done.4, bf16[64,32]{1,0:T(8,128)(2,1)S(1)} %copy.8.depth_factor, f32[48,48,128]{2,1,0:T(8,128)S(1)} %shard_map.78.waves, f32[96,1536]{1,0:T(8,128)S(1)} %shard_map.79.rest_0_, bf16[48,1664]{1,0:T(8,128)(2,1)S(1)} %shard_map.76.rest_1_, ...), custom_call_target="tpu_custom_call" | custom-call | flops 113246208 | bytes 2879488 | tf_op jit(solution)/shard_map/pallas_call | solution.py:360
  (15 shorter events, 0.0 us)
Async XLA Ops:
  0.0 13.7 %copy-start = (f32[16,6144]{1,0:T(8,128)S(1)}, f32[16,6144]{1,0:T(8,128)}, u32[]{:S(2)}) copy-start(f32[16,6144]{1,0:T(8,128)} %pressure.2) | copy-start | bytes 1179652
  0.0 13.7 %copy-start.1 = (f32[16,6144]{1,0:T(8,128)S(1)}, f32[16,6144]{1,0:T(8,128)}, u32[]{:S(2)}) copy-start(f32[16,6144]{1,0:T(8,128)} %previous.3) | copy-start | bytes 1179652
  0.0 6.9 %collective-permute-start = (bf16[3,48,3072]{2,1,0:T(8,128)(2,1)}, bf16[3,48,3072]{2,1,0:T(8,128)(2,1)S(1)}, u32[]{:S(2)}, u32[]{:S(2)}) collective-permute-start(bf16[3,48,3072]{2,1,0:T(8,128)(2,1)} %core.1), channel_id=1, source_target_pairs={{0,4},{4,0},{8,12},{12,8},{16,20},{20,16},{24,28},{28,24},{1,5},{5... | collective-permute-start | bytes 2654216 | tf_op jit(solution)/shard_map/ppermute | solution.py:391
  0.0 4.0 %collective-permute-start.1 = (bf16[16,384]{1,0:T(8,128)(2,1)}, bf16[16,384]{1,0:T(8,128)(2,1)S(1)}, u32[]{:S(2)}, u32[]{:S(2)}) collective-permute-start(bf16[16,384]{1,0:T(8,128)(2,1)} %rest_0_.1), channel_id=1, source_target_pairs={{0,8},{4,12},{8,0},{12,4},{16,24},{20,28},{24,16},{28,20},{1,9},{5... | collective-permute-start | bytes 36872 | tf_op jit(solution)/shard_map/ppermute | solution.py:390
  1.6 3.9 %collective-permute-start.2 = (bf16[16,384]{1,0:T(8,128)(2,1)}, bf16[16,384]{1,0:T(8,128)(2,1)S(1)}, u32[]{:S(2)}, u32[]{:S(2)}) collective-permute-start(bf16[16,384]{1,0:T(8,128)(2,1)} %rest_0_.1), channel_id=1, source_target_pairs={{0,16},{4,20},{8,24},{12,28},{16,0},{20,4},{24,8},{28,12},{1,17},{... | collective-permute-start | bytes 36872 | tf_op jit(solution)/shard_map/ppermute | solution.py:390
  2.1 4.8 %collective-permute-start.3 = (bf16[16,384]{1,0:T(8,128)(2,1)}, bf16[16,384]{1,0:T(8,128)(2,1)S(1)}, u32[]{:S(2)}, u32[]{:S(2)}) collective-permute-start(bf16[16,384]{1,0:T(8,128)(2,1)} %rest_0_.1), channel_id=1, source_target_pairs={{0,24},{4,28},{8,16},{12,20},{16,8},{20,12},{24,0},{28,4},{1,25},{... | collective-permute-start | bytes 36872 | tf_op jit(solution)/shard_map/ppermute | solution.py:390
  6.9 1.2 %copy-start.2 = (bf16[3,48,3072]{2,1,0:T(8,128)(2,1)S(1)}, bf16[3,48,3072]{2,1,0:T(8,128)(2,1)}, u32[]{:S(2)}) copy-start(bf16[3,48,3072]{2,1,0:T(8,128)(2,1)} %core.1) | copy-start | bytes 2654212
  8.1 0.7 %copy-start.5 = (bf16[16,384]{1,0:T(8,128)(2,1)S(1)}, bf16[16,384]{1,0:T(8,128)(2,1)}, u32[]{:S(2)}) copy-start(bf16[16,384]{1,0:T(8,128)(2,1)} %rest_0_.1) | copy-start | bytes 36868
  8.8 5.0 %copy-start.3 = (bf16[16,6144]{1,0:T(8,128)(2,1)S(1)}, bf16[16,6144]{1,0:T(8,128)(2,1)}, u32[]{:S(2)}) copy-start(bf16[16,6144]{1,0:T(8,128)(2,1)} %velocity.3) | copy-start | bytes 589828
  10.2 9.9 %collective-permute-start.4 = (bf16[48,1664]{1,0:T(8,128)(2,1)S(1)}, bf16[48,1664]{1,0:T(8,128)(2,1)S(1)}, u32[]{:S(2)}, u32[]{:S(2)}) collective-permute-start(bf16[48,1664]{1,0:T(8,128)(2,1)S(1)} %get-tuple-element.37), channel_id=1, source_target_pairs={{0,8},{4,12},{8,0},{12,4},{16,24},{20,28},{24,16},{28,20},{1,9},{5... | collective-permute-start | bytes 479240 | tf_op jit(solution)/shard_map/ppermute | solution.py:403
  10.8 9.3 %collective-permute-start.5 = (bf16[48,1664]{1,0:T(8,128)(2,1)S(1)}, bf16[48,1664]{1,0:T(8,128)(2,1)S(1)}, u32[]{:S(2)}, u32[]{:S(2)}) collective-permute-start(bf16[48,1664]{1,0:T(8,128)(2,1)S(1)} %get-tuple-element.38), channel_id=1, source_target_pairs={{0,16},{4,20},{8,24},{12,28},{16,0},{20,4},{24,8},{28,12},{1,17},{... | collective-permute-start | bytes 479240 | tf_op jit(solution)/shard_map/ppermute | solution.py:403
  12.3 7.8 %collective-permute-start.6 = (bf16[48,1664]{1,0:T(8,128)(2,1)S(1)}, bf16[48,1664]{1,0:T(8,128)(2,1)S(1)}, u32[]{:S(2)}, u32[]{:S(2)}) collective-permute-start(bf16[48,1664]{1,0:T(8,128)(2,1)S(1)} %get-tuple-element.39), channel_id=1, source_target_pairs={{0,24},{4,28},{8,16},{12,20},{16,8},{20,12},{24,0},{28,4},{1,25},{... | collective-permute-start | bytes 479240 | tf_op jit(solution)/shard_map/ppermute | solution.py:403
  14.2 10.3 %collective-permute-start.10 = (bf16[48,896]{1,0:T(8,128)(2,1)S(1)}, bf16[48,896]{1,0:T(8,128)(2,1)S(1)}, u32[]{:S(2)}, u32[]{:S(2)}) collective-permute-start(bf16[48,896]{1,0:T(8,128)(2,1)S(1)} %get-tuple-element.51), channel_id=1, source_target_pairs={{0,1},{1,2},{2,3},{4,5},{5,6},{6,7},{8,9},{9,10},{10,11},{12,13},{... | collective-permute-start | bytes 258056 | tf_op jit(solution)/shard_map/ppermute | solution.py:415
  17.7 6.8 %collective-permute-start.11 = (bf16[48,896]{1,0:T(8,128)(2,1)S(1)}, bf16[48,896]{1,0:T(8,128)(2,1)S(1)}, u32[]{:S(2)}, u32[]{:S(2)}) collective-permute-start(bf16[48,896]{1,0:T(8,128)(2,1)S(1)} %get-tuple-element.52), channel_id=1, source_target_pairs={{1,0},{2,1},{3,2},{5,4},{6,5},{7,6},{9,8},{10,9},{11,10},{13,12},{... | collective-permute-start | bytes 258056 | tf_op jit(solution)/shard_map/ppermute | solution.py:416
  20.1 34.2 %copy-start.6 = (bf16[64,32]{0,1:T(8,128)(2,1)S(1)}, bf16[64,32]{0,1:T(8,128)(2,1)}, u32[]{:S(2)}) copy-start(bf16[64,32]{0,1:T(8,128)(2,1)} %param.13) | copy-start | bytes 12292
  20.1 34.3 %copy-start.4 = (bf16[96,384]{1,0:T(8,128)(2,1)S(1)}, bf16[96,384]{1,0:T(8,128)(2,1)}, u32[]{:S(2)}) copy-start(bf16[96,384]{1,0:T(8,128)(2,1)} %second.3) | copy-start | bytes 221188
  20.1 8.6 %collective-permute-start.7 = (bf16[48,1664]{1,0:T(8,128)(2,1)S(1)}, bf16[48,1664]{1,0:T(8,128)(2,1)S(1)}, u32[]{:S(2)}, u32[]{:S(2)}) collective-permute-start(bf16[48,1664]{1,0:T(8,128)(2,1)S(1)} %get-tuple-element.43), channel_id=1, source_target_pairs={{0,8},{4,12},{8,0},{12,4},{16,24},{20,28},{24,16},{28,20},{1,9},{5... | collective-permute-start | bytes 479240 | tf_op jit(solution)/shard_map/ppermute | solution.py:421
  20.8 7.8 %collective-permute-start.8 = (bf16[48,1664]{1,0:T(8,128)(2,1)S(1)}, bf16[48,1664]{1,0:T(8,128)(2,1)S(1)}, u32[]{:S(2)}, u32[]{:S(2)}) collective-permute-start(bf16[48,1664]{1,0:T(8,128)(2,1)S(1)} %get-tuple-element.44), channel_id=1, source_target_pairs={{0,16},{4,20},{8,24},{12,28},{16,0},{20,4},{24,8},{28,12},{1,17},{... | collective-permute-start | bytes 479240 | tf_op jit(solution)/shard_map/ppermute | solution.py:421
  22.2 6.4 %collective-permute-start.9 = (bf16[48,1664]{1,0:T(8,128)(2,1)S(1)}, bf16[48,1664]{1,0:T(8,128)(2,1)S(1)}, u32[]{:S(2)}, u32[]{:S(2)}) collective-permute-start(bf16[48,1664]{1,0:T(8,128)(2,1)S(1)} %get-tuple-element.45), channel_id=1, source_target_pairs={{0,24},{4,28},{8,16},{12,20},{16,8},{20,12},{24,0},{28,4},{1,25},{... | collective-permute-start | bytes 479240 | tf_op jit(solution)/shard_map/ppermute | solution.py:421
  24.5 5.3 %collective-permute-start.12 = (bf16[48,1664]{1,0:T(8,128)(2,1)S(1)}, bf16[48,1664]{1,0:T(8,128)(2,1)S(1)}, u32[]{:S(2)}, u32[]{:S(2)}) collective-permute-start(bf16[48,1664]{1,0:T(8,128)(2,1)S(1)} %shard_map.74.rest_0_), channel_id=1, source_target_pairs={{0,1},{1,0},{2,3},{3,2},{4,5},{5,4},{6,7},{7,6},{8,9},{9,8},{10,11... | collective-permute-start | bytes 479240 | tf_op jit(solution)/shard_map/ppermute | solution.py:454
  25.2 7.5 %collective-permute-start.13 = (bf16[48,1664]{1,0:T(8,128)(2,1)S(1)}, bf16[48,1664]{1,0:T(8,128)(2,1)S(1)}, u32[]{:S(2)}, u32[]{:S(2)}) collective-permute-start(bf16[48,1664]{1,0:T(8,128)(2,1)S(1)} %shard_map.74.rest_0_), channel_id=1, source_target_pairs={{0,2},{1,3},{2,0},{3,1},{4,6},{5,7},{6,4},{7,5},{8,10},{9,11},{10,... | collective-permute-start | bytes 479240 | tf_op jit(solution)/shard_map/ppermute | solution.py:454
  33.6 22.0 %collective-permute-start.14 = (bf16[32,7552]{1,0:T(8,128)(2,1)}, bf16[32,7552]{1,0:T(8,128)(2,1)S(1)}, u32[]{:S(2)}, u32[]{:S(2)}) collective-permute-start(bf16[32,7552]{1,0:T(8,128)(2,1)} %get-tuple-element.62), channel_id=1, source_target_pairs={{0,4},{4,8},{8,12},{12,16},{16,20},{20,24},{24,28},{1,5},{5,9},{9,... | collective-permute-start | bytes 1449992 | tf_op jit(solution)/shard_map/ppermute | solution.py:457
  35.5 20.1 %collective-permute-start.15 = (bf16[32,7552]{1,0:T(8,128)(2,1)}, bf16[32,7552]{1,0:T(8,128)(2,1)S(1)}, u32[]{:S(2)}, u32[]{:S(2)}) collective-permute-start(bf16[32,7552]{1,0:T(8,128)(2,1)} %get-tuple-element.63), channel_id=1, source_target_pairs={{4,0},{8,4},{12,8},{16,12},{20,16},{24,20},{28,24},{5,1},{9,5},{13... | collective-permute-start | bytes 1449992 | tf_op jit(solution)/shard_map/ppermute | solution.py:458
  40.0 12.5 %collective-permute-start.16 = (bf16[48,1664]{1,0:T(8,128)(2,1)S(1)}, bf16[48,1664]{1,0:T(8,128)(2,1)S(1)}, u32[]{:S(2)}, u32[]{:S(2)}) collective-permute-start(bf16[48,1664]{1,0:T(8,128)(2,1)S(1)} %shard_map.74.rest_0_), channel_id=1, source_target_pairs={{0,3},{1,2},{2,1},{3,0},{4,7},{5,6},{6,5},{7,4},{8,11},{9,10},{10,... | collective-permute-start | bytes 479240 | tf_op jit(solution)/shard_map/ppermute | solution.py:454
  41.4 22.1 %collective-permute-start.17 = (bf16[48,1664]{1,0:T(8,128)(2,1)S(1)}, bf16[48,1664]{1,0:T(8,128)(2,1)S(1)}, u32[]{:S(2)}, u32[]{:S(2)}) collective-permute-start(bf16[48,1664]{1,0:T(8,128)(2,1)S(1)} %shard_map.76.rest_1_), channel_id=1, source_target_pairs={{0,1},{1,0},{2,3},{3,2},{4,5},{5,4},{6,7},{7,6},{8,9},{9,8},{10,11... | collective-permute-start | bytes 479240 | tf_op jit(solution)/shard_map/ppermute | solution.py:454
  44.4 19.1 %collective-permute-start.18 = (bf16[48,1664]{1,0:T(8,128)(2,1)S(1)}, bf16[48,1664]{1,0:T(8,128)(2,1)S(1)}, u32[]{:S(2)}, u32[]{:S(2)}) collective-permute-start(bf16[48,1664]{1,0:T(8,128)(2,1)S(1)} %shard_map.76.rest_1_), channel_id=1, source_target_pairs={{0,2},{1,3},{2,0},{3,1},{4,6},{5,7},{6,4},{7,5},{8,10},{9,11},{10,... | collective-permute-start | bytes 479240 | tf_op jit(solution)/shard_map/ppermute | solution.py:454
  52.6 11.0 %collective-permute-start.19 = (bf16[48,1664]{1,0:T(8,128)(2,1)S(1)}, bf16[48,1664]{1,0:T(8,128)(2,1)S(1)}, u32[]{:S(2)}, u32[]{:S(2)}) collective-permute-start(bf16[48,1664]{1,0:T(8,128)(2,1)S(1)} %shard_map.76.rest_1_), channel_id=1, source_target_pairs={{0,3},{1,2},{2,1},{3,0},{4,7},{5,6},{6,5},{7,4},{8,11},{9,10},{10,... | collective-permute-start | bytes 479240 | tf_op jit(solution)/shard_map/ppermute | solution.py:454

commit v2 on v1

--- a/solution.py
+++ b/solution.py
@@ -76,10 +76,10 @@
     return [(start, 16) for start in range(0, rows, 16)] if rows % 16 == 0 else [(0, rows)]
 
 
-def project_kernel(chips, parts, core, other, *rest):
-    factors, outs, (partial,) = rest[:chips], rest[chips:-1], rest[-1:]
+def project_kernel(chips, core, other, *rest):
+    factors, mine, sends, (partial,) = rest[:chips], rest[chips], rest[chips + 1 : -1], rest[-1:]
     steps, rank, flat = core.shape
-    lines = partial.shape[1]
+    lines = mine.shape[0]
     cells = lines // steps
     place = lax.axis_index("gx")
     factor = jnp.concatenate([ref[...] for ref in factors], axis=0)
@@ -90,22 +90,19 @@
         dot(factor, jnp.where(offset == owner * rank, 1.0, 0.0).astype(BF16)).astype(BF16)
         for owner in (place, place + 1 - 2 * (place % 2))
     ]
-    share = flat // parts
-    width = 512 if share % 512 == 0 else 256
-    for part in range(parts):
-        mine, sends = outs[part * chips], outs[part * chips + 1 : (part + 1) * chips]
-        for step in range(steps):
-            for low in range(0, share, width):
-                lanes = slice(part * share + low, part * share + low + width)
-                value = dot(own_rows, core[step, :, lanes]) + dot(other_rows, other[step, :, lanes])
-                mine[step * cells : (step + 1) * cells, low : low + width] = value[:cells]
-                for distance in range(1, chips):
-                    partial[distance - 1, step * cells : (step + 1) * cells, low : low + width] = value[
-                        distance * cells : (distance + 1) * cells
-                    ]
-        for distance in range(1, chips):
-            for start, count in pieces(lines):
-                put_codes(sends[distance - 1], start, partial[distance - 1, start : start + count, :], share)
+    width = 512 if flat % 512 == 0 else 256
+    for step in range(steps):
+        for low in range(0, flat, width):
+            lanes = slice(low, low + width)
+            value = dot(own_rows, core[step, :, lanes]) + dot(other_rows, other[step, :, lanes])
+            mine[step * cells : (step + 1) * cells, lanes] = value[:cells]
+            for distance in range(1, chips):
+                partial[distance - 1, step * cells : (step + 1) * cells, lanes] = value[
+                    distance * cells : (distance + 1) * cells
+                ]
+    for distance in range(1, chips):
+        for start, count in pieces(lines):
+            put_codes(sends[distance - 1], start, partial[distance - 1, start : start + count, :], flat)
 
 
 def gather_kernel(depth, steps, mine, *rest):
@@ -138,47 +135,57 @@
         put_codes(codes, start, turned[start : start + count, :], turned.shape[1])
 
 
-def contract_second(part, parts, depth, second, blocks, upper, lower, total, earlier):
-    count_y, rows, flat = upper.shape
+def contract_second(depth, second, blocks, total, earlier, terms):
+    rows, flat = blocks[0][1].shape[0], total.shape[1]
     quads = LANES // depth
     ranks = second.shape[1]
     place = lax.axis_index("gy")
+    inner = (place == 1) | (place == 2)
     width = 512 if flat % 512 == 0 else 256
-    for distance, block in enumerate(blocks):
+    columns = []
+    inside = lax.broadcasted_iota(jnp.int32, (ranks, rows), 1)
+    inside = inside % (rows // quads) * quads + inside // (rows // quads)
+    offset = lax.broadcasted_iota(jnp.int32, (ranks, rows), 0) - inside
+    for at, (distance, *options) in enumerate(blocks):
         owner = jnp.bitwise_xor(place, distance)
+        chosen = jnp.where(offset == owner * rows, 1.0, 0.0).astype(BF16)
+        columns.append(dot(second[...], chosen).astype(BF16))
         for start, count in pieces(rows):
-            unit = units(block, start, count, flat)
+            unit = units(options[0], start, count, flat)
+            if len(options) > 1:
+                unit = jnp.where(inner, unit, units(options[1], start, count, flat))
             for low in range(0, flat, LANES):
-                high, rest_of = split(decode(block[start : start + count, low : low + LANES], unit))
-                upper[owner, start : start + count, low : low + LANES] = high
-                lower[owner, start : start + count, low : low + LANES] = rest_of
-    shape = (ranks, count_y * rows)
-    column = lax.broadcasted_iota(jnp.int32, shape, 1)
-    inside = column % rows
-    groups = rows // quads
-    rank = column // rows * (rows * parts) + part * rows + inside % groups * quads + inside // groups
-    chosen = jnp.where(lax.broadcasted_iota(jnp.int32, shape, 0) == rank, 1.0, 0.0).astype(BF16)
-    columns = dot(second[...], chosen).astype(BF16)
-    together = count_y if rows % 16 == 0 else 1
+                codes = options[0][start : start + count, low : low + LANES].astype(F32)
+                if len(options) > 1:
+                    codes = jnp.where(
+                        inner, codes, options[1][start : start + count, low : low + LANES].astype(F32)
+                    )
+                high, rest_of = split(decode(codes, unit))
+                terms[2 * at, start : start + count, low : low + LANES] = high
+                terms[2 * at + 1, start : start + count, low : low + LANES] = rest_of
+    together = len(blocks) if rows % 16 == 0 else 1
     for low in range(0, flat, width):
         value = None if earlier is None else earlier[:, low : low + width]
-        for first in range(0, count_y, together):
-            left = columns[:, first * rows : (first + together) * rows]
-            for ref in (upper, lower):
-                right = ref[first : first + together, :, low : low + width].reshape(together * rows, width)
-                value = dot(left, right) if value is None else value + dot(left, right)
+        for at in range(0, len(blocks), together):
+            left = jnp.concatenate([columns[k // 2] for k in range(2 * at, 2 * (at + together))], axis=1)
+            right = [terms[k, :, low : low + width] for k in range(2 * at, 2 * (at + together))]
+            if rows % 16 == 0:
+                products = [dot(left, jnp.concatenate(right, axis=0))]
+            else:
+                products = [dot(columns[at], part) for part in right]
+            for product in products:
+                value = product if value is None else value + product
         total[:, low : low + width] = value
 
 
-def early_kernel(part, parts, depth, second, *rest):
-    blocks, (total, upper, lower) = rest[:-3], rest[-3:]
-    contract_second(part, parts, depth, second, blocks, upper, lower, total, None)
-
-
-def image_kernel(part, parts, depth, steps, second, depth_factor, waves, *rest):
-    rest, (image, upper, lower, mixed, spread) = rest[:-5], rest[-5:]
-    earlier, blocks = (rest[0], rest[1:]) if part > 0 else (None, rest)
-    contract_second(part, parts, depth, second, blocks, upper, lower, mixed, earlier)
+def early_kernel(depth, distances, second, *rest):
+    blocks, (total, terms) = rest[:-2], rest[-2:]
+    contract_second(depth, second, list(zip(distances, blocks)), total, None, terms)
+
+
+def image_kernel(depth, steps, distance, second, depth_factor, waves, earlier, *rest):
+    blocks, (image, terms, mixed, spread) = rest[:-4], rest[-4:]
+    contract_second(depth, second, [(distance, *blocks)], mixed, earlier, terms)
     flat = mixed.shape[1]
     cells = image.shape[0]
     levels = depth_factor.shape[0]
@@ -195,35 +202,52 @@
     shape = square.shape
     same = lax.broadcasted_iota(jnp.int32, shape, 0) // levels == lax.broadcasted_iota(jnp.int32, shape, 1) // depth
     square = jnp.where(same, square, 0.0).astype(BF16)
+    square = jnp.concatenate([square, square], axis=1)
     tiles = quads * levels // LANES
     contract = (((1,), (1,)), ((), ()))
     rest_x = cells // quads
-    for quad in range(mixed.shape[0] // quads):
-        turned = [
-            swap_groups(
-                [spread[(quad * quads + j) * pad + top : (quad * quads + j) * pad + top + 8, :] for j in range(quads)],
-                depth,
-            )
-            for top in range(0, pad, 8)
-        ]
-        high, rest_of = split(jnp.concatenate([piece[i] for i in range(quads) for piece in turned], axis=0))
-        source = lax.dot_general(high, square, contract, preferred_element_type=F32) + lax.dot_general(
-            rest_of, square, contract, preferred_element_type=F32
+    many = mixed.shape[0] // quads
+    batch = 4 if many % 4 == 0 else 1
+    for first in range(0, many, batch):
+        stack = []
+        for quad in range(first, first + batch):
+            turned = [
+                swap_groups(
+                    [
+                        spread[(quad * quads + j) * pad + top : (quad * quads + j) * pad + top + 8, :]
+                        for j in range(quads)
+                    ],
+                    depth,
+                )
+                for top in range(0, pad, 8)
+            ]
+            stack += [piece[i] for i in range(quads) for piece in turned]
+        high, rest_of = split(jnp.concatenate(stack, axis=0))
+        source = lax.dot_general(
+            jnp.concatenate([high, rest_of], axis=1), square, contract, preferred_element_type=F32
         )
-        for tile in range(tiles):
-            at = quad * tiles + tile
-            total = None
-            for step in range(steps):
-                value = jnp.concatenate(
-                    [
-                        source[i * pad + step * rest_x : i * pad + (step + 1) * rest_x, tile * LANES : (tile + 1) * LANES]
-                        for i in range(quads)
-                    ],
-                    axis=0,
-                )
-                value = value * waves[at, step * cells : (step + 1) * cells, :]
-                total = value if total is None else total + value
-            image[:, at * LANES : (at + 1) * LANES] = total
+        for quad in range(first, first + batch):
+            base = (quad - first) * quads * pad
+            for tile in range(tiles):
+                at = quad * tiles + tile
+                lanes = slice(tile * LANES, (tile + 1) * LANES)
+                total = None
+                for step in range(steps):
+                    value = jnp.concatenate(
+                        [
+                            source[base + i * pad + step * rest_x : base + i * pad + (step + 1) * rest_x, lanes]
+                            for i in range(quads)
+                        ],
+                        axis=0,
+                    )
+                    value = value * waves[at, step * cells : (step + 1) * cells, :]
+                    total = value if total is None else total + value
+                image[:, at * LANES : (at + 1) * LANES] = total
+
+
+def lift_kernel(core, factor, core_near, factor_near):
+    core_near[...] = core[...]
+    factor_near[...] = factor[...]
 
 
 def pack_kernel(pressure, previous, velocity, own, up, down):
@@ -309,6 +333,8 @@
     bands = jnp.concatenate([band_upper, band_upper, band_lower], axis=0)
     front = lax.broadcasted_iota(jnp.int32, (1, LANES), 1) < levels
     count = 4
+    for tile in list(range(edge - inner)) + list(range(edge + own_tiles + inner, 2 * edge + own_tiles)):
+        second[tile, :, :] = jnp.zeros((3 * cells, LANES), F32)
 
     def advance(now, before, shift, tile_shift, later, out_row, top, rows, tile):
         tiles = [now[tile + step, top : top + rows, :] for step in range(-2, count + 2)]
@@ -340,15 +366,16 @@
     chain = [(first, prior, half, edge - inner, second), (second, first, 0, 0, third), (third, second, 0, 0, None)]
     for step in range(steps):
         now, before, shift, tile_shift, later = chain[step]
-        margin = (steps - 1 - step) * (edge // steps)
-        tops = (cells - half, 2 * cells - half) if later is not None else (cells,)
+        top, rows = (cells - half, 2 * cells) if later is not None else (cells, cells)
+        margin = inner if later is not None else 0
 
         def loop(block, carry):
-            for top in tops:
-                advance(now, before, shift, tile_shift, later, step * cells, top, cells, edge - margin + count * block)
+            for group in range(2):
+                tile = edge - margin + 2 * count * block + group * count
+                advance(now, before, shift, tile_shift, later, step * cells, top, rows, tile)
             return carry
 
-        lax.fori_loop(0, (own_tiles + 2 * margin) // count, loop, 0)
+        lax.fori_loop(0, (own_tiles + 2 * margin) // (2 * count), loop, 0)
         if later is not None:
             for tile in range(own_tiles):
                 waves[tile, step * cells : (step + 1) * cells, :] = later[edge + tile, cells : 2 * cells, :]
@@ -380,29 +407,32 @@
     chips = count_x // 2
     span = 4 * steps * levels
     near = span * 2 // 3
-    parts = 2 if local_second % 32 == 0 else 1
-    rows = local_second // parts
-    share = core_flat // parts
-    groups_pad = (share // LANES + 7) // 8 * 8
+    groups_pad = (core_flat // LANES + 7) // 8 * 8
     lines_pad = (lines * depth // LANES + 7) // 8 * 8
 
     across = [[(i, 2 * ((i // 2) ^ distance) + i % 2) for i in range(count_x)] for distance in range(1, chips)]
-    factors = [first_factor] + [lax.ppermute(first_factor, "gx", route) for route in across]
+    factors = [lax.ppermute(first_factor, "gx", route) for route in across]
     other = lax.ppermute(tucker_core, "gx", [(i, i + 1 - 2 * (i % 2)) for i in range(count_x)])
-
-    outs = call(
-        functools.partial(project_kernel, chips, parts),
-        ([shape_of(lines, share)] + [shape_of(lines, share + LANES, dtype=BF16)] * (chips - 1)) * parts,
-        [pltpu.VMEM((chips - 1, lines, share), F32)],
+    core_near, factor_near = call(
+        lift_kernel,
+        [shape_of(*array.shape, dtype=BF16) for array in (tucker_core, first_factor)],
+        [],
+        1000,
+        tucker_core,
+        first_factor,
+    )
+    mine, *sends = call(
+        functools.partial(project_kernel, chips),
+        [shape_of(lines, core_flat)] + [shape_of(lines, core_flat + LANES, dtype=BF16)] * (chips - 1),
+        [pltpu.VMEM((chips - 1, lines, core_flat), F32)],
         4 * lines * chips * rank * core_flat,
-        tucker_core,
+        core_near,
         other,
+        factor_near,
         *factors,
     )
-    outs = [outs[part * chips : (part + 1) * chips] for part in range(parts)]
-    received = [[lax.ppermute(send, "gx", route) for send, route in zip(outs[0][1:], across)]]
-
-    pressure_later, _ = lax.optimization_barrier((pressure, outs[0][0]))
+    received = [lax.ppermute(send, "gx", route) for send, route in zip(sends, across)]
+    pressure_later, _ = lax.optimization_barrier((pressure, mine))
     own, up, down = call(
         pack_kernel,
         [shape_of(3 * cells, flat + LANES, dtype=BF16)] + [shape_of(3 * cells, span + LANES, dtype=BF16)] * 2,
@@ -414,45 +444,39 @@
     )
     low = lax.ppermute(up, "gy", [(i, i + 1) for i in range(count_y - 1)])
     high = lax.ppermute(down, "gy", [(i + 1, i) for i in range(count_y - 1)])
-    mixed, blocks = [], []
-    for part in range(parts):
-        if part + 1 < parts:
-            received[part], sends = lax.optimization_barrier((received[part], outs[part + 1][1:]))
-            received.append([lax.ppermute(send, "gx", route) for send, route in zip(sends, across)])
-        if part > 0:
-            received[part], blocks[1:3] = lax.optimization_barrier((received[part], blocks[1:3]))
-            mixed = call(
-                functools.partial(early_kernel, part - 1, parts, depth),
-                [shape_of(second_factor.shape[0], lines * depth)],
-                [pltpu.VMEM((count_y, rows, lines * depth), BF16)] * 2,
-                4 * second_factor.shape[0] * count_y * rows * lines * depth,
-                second_factor,
-                *blocks,
-            )
-        (codes,) = call(
-            functools.partial(gather_kernel, depth, steps),
-            [shape_of(rows, lines * depth + LANES, dtype=BF16)],
-            [pltpu.VMEM((lines * groups_pad, LANES), F32), pltpu.VMEM((rows, lines * depth), F32)],
-            30 * chips * lines * share,
-            outs[part][0],
-            *received[part],
-        )
-        if part == 0:
-            codes, low, high = lax.optimization_barrier((codes, low, high))
-            ahead, behind = call(
-                edge_kernel,
-                [shape_of(2 * cells, flat + 2 * near + 3 * LANES, dtype=BF16)] * 2,
-                [],
-                1000,
-                own,
-                low,
-                high,
-            )
-        if part == parts - 1:
-            codes, ahead, behind = lax.optimization_barrier((codes, ahead, behind))
-        blocks = [codes] + [
-            lax.ppermute(codes, "gy", [(i, i ^ distance) for i in range(count_y)]) for distance in range(1, count_y)
+
+    (codes,) = call(
+        functools.partial(gather_kernel, depth, steps),
+        [shape_of(local_second, lines * depth + LANES, dtype=BF16)],
+        [pltpu.VMEM((lines * groups_pad, LANES), F32), pltpu.VMEM((local_second, lines * depth), F32)],
+        30 * chips * lines * core_flat,
+        mine,
+        *received,
+    )
+    codes, low, high = lax.optimization_barrier((codes, low, high))
+    ahead, behind = call(
+        edge_kernel,
+        [shape_of(2 * cells, flat + 2 * near + 3 * LANES, dtype=BF16)] * 2,
+        [],
+        1000,
+        own,
+        low,
+        high,
+    )
+
+    def far(distance):
+        return lax.ppermute(codes, "gy", [(i, i ^ distance) for i in range(count_y)])
+
+    if count_y == 4:
+        blocks = [codes, far(1), far(2)]
+        codes_later, blocks[2] = lax.optimization_barrier((codes, blocks[2]))
+        last = [
+            lax.ppermute(codes_later, "gy", [(1, 2), (2, 1)]),
+            lax.ppermute(blocks[2], "gy", [(1, 0), (2, 3)]),
         ]
+    else:
+        blocks = [codes] + [far(distance) for distance in range(1, count_y - 1)]
+        last = [far(count_y - 1)]
 
     left = lax.ppermute(ahead, "gx", [(i, i + 1) for i in range(count_x - 1)])
     right = lax.ppermute(behind, "gx", [(i + 1, i) for i in range(count_x - 1)])
@@ -471,17 +495,28 @@
         high,
     )
     cells_y = second_factor.shape[0]
+    (mixed,) = call(
+        functools.partial(early_kernel, depth, tuple(range(count_y - 1))),
+        [shape_of(cells_y, lines * depth)],
+        [pltpu.VMEM((2 * (count_y - 1), local_second, lines * depth), BF16)],
+        4 * cells_y * count_y * local_second * lines * depth,
+        second_factor,
+        *blocks,
+    )
     (image,) = call(
-        functools.partial(image_kernel, parts - 1, parts, depth, steps),
+        functools.partial(image_kernel, depth, steps, count_y - 1),
         [shape_of(cells, flat)],
-        [pltpu.VMEM((count_y, rows, lines * depth), BF16)] * 2
-        + [pltpu.VMEM((cells_y, lines * depth), F32), pltpu.VMEM((cells_y * lines_pad, LANES), F32)],
-        4 * cells_y * count_y * rows * lines * depth,
+        [
+            pltpu.VMEM((2, local_second, lines * depth), BF16),
+            pltpu.VMEM((cells_y, lines * depth), F32),
+            pltpu.VMEM((cells_y * lines_pad, LANES), F32),
+        ],
+        4 * cells_y * local_second * lines * depth,
         second_factor,
         depth_factor,
         waves,
-        *mixed,
-        *blocks,
+        mixed,
+        *last,
     )
     return image
 

time: 67.2 us -> 59.6 us (0.89)
  the two profiles are of different devices: /device:TPU:12 before, /device:TPU:0 now
where the time goes in v2:
time: 59.6 us; the launch traced here: 59.2 us
  starting transfers between devices  21.9 us (37%)
  waiting for transfers between devices  20.2 us (34%)
  Pallas kernels  15 us (25%)
  local copies, waits for them, and re-layouts  1.99 us (3%)
    pallas_call x8, Pallas kernels, call(): pl.pallas_call(kernel, out_shape=outs, scratch_shapes=scratch, cost_estim...  15 us
    ppermute x2, waiting for transfers between devices, far(): lax.ppermute(codes, 'gy', [(i, i ^ distance) for i in range(count_y)])  11.5 us
    ppermute x3, waiting for transfers between devices, body(): lax.ppermute(send, 'gx', route)  5.83 us
    ppermute x2, starting transfers between devices, far(): lax.ppermute(codes, 'gy', [(i, i ^ distance) for i in range(count_y)])  4.29 us
    ppermute x3, starting transfers between devices, body(): factors = [lax.ppermute(first_factor, 'gx', route) for route in across]  4.11 us
    ppermute x3, starting transfers between devices, body(): lax.ppermute(send, 'gx', route)  3.55 us
    ppermute x1, starting transfers between devices, body(): low = lax.ppermute(up, 'gy', [(i, i + 1) for i in range(count_y - 1)])  3.49 us
    ppermute x3, waiting for transfers between devices, body(): factors = [lax.ppermute(first_factor, 'gx', route) for route in across]  2.82 us
  transfers between devices with their start and end apart: 15, of which 6 were waited for; matrix products, arithmetic and copies ran while one was open for 0% of the time, Pallas kernels for 18%

profile of v2, /device:TPU:0, one launch (start us, length us, event | category | flops | bytes accessed | tf_op | source)
XLA Modules:
  0.0 59.2 jit_solution(10602252314973650401)
XLA Ops:
  0.0 0.5 collective-permute-start
  0.5 2.6 %collective-permute-start.1 = (bf16[16,384]{1,0:T(8,128)(2,1)}, bf16[16,384]{1,0:T(8,128)(2,1)S(1)}, u32[]{:S(2)}, u32[]{:S(2)}) collective-permute-start(bf16[16,384]{1,0:T(8,128)(2,1)} %factor.1), channel_id=1, source_target_pairs={{0,8},{4,12},{8,0},{12,4},{16,24},{20,28},{24,16},{28,20},{1,9},{5... | collective-permute-start | bytes 36872 | tf_op jit(solution)/shard_map/ppermute | solution.py:414
  3.0 1.5 %collective-permute-start.2 = (bf16[16,384]{1,0:T(8,128)(2,1)}, bf16[16,384]{1,0:T(8,128)(2,1)S(1)}, u32[]{:S(2)}, u32[]{:S(2)}) collective-permute-start(bf16[16,384]{1,0:T(8,128)(2,1)} %factor.1), channel_id=1, source_target_pairs={{0,16},{4,20},{8,24},{12,28},{16,0},{20,4},{24,8},{28,12},{1,17},{... | collective-permute-start | bytes 36872 | tf_op jit(solution)/shard_map/ppermute | solution.py:414
  4.5 0.0 collective-permute-start.3
  4.6 1.2 %copy-done.2 = bf16[3,48,3072]{2,1,0:T(8,128)(2,1)S(1)} copy-done((bf16[3,48,3072]{2,1,0:T(8,128)(2,1)S(1)}, bf16[3,48,3072]{2,1,0:T(8,128)(2,1)}, u32[]{:S(2)}) %copy-start.2) | copy-done | bytes 884760
  5.7 0.7 %copy-done.5 = bf16[16,384]{1,0:T(8,128)(2,1)S(1)} copy-done((bf16[16,384]{1,0:T(8,128)(2,1)S(1)}, bf16[16,384]{1,0:T(8,128)(2,1)}, u32[]{:S(2)}) %copy-start.5) | copy-done | bytes 12312
  6.5 0.1 shard_map.73
  6.5 0.0 collective-permute-done.1.rest_1_
  6.5 0.4 collective-permute-done.2.rest_2_
  6.9 2.4 %collective-permute-done.3.rest_3_ = bf16[16,384]{1,0:T(8,128)(2,1)S(1)} collective-permute-done((bf16[16,384]{1,0:T(8,128)(2,1)}, bf16[16,384]{1,0:T(8,128)(2,1)S(1)}, u32[]{:S(2)}, u32[]{:S(2)}) %collective-permute-start.3) | collective-permute-done | bytes 12320 | tf_op jit(solution)/shard_map/ppermute | solution.py:414
  9.3 0.0 collective-permute-done.other
  9.3 1.4 %shard_map.74 = (f32[48,3072]{1,0:T(8,128)S(1)}, bf16[48,3200]{1,0:T(8,128)(2,1)S(1)}, bf16[48,3200]{1,0:T(8,128)(2,1)S(1)}, bf16[48,3200]{1,0:T(8,128)(2,1)S(1)}) custom-call(bf16[3,48,3072]{2,1,0:T(8,128)(2,1)S(1)} %get-tuple-element.22.core, bf16[3,48,3072]{2,1,0:T(8,128)(2,1)S(1)} %collective-permute-done.other, ...), custom_call_target="tpu_custom_call" | custom-call | flops 113246208 | bytes 3330048 | tf_op jit(solution)/shard_map/pallas_call | solution.py:387
  10.8 0.6 %collective-permute-start.4 = (bf16[48,3200]{1,0:T(8,128)(2,1)S(1)}, bf16[48,3200]{1,0:T(8,128)(2,1)S(1)}, u32[]{:S(2)}, u32[]{:S(2)}) collective-permute-start(bf16[48,3200]{1,0:T(8,128)(2,1)S(1)} %get-tuple-element.27), channel_id=1, source_target_pairs={{0,8},{4,12},{8,0},{12,4},{16,24},{20,28},{24,16},{28,20},{1,9},{5... | collective-permute-start | bytes 921608 | tf_op jit(solution)/shard_map/ppermute | solution.py:434
  11.4 0.1 collective-permute-start.5
  11.5 2.8 %collective-permute-start.6 = (bf16[48,3200]{1,0:T(8,128)(2,1)S(1)}, bf16[48,3200]{1,0:T(8,128)(2,1)S(1)}, u32[]{:S(2)}, u32[]{:S(2)}) collective-permute-start(bf16[48,3200]{1,0:T(8,128)(2,1)S(1)} %get-tuple-element.29), channel_id=1, source_target_pairs={{0,24},{4,28},{8,16},{12,20},{16,8},{20,12},{24,0},{28,4},{1,25},{... | collective-permute-start | bytes 921608 | tf_op jit(solution)/shard_map/ppermute | solution.py:434
  14.4 0.0 copy-done
  14.4 0.0 copy-done.1
  14.4 0.0 copy-done.3
  14.4 0.5 shard_map.75
  14.8 3.5 %collective-permute-start.7 = (bf16[48,896]{1,0:T(8,128)(2,1)S(1)}, bf16[48,896]{1,0:T(8,128)(2,1)S(1)}, u32[]{:S(2)}, u32[]{:S(2)}) collective-permute-start(bf16[48,896]{1,0:T(8,128)(2,1)S(1)} %get-tuple-element.30), channel_id=1, source_target_pairs={{0,1},{1,2},{2,3},{4,5},{5,6},{6,7},{8,9},{9,10},{10,11},{12,13},{... | collective-permute-start | bytes 258056 | tf_op jit(solution)/shard_map/ppermute | solution.py:445
  18.3 0.0 copy-start.6
  18.3 0.0 copy-start.4
  18.3 1.4 %collective-permute-start.8 = (bf16[48,896]{1,0:T(8,128)(2,1)S(1)}, bf16[48,896]{1,0:T(8,128)(2,1)S(1)}, u32[]{:S(2)}, u32[]{:S(2)}) collective-permute-start(bf16[48,896]{1,0:T(8,128)(2,1)S(1)} %get-tuple-element.31), channel_id=1, source_target_pairs={{1,0},{2,1},{3,2},{5,4},{6,5},{7,6},{9,8},{10,9},{11,10},{13,12},{... | collective-permute-start | bytes 258056 | tf_op jit(solution)/shard_map/ppermute | solution.py:446
  19.8 1.3 %collective-permute-done.4.rest_0_ = bf16[48,3200]{1,0:T(8,128)(2,1)S(1)} collective-permute-done((bf16[48,3200]{1,0:T(8,128)(2,1)S(1)}, bf16[48,3200]{1,0:T(8,128)(2,1)S(1)}, u32[]{:S(2)}, u32[]{:S(2)}) %collective-permute-start.4) | collective-permute-done | bytes 307232 | tf_op jit(solution)/shard_map/ppermute | solution.py:434
  21.1 4.5 %collective-permute-done.5.rest_1_ = bf16[48,3200]{1,0:T(8,128)(2,1)S(1)} collective-permute-done((bf16[48,3200]{1,0:T(8,128)(2,1)S(1)}, bf16[48,3200]{1,0:T(8,128)(2,1)S(1)}, u32[]{:S(2)}, u32[]{:S(2)}) %collective-permute-start.5) | collective-permute-done | bytes 307232 | tf_op jit(solution)/shard_map/ppermute | solution.py:434
  25.6 0.0 collective-permute-done.6.rest_2_
  25.6 1.9 %shard_map.76.rest_0_ = bf16[96,1664]{1,0:T(8,128)(2,1)S(1)} custom-call(f32[48,3072]{1,0:T(8,128)S(1)} %get-tuple-element.24.mine, bf16[48,3200]{1,0:T(8,128)(2,1)S(1)} %collective-permute-done.4.rest_0_, bf16[48,3200]{1,0:T(8,128)(2,1)S(1)} %collective-permute-done.5.rest_1_, bf16[48,3200]{1,0:T(8,128)(2,1)S(1)} %collective-permute-done.6.rest_2_), custom_call_target="tpu_custom_call" | custom-call | flops 17694720 | bytes 1830912 | tf_op jit(solution)/shard_map/pallas_call | solution.py:387
  27.5 0.0 collective-permute-done.7.low
  27.5 0.0 collective-permute-done.8.high
  27.6 2.7 %collective-permute-start.12 = (bf16[96,1664]{1,0:T(8,128)(2,1)S(1)}, bf16[96,1664]{1,0:T(8,128)(2,1)S(1)}, u32[]{:S(2)}, u32[]{:S(2)}) collective-permute-start(bf16[96,1664]{1,0:T(8,128)(2,1)S(1)} %shard_map.76.rest_0_), channel_id=1, source_target_pairs={{0,2},{1,3},{2,0},{3,1},{4,6},{5,7},{6,4},{7,5},{8,10},{9,11},{10,... | collective-permute-start | bytes 958472 | tf_op jit(solution)/shard_map/ppermute | solution.py:468
  30.2 1.0 %shard_map.77 = (bf16[32,7552]{1,0:T(8,128)(2,1)}, bf16[32,7552]{1,0:T(8,128)(2,1)}) custom-call(bf16[48,6272]{1,0:T(8,128)(2,1)S(1)} %get-tuple-element.26.own, bf16[48,896]{1,0:T(8,128)(2,1)S(1)} %collective-permute-done.7.low, bf16[48,896]{1,0:T(8,128)(2,1)S(1)} %collective-permute-done.8.high), custom_call_target="tpu_custom_call" | custom-call | flops 1000 | bytes 1740800 | tf_op jit(solution)/shard_map/pallas_call | solution.py:387
  31.2 1.3 %collective-permute-start.9 = (bf16[32,7552]{1,0:T(8,128)(2,1)}, bf16[32,7552]{1,0:T(8,128)(2,1)S(1)}, u32[]{:S(2)}, u32[]{:S(2)}) collective-permute-start(bf16[32,7552]{1,0:T(8,128)(2,1)} %get-tuple-element.34), channel_id=1, source_target_pairs={{0,4},{4,8},{8,12},{12,16},{16,20},{20,24},{24,28},{1,5},{5,9},{9,... | collective-permute-start | bytes 1449992 | tf_op jit(solution)/shard_map/ppermute | solution.py:481
  32.5 1.3 %collective-permute-start.10 = (bf16[32,7552]{1,0:T(8,128)(2,1)}, bf16[32,7552]{1,0:T(8,128)(2,1)S(1)}, u32[]{:S(2)}, u32[]{:S(2)}) collective-permute-start(bf16[32,7552]{1,0:T(8,128)(2,1)} %get-tuple-element.35), channel_id=1, source_target_pairs={{4,0},{8,4},{12,8},{16,12},{20,16},{24,20},{28,24},{5,1},{9,5},{13... | collective-permute-start | bytes 1449992 | tf_op jit(solution)/shard_map/ppermute | solution.py:482
  33.8 1.6 %collective-permute-start.11 = (bf16[96,1664]{1,0:T(8,128)(2,1)S(1)}, bf16[96,1664]{1,0:T(8,128)(2,1)S(1)}, u32[]{:S(2)}, u32[]{:S(2)}) collective-permute-start(bf16[96,1664]{1,0:T(8,128)(2,1)S(1)} %shard_map.76.rest_0_), channel_id=1, source_target_pairs={{0,1},{1,0},{2,3},{3,2},{4,5},{5,4},{6,7},{7,6},{8,9},{9,8},{10,11... | collective-permute-start | bytes 958472 | tf_op jit(solution)/shard_map/ppermute | solution.py:468
  35.5 6.9 %collective-permute-done.12.rest_2_ = bf16[96,1664]{1,0:T(8,128)(2,1)S(1)} collective-permute-done((bf16[96,1664]{1,0:T(8,128)(2,1)S(1)}, bf16[96,1664]{1,0:T(8,128)(2,1)S(1)}, u32[]{:S(2)}, u32[]{:S(2)}) %collective-permute-start.12) | collective-permute-done | bytes 319520 | tf_op jit(solution)/shard_map/ppermute | solution.py:468
  42.4 0.7 %collective-permute-start.13 = (bf16[96,1664]{1,0:T(8,128)(2,1)S(1)}, bf16[96,1664]{1,0:T(8,128)(2,1)S(1)}, u32[]{:S(2)}, u32[]{:S(2)}) collective-permute-start(bf16[96,1664]{1,0:T(8,128)(2,1)S(1)} %shard_map.76.rest_0_), channel_id=1, source_target_pairs={{1,2},{2,1},{5,6},{6,5},{9,10},{10,9},{13,14},{14,13},{17,18},{18,... | collective-permute-start | bytes 958472 | tf_op jit(solution)/shard_map/ppermute | solution.py:474
  43.1 1.3 %collective-permute-start.14 = (bf16[96,1664]{1,0:T(8,128)(2,1)S(1)}, bf16[96,1664]{1,0:T(8,128)(2,1)}, u32[]{:S(2)}, u32[]{:S(2)}) collective-permute-start(bf16[96,1664]{1,0:T(8,128)(2,1)S(1)} %collective-permute-done.12.rest_2_), channel_id=1, source_target_pairs={{1,0},{2,3},{5,4},{6,7},{9,8},{10,11},{13,12},{14,15},{17,16},{18,... | collective-permute-start | bytes 958472 | tf_op jit(solution)/shard_map/ppermute | solution.py:475
  44.4 0.0 copy-done.6
  44.4 0.1 copy.8.depth_factor
  44.5 4.6 %collective-permute-done.11.rest_1_ = bf16[96,1664]{1,0:T(8,128)(2,1)S(1)} collective-permute-done((bf16[96,1664]{1,0:T(8,128)(2,1)S(1)}, bf16[96,1664]{1,0:T(8,128)(2,1)S(1)}, u32[]{:S(2)}, u32[]{:S(2)}) %collective-permute-start.11) | collective-permute-done | bytes 319520 | tf_op jit(solution)/shard_map/ppermute | solution.py:468
  49.1 0.0 copy-done.4
  49.1 1.6 %shard_map.79.earlier = f32[96,1536]{1,0:T(8,128)S(1)} custom-call(bf16[96,384]{1,0:T(8,128)(2,1)S(1)} %copy-done.4, bf16[96,1664]{1,0:T(8,128)(2,1)S(1)} %shard_map.76.rest_0_, bf16[96,1664]{1,0:T(8,128)(2,1)S(1)} %collective-permute-done.11.rest_1_, bf16[96,1664]{1,0:T(8,128)(2,1)S(1)} %collective-permute-done.12.rest_2_), custom_call_target="tpu_custom_call" | custom-call | flops 226492416 | bytes 1622016 | tf_op jit(solution)/shard_map/pallas_call | solution.py:387
  50.7 0.0 collective-permute-done.9.left
  50.7 0.0 collective-permute-done.10.right
  50.7 5.3 %shard_map.78.waves = f32[48,48,128]{2,1,0:T(8,128)S(1)} custom-call(f32[16,6144]{1,0:T(8,128)S(1)} %copy-done, f32[16,6144]{1,0:T(8,128)S(1)} %copy-done.1, bf16[16,6144]{1,0:T(8,128)(2,1)S(1)} %copy-done.3, bf16[32,7552]{1,0:T(8,128)(2,1)S(1)} %collective-permute-done.9.left, bf16[32,7552]{1,0:T(8,128)(2,1)S(1)} %collective-permute-done.10.right, ...), custom_call_target="tpu_custom_call" | custom-call | flops 44236800 | bytes 3301376 | tf_op jit(solution)/shard_map/pallas_call | solution.py:387
  56.0 0.0 collective-permute-done.13.rest_0_
  56.0 0.0 collective-permute-done.14.rest_1_
  56.0 3.2 %shard_map.80 = f32[16,6144]{1,0:T(8,128)} custom-call(bf16[96,384]{1,0:T(8,128)(2,1)S(1)} %copy-done.4, bf16[64,32]{1,0:T(8,128)(2,1)S(1)} %copy.8.depth_factor, f32[48,48,128]{2,1,0:T(8,128)S(1)} %shard_map.78.waves, f32[96,1536]{1,0:T(8,128)S(1)} %shard_map.79.earlier, bf16[96,1664]{1,0:T(8,128)(2,1)S(1)} %collective-permute-done.13.rest_0_, ...), custom_call_target="tpu_custom_call" | custom-call | flops 56623104 | bytes 2879488 | tf_op jit(solution)/shard_map/pallas_call | solution.py:387
  (5 shorter events, 0.0 us)
Async XLA Ops:
  0.0 14.4 %copy-start = (f32[16,6144]{1,0:T(8,128)S(1)}, f32[16,6144]{1,0:T(8,128)}, u32[]{:S(2)}) copy-start(f32[16,6144]{1,0:T(8,128)} %pressure.2) | copy-start | bytes 1179652
  0.0 14.4 %copy-start.1 = (f32[16,6144]{1,0:T(8,128)S(1)}, f32[16,6144]{1,0:T(8,128)}, u32[]{:S(2)}) copy-start(f32[16,6144]{1,0:T(8,128)} %previous.3) | copy-start | bytes 1179652
  0.0 9.3 %collective-permute-start = (bf16[3,48,3072]{2,1,0:T(8,128)(2,1)}, bf16[3,48,3072]{2,1,0:T(8,128)(2,1)S(1)}, u32[]{:S(2)}, u32[]{:S(2)}) collective-permute-start(bf16[3,48,3072]{2,1,0:T(8,128)(2,1)} %core.1), channel_id=1, source_target_pairs={{0,4},{4,0},{8,12},{12,8},{16,20},{20,16},{24,28},{28,24},{1,5},{5... | collective-permute-start | bytes 2654216 | tf_op jit(solution)/shard_map/ppermute | solution.py:415
  0.5 6.1 %collective-permute-start.1 = (bf16[16,384]{1,0:T(8,128)(2,1)}, bf16[16,384]{1,0:T(8,128)(2,1)S(1)}, u32[]{:S(2)}, u32[]{:S(2)}) collective-permute-start(bf16[16,384]{1,0:T(8,128)(2,1)} %factor.1), channel_id=1, source_target_pairs={{0,8},{4,12},{8,0},{12,4},{16,24},{20,28},{24,16},{28,20},{1,9},{5... | collective-permute-start | bytes 36872 | tf_op jit(solution)/shard_map/ppermute | solution.py:414
  3.0 3.9 %collective-permute-start.2 = (bf16[16,384]{1,0:T(8,128)(2,1)}, bf16[16,384]{1,0:T(8,128)(2,1)S(1)}, u32[]{:S(2)}, u32[]{:S(2)}) collective-permute-start(bf16[16,384]{1,0:T(8,128)(2,1)} %factor.1), channel_id=1, source_target_pairs={{0,16},{4,20},{8,24},{12,28},{16,0},{20,4},{24,8},{28,12},{1,17},{... | collective-permute-start | bytes 36872 | tf_op jit(solution)/shard_map/ppermute | solution.py:414
  4.5 4.8 %collective-permute-start.3 = (bf16[16,384]{1,0:T(8,128)(2,1)}, bf16[16,384]{1,0:T(8,128)(2,1)S(1)}, u32[]{:S(2)}, u32[]{:S(2)}) collective-permute-start(bf16[16,384]{1,0:T(8,128)(2,1)} %factor.1), channel_id=1, source_target_pairs={{0,24},{4,28},{8,16},{12,20},{16,8},{20,12},{24,0},{28,4},{1,25},{... | collective-permute-start | bytes 36872 | tf_op jit(solution)/shard_map/ppermute | solution.py:414
  4.6 1.2 %copy-start.2 = (bf16[3,48,3072]{2,1,0:T(8,128)(2,1)S(1)}, bf16[3,48,3072]{2,1,0:T(8,128)(2,1)}, u32[]{:S(2)}) copy-start(bf16[3,48,3072]{2,1,0:T(8,128)(2,1)} %core.1) | copy-start | bytes 2654212
  5.7 0.7 %copy-start.5 = (bf16[16,384]{1,0:T(8,128)(2,1)S(1)}, bf16[16,384]{1,0:T(8,128)(2,1)}, u32[]{:S(2)}) copy-start(bf16[16,384]{1,0:T(8,128)(2,1)} %factor.1) | copy-start | bytes 36868
  6.4 7.9 %copy-start.3 = (bf16[16,6144]{1,0:T(8,128)(2,1)S(1)}, bf16[16,6144]{1,0:T(8,128)(2,1)}, u32[]{:S(2)}) copy-start(bf16[16,6144]{1,0:T(8,128)(2,1)} %velocity.3) | copy-start | bytes 589828
  10.8 10.3 %collective-permute-start.4 = (bf16[48,3200]{1,0:T(8,128)(2,1)S(1)}, bf16[48,3200]{1,0:T(8,128)(2,1)S(1)}, u32[]{:S(2)}, u32[]{:S(2)}) collective-permute-start(bf16[48,3200]{1,0:T(8,128)(2,1)S(1)} %get-tuple-element.27), channel_id=1, source_target_pairs={{0,8},{4,12},{8,0},{12,4},{16,24},{20,28},{24,16},{28,20},{1,9},{5... | collective-permute-start | bytes 921608 | tf_op jit(solution)/shard_map/ppermute | solution.py:434
  11.4 14.2 %collective-permute-start.5 = (bf16[48,3200]{1,0:T(8,128)(2,1)S(1)}, bf16[48,3200]{1,0:T(8,128)(2,1)S(1)}, u32[]{:S(2)}, u32[]{:S(2)}) collective-permute-start(bf16[48,3200]{1,0:T(8,128)(2,1)S(1)} %get-tuple-element.28), channel_id=1, source_target_pairs={{0,16},{4,20},{8,24},{12,28},{16,0},{20,4},{24,8},{28,12},{1,17},{... | collective-permute-start | bytes 921608 | tf_op jit(solution)/shard_map/ppermute | solution.py:434
  11.5 14.1 %collective-permute-start.6 = (bf16[48,3200]{1,0:T(8,128)(2,1)S(1)}, bf16[48,3200]{1,0:T(8,128)(2,1)S(1)}, u32[]{:S(2)}, u32[]{:S(2)}) collective-permute-start(bf16[48,3200]{1,0:T(8,128)(2,1)S(1)} %get-tuple-element.29), channel_id=1, source_target_pairs={{0,24},{4,28},{8,16},{12,20},{16,8},{20,12},{24,0},{28,4},{1,25},{... | collective-permute-start | bytes 921608 | tf_op jit(solution)/shard_map/ppermute | solution.py:434
  14.8 12.7 %collective-permute-start.7 = (bf16[48,896]{1,0:T(8,128)(2,1)S(1)}, bf16[48,896]{1,0:T(8,128)(2,1)S(1)}, u32[]{:S(2)}, u32[]{:S(2)}) collective-permute-start(bf16[48,896]{1,0:T(8,128)(2,1)S(1)} %get-tuple-element.30), channel_id=1, source_target_pairs={{0,1},{1,2},{2,3},{4,5},{5,6},{6,7},{8,9},{9,10},{10,11},{12,13},{... | collective-permute-start | bytes 258056 | tf_op jit(solution)/shard_map/ppermute | solution.py:445
  18.3 26.1 %copy-start.6 = (bf16[64,32]{0,1:T(8,128)(2,1)S(1)}, bf16[64,32]{0,1:T(8,128)(2,1)}, u32[]{:S(2)}) copy-start(bf16[64,32]{0,1:T(8,128)(2,1)} %param.13) | copy-start | bytes 12292
  18.3 30.7 %copy-start.4 = (bf16[96,384]{1,0:T(8,128)(2,1)S(1)}, bf16[96,384]{1,0:T(8,128)(2,1)}, u32[]{:S(2)}) copy-start(bf16[96,384]{1,0:T(8,128)(2,1)} %second.3) | copy-start | bytes 221188
  18.3 9.2 %collective-permute-start.8 = (bf16[48,896]{1,0:T(8,128)(2,1)S(1)}, bf16[48,896]{1,0:T(8,128)(2,1)S(1)}, u32[]{:S(2)}, u32[]{:S(2)}) collective-permute-start(bf16[48,896]{1,0:T(8,128)(2,1)S(1)} %get-tuple-element.31), channel_id=1, source_target_pairs={{1,0},{2,1},{3,2},{5,4},{6,5},{7,6},{9,8},{10,9},{11,10},{13,12},{... | collective-permute-start | bytes 258056 | tf_op jit(solution)/shard_map/ppermute | solution.py:446
  27.6 14.9 %collective-permute-start.12 = (bf16[96,1664]{1,0:T(8,128)(2,1)S(1)}, bf16[96,1664]{1,0:T(8,128)(2,1)S(1)}, u32[]{:S(2)}, u32[]{:S(2)}) collective-permute-start(bf16[96,1664]{1,0:T(8,128)(2,1)S(1)} %shard_map.76.rest_0_), channel_id=1, source_target_pairs={{0,2},{1,3},{2,0},{3,1},{4,6},{5,7},{6,4},{7,5},{8,10},{9,11},{10,... | collective-permute-start | bytes 958472 | tf_op jit(solution)/shard_map/ppermute | solution.py:468
  31.2 19.5 %collective-permute-start.9 = (bf16[32,7552]{1,0:T(8,128)(2,1)}, bf16[32,7552]{1,0:T(8,128)(2,1)S(1)}, u32[]{:S(2)}, u32[]{:S(2)}) collective-permute-start(bf16[32,7552]{1,0:T(8,128)(2,1)} %get-tuple-element.34), channel_id=1, source_target_pairs={{0,4},{4,8},{8,12},{12,16},{16,20},{20,24},{24,28},{1,5},{5,9},{9,... | collective-permute-start | bytes 1449992 | tf_op jit(solution)/shard_map/ppermute | solution.py:481
  32.5 18.2 %collective-permute-start.10 = (bf16[32,7552]{1,0:T(8,128)(2,1)}, bf16[32,7552]{1,0:T(8,128)(2,1)S(1)}, u32[]{:S(2)}, u32[]{:S(2)}) collective-permute-start(bf16[32,7552]{1,0:T(8,128)(2,1)} %get-tuple-element.35), channel_id=1, source_target_pairs={{4,0},{8,4},{12,8},{16,12},{20,16},{24,20},{28,24},{5,1},{9,5},{13... | collective-permute-start | bytes 1449992 | tf_op jit(solution)/shard_map/ppermute | solution.py:482
  33.8 15.2 %collective-permute-start.11 = (bf16[96,1664]{1,0:T(8,128)(2,1)S(1)}, bf16[96,1664]{1,0:T(8,128)(2,1)S(1)}, u32[]{:S(2)}, u32[]{:S(2)}) collective-permute-start(bf16[96,1664]{1,0:T(8,128)(2,1)S(1)} %shard_map.76.rest_0_), channel_id=1, source_target_pairs={{0,1},{1,0},{2,3},{3,2},{4,5},{5,4},{6,7},{7,6},{8,9},{9,8},{10,11... | collective-permute-start | bytes 958472 | tf_op jit(solution)/shard_map/ppermute | solution.py:468
  42.4 13.6 %collective-permute-start.13 = (bf16[96,1664]{1,0:T(8,128)(2,1)S(1)}, bf16[96,1664]{1,0:T(8,128)(2,1)S(1)}, u32[]{:S(2)}, u32[]{:S(2)}) collective-permute-start(bf16[96,1664]{1,0:T(8,128)(2,1)S(1)} %shard_map.76.rest_0_), channel_id=1, source_target_pairs={{1,2},{2,1},{5,6},{6,5},{9,10},{10,9},{13,14},{14,13},{17,18},{18,... | collective-permute-start | bytes 958472 | tf_op jit(solution)/shard_map/ppermute | solution.py:474
  43.1 12.9 %collective-permute-start.14 = (bf16[96,1664]{1,0:T(8,128)(2,1)S(1)}, bf16[96,1664]{1,0:T(8,128)(2,1)}, u32[]{:S(2)}, u32[]{:S(2)}) collective-permute-start(bf16[96,1664]{1,0:T(8,128)(2,1)S(1)} %collective-permute-done.12.rest_2_), channel_id=1, source_target_pairs={{1,0},{2,3},{5,4},{6,7},{9,8},{10,11},{13,12},{14,15},{17,16},{18,... | collective-permute-start | bytes 958472 | tf_op jit(solution)/shard_map/ppermute | solution.py:475

commit v3 on v2

--- a/solution.py
+++ b/solution.py
@@ -411,7 +411,7 @@
     lines_pad = (lines * depth // LANES + 7) // 8 * 8
 
     across = [[(i, 2 * ((i // 2) ^ distance) + i % 2) for i in range(count_x)] for distance in range(1, chips)]
-    factors = [lax.ppermute(first_factor, "gx", route) for route in across]
+    factors = [lax.ppermute(first_factor, "gx", route) for route in across[::-1]][::-1]
     other = lax.ppermute(tucker_core, "gx", [(i, i + 1 - 2 * (i % 2)) for i in range(count_x)])
     core_near, factor_near = call(
         lift_kernel,
@@ -445,15 +445,6 @@
     low = lax.ppermute(up, "gy", [(i, i + 1) for i in range(count_y - 1)])
     high = lax.ppermute(down, "gy", [(i + 1, i) for i in range(count_y - 1)])
 
-    (codes,) = call(
-        functools.partial(gather_kernel, depth, steps),
-        [shape_of(local_second, lines * depth + LANES, dtype=BF16)],
-        [pltpu.VMEM((lines * groups_pad, LANES), F32), pltpu.VMEM((local_second, lines * depth), F32)],
-        30 * chips * lines * core_flat,
-        mine,
-        *received,
-    )
-    codes, low, high = lax.optimization_barrier((codes, low, high))
     ahead, behind = call(
         edge_kernel,
         [shape_of(2 * cells, flat + 2 * near + 3 * LANES, dtype=BF16)] * 2,
@@ -464,18 +455,31 @@
         high,
     )
 
+    mine, ahead, behind = lax.optimization_barrier((mine, ahead, behind))
+    (codes,) = call(
+        functools.partial(gather_kernel, depth, steps),
+        [shape_of(local_second, lines * depth + LANES, dtype=BF16)],
+        [pltpu.VMEM((lines * groups_pad, LANES), F32), pltpu.VMEM((local_second, lines * depth), F32)],
+        30 * chips * lines * core_flat,
+        mine,
+        *received,
+    )
+    codes, ahead, behind = lax.optimization_barrier((codes, ahead, behind))
+
     def far(distance):
         return lax.ppermute(codes, "gy", [(i, i ^ distance) for i in range(count_y)])
 
     if count_y == 4:
-        blocks = [codes, far(1), far(2)]
-        codes_later, blocks[2] = lax.optimization_barrier((codes, blocks[2]))
+        distances = (0, 2, 1)
+        blocks = [codes, far(2), far(1)]
+        codes_later, blocks = lax.optimization_barrier((codes, blocks))
         last = [
             lax.ppermute(codes_later, "gy", [(1, 2), (2, 1)]),
-            lax.ppermute(blocks[2], "gy", [(1, 0), (2, 3)]),
+            lax.ppermute(blocks[1], "gy", [(1, 0), (2, 3)]),
         ]
     else:
-        blocks = [codes] + [far(distance) for distance in range(1, count_y - 1)]
+        distances = tuple(range(count_y - 1))
+        blocks = [codes] + [far(distance) for distance in distances[1:]]
         last = [far(count_y - 1)]
 
     left = lax.ppermute(ahead, "gx", [(i, i + 1) for i in range(count_x - 1)])
@@ -496,7 +500,7 @@
     )
     cells_y = second_factor.shape[0]
     (mixed,) = call(
-        functools.partial(early_kernel, depth, tuple(range(count_y - 1))),
+        functools.partial(early_kernel, depth, distances),
         [shape_of(cells_y, lines * depth)],
         [pltpu.VMEM((2 * (count_y - 1), local_second, lines * depth), BF16)],
         4 * cells_y * count_y * local_second * lines * depth,

time: 59.6 us -> 57.5 us (0.965)
  waiting for transfers between devices: 20.2 us -> 18.5 us
    ppermute x3, waiting for transfers between devices: 5.83 us -> 0.01 us  [body(): lax.ppermute(send, 'gx', route)]
    ppermute x1, waiting for transfers between devices: 0.01 us -> 4.3 us  [body(): high = lax.ppermute(down, 'gy', [(i + 1, i) for i in range(count_y - 1)])]
    ppermute x2, waiting for transfers between devices: 11.5 us -> 8.22 us  [far(): lax.ppermute(codes, 'gy', [(i, i ^ distance) for i in range(count_y)])]
    ppermute x4, waiting for transfers between devices: 2.82 us -> 5.15 us  [the longest x3 2.82 us: body(): lax.ppermute(first_factor, 'gx', route)]
    ppermute x1, waiting for transfers between devices: 0.01 us -> 0.78 us  [body(): low = lax.ppermute(up, 'gy', [(i, i + 1) for i in range(count_y - 1)])]
  transfers between devices with their start and end apart: 15 -> 15, of which waited for: 6 -> 7; matrix products, arithmetic and copies ran while one was open for 0% -> 0% of each run, Pallas kernels for 18% -> 15%
where the time goes in v3:
time: 57.5 us; the launch traced here: 57.2 us
  starting transfers between devices  21.6 us (38%)
  waiting for transfers between devices  18.5 us (32%)
  Pallas kernels  15 us (26%)
  local copies, waits for them, and re-layouts  1.99 us (3%)
    pallas_call x8, Pallas kernels, call(): pl.pallas_call(kernel, out_shape=outs, scratch_shapes=scratch, cost_estim...  15 us
    ppermute x2, waiting for transfers between devices, far(): lax.ppermute(codes, 'gy', [(i, i ^ distance) for i in range(count_y)])  8.22 us
    ppermute x1, waiting for transfers between devices, body(): high = lax.ppermute(down, 'gy', [(i + 1, i) for i in range(count_y - 1)])  4.3 us
    ppermute x3, starting transfers between devices, body(): lax.ppermute(first_factor, 'gx', route)  4.11 us
    ppermute x2, starting transfers between devices, far(): lax.ppermute(codes, 'gy', [(i, i ^ distance) for i in range(count_y)])  4.1 us
    ppermute x3, starting transfers between devices, body(): lax.ppermute(send, 'gx', route)  3.55 us
    ppermute x1, starting transfers between devices, body(): low = lax.ppermute(up, 'gy', [(i, i + 1) for i in range(count_y - 1)])  3.49 us
    ppermute x3, waiting for transfers between devices, body(): lax.ppermute(first_factor, 'gx', route)  2.82 us
  transfers between devices with their start and end apart: 15, of which 7 were waited for; matrix products, arithmetic and copies ran while one was open for 0% of the time, Pallas kernels for 15%

profile of v3, /device:TPU:0, one launch (start us, length us, event | category | flops | bytes accessed | tf_op | source)
XLA Modules:
  0.0 57.2 jit_solution(500065087656323859)
XLA Ops:
  0.0 0.0 copy-start
  0.0 0.0 copy-start.1
  0.0 0.5 collective-permute-start
  0.5 2.6 %collective-permute-start.1 = (bf16[16,384]{1,0:T(8,128)(2,1)}, bf16[16,384]{1,0:T(8,128)(2,1)S(1)}, u32[]{:S(2)}, u32[]{:S(2)}) collective-permute-start(bf16[16,384]{1,0:T(8,128)(2,1)} %factor.1), channel_id=1, source_target_pairs={{0,8},{4,12},{8,0},{12,4},{16,24},{20,28},{24,16},{28,20},{1,9},{5... | collective-permute-start | bytes 36872 | tf_op jit(solution)/shard_map/ppermute | solution.py:414
  3.0 1.5 %collective-permute-start.2 = (bf16[16,384]{1,0:T(8,128)(2,1)}, bf16[16,384]{1,0:T(8,128)(2,1)S(1)}, u32[]{:S(2)}, u32[]{:S(2)}) collective-permute-start(bf16[16,384]{1,0:T(8,128)(2,1)} %factor.1), channel_id=1, source_target_pairs={{0,16},{4,20},{8,24},{12,28},{16,0},{20,4},{24,8},{28,12},{1,17},{... | collective-permute-start | bytes 36872 | tf_op jit(solution)/shard_map/ppermute | solution.py:414
  4.5 0.0 collective-permute-start.3
  4.6 1.2 %copy-done.2 = bf16[3,48,3072]{2,1,0:T(8,128)(2,1)S(1)} copy-done((bf16[3,48,3072]{2,1,0:T(8,128)(2,1)S(1)}, bf16[3,48,3072]{2,1,0:T(8,128)(2,1)}, u32[]{:S(2)}) %copy-start.2) | copy-done | bytes 884760
  5.7 0.7 %copy-done.5 = bf16[16,384]{1,0:T(8,128)(2,1)S(1)} copy-done((bf16[16,384]{1,0:T(8,128)(2,1)S(1)}, bf16[16,384]{1,0:T(8,128)(2,1)}, u32[]{:S(2)}) %copy-start.5) | copy-done | bytes 12312
  6.5 0.1 shard_map.73
  6.5 0.0 collective-permute-done.1.rest_1_
  6.5 0.4 collective-permute-done.2.rest_2_
  6.9 2.4 %collective-permute-done.3.rest_3_ = bf16[16,384]{1,0:T(8,128)(2,1)S(1)} collective-permute-done((bf16[16,384]{1,0:T(8,128)(2,1)}, bf16[16,384]{1,0:T(8,128)(2,1)S(1)}, u32[]{:S(2)}, u32[]{:S(2)}) %collective-permute-start.3) | collective-permute-done | bytes 12320 | tf_op jit(solution)/shard_map/ppermute | solution.py:414
  9.3 0.0 collective-permute-done.other
  9.3 1.4 %shard_map.74 = (f32[48,3072]{1,0:T(8,128)S(1)}, bf16[48,3200]{1,0:T(8,128)(2,1)S(1)}, bf16[48,3200]{1,0:T(8,128)(2,1)S(1)}, bf16[48,3200]{1,0:T(8,128)(2,1)S(1)}) custom-call(bf16[3,48,3072]{2,1,0:T(8,128)(2,1)S(1)} %get-tuple-element.27.core, bf16[3,48,3072]{2,1,0:T(8,128)(2,1)S(1)} %collective-permute-done.other, ...), custom_call_target="tpu_custom_call" | custom-call | flops 113246208 | bytes 3330048 | tf_op jit(solution)/shard_map/pallas_call | solution.py:387
  10.8 0.6 %collective-permute-start.6 = (bf16[48,3200]{1,0:T(8,128)(2,1)S(1)}, bf16[48,3200]{1,0:T(8,128)(2,1)S(1)}, u32[]{:S(2)}, u32[]{:S(2)}) collective-permute-start(bf16[48,3200]{1,0:T(8,128)(2,1)S(1)} %get-tuple-element.37), channel_id=1, source_target_pairs={{0,8},{4,12},{8,0},{12,4},{16,24},{20,28},{24,16},{28,20},{1,9},{5... | collective-permute-start | bytes 921608 | tf_op jit(solution)/shard_map/ppermute | solution.py:434
  11.4 0.1 collective-permute-start.7
  11.5 2.8 %collective-permute-start.8 = (bf16[48,3200]{1,0:T(8,128)(2,1)S(1)}, bf16[48,3200]{1,0:T(8,128)(2,1)S(1)}, u32[]{:S(2)}, u32[]{:S(2)}) collective-permute-start(bf16[48,3200]{1,0:T(8,128)(2,1)S(1)} %get-tuple-element.39), channel_id=1, source_target_pairs={{0,24},{4,28},{8,16},{12,20},{16,8},{20,12},{24,0},{28,4},{1,25},{... | collective-permute-start | bytes 921608 | tf_op jit(solution)/shard_map/ppermute | solution.py:434
  14.4 0.0 copy-done
  14.4 0.0 copy-done.1
  14.4 0.0 copy-done.3
  14.4 0.5 shard_map.75
  14.8 3.5 %collective-permute-start.4 = (bf16[48,896]{1,0:T(8,128)(2,1)S(1)}, bf16[48,896]{1,0:T(8,128)(2,1)S(1)}, u32[]{:S(2)}, u32[]{:S(2)}) collective-permute-start(bf16[48,896]{1,0:T(8,128)(2,1)S(1)} %get-tuple-element.32), channel_id=1, source_target_pairs={{0,1},{1,2},{2,3},{4,5},{5,6},{6,7},{8,9},{9,10},{10,11},{12,13},{... | collective-permute-start | bytes 258056 | tf_op jit(solution)/shard_map/ppermute | solution.py:445
  18.3 1.3 %collective-permute-start.5 = (bf16[48,896]{1,0:T(8,128)(2,1)S(1)}, bf16[48,896]{1,0:T(8,128)(2,1)S(1)}, u32[]{:S(2)}, u32[]{:S(2)}) collective-permute-start(bf16[48,896]{1,0:T(8,128)(2,1)S(1)} %get-tuple-element.33), channel_id=1, source_target_pairs={{1,0},{2,1},{3,2},{5,4},{6,5},{7,6},{9,8},{10,9},{11,10},{13,12},{... | collective-permute-start | bytes 258056 | tf_op jit(solution)/shard_map/ppermute | solution.py:446
  19.6 0.8 %collective-permute-done.4.low = bf16[48,896]{1,0:T(8,128)(2,1)S(1)} collective-permute-done((bf16[48,896]{1,0:T(8,128)(2,1)S(1)}, bf16[48,896]{1,0:T(8,128)(2,1)S(1)}, u32[]{:S(2)}, u32[]{:S(2)}) %collective-permute-start.4) | collective-permute-done | bytes 86048 | tf_op jit(solution)/shard_map/ppermute | solution.py:445
  20.4 4.3 %collective-permute-done.5.high = bf16[48,896]{1,0:T(8,128)(2,1)S(1)} collective-permute-done((bf16[48,896]{1,0:T(8,128)(2,1)S(1)}, bf16[48,896]{1,0:T(8,128)(2,1)S(1)}, u32[]{:S(2)}, u32[]{:S(2)}) %collective-permute-start.5) | collective-permute-done | bytes 86048 | tf_op jit(solution)/shard_map/ppermute | solution.py:446
  24.7 1.0 %shard_map.76 = (bf16[32,7552]{1,0:T(8,128)(2,1)}, bf16[32,7552]{1,0:T(8,128)(2,1)}) custom-call(bf16[48,6272]{1,0:T(8,128)(2,1)S(1)} %get-tuple-element.31.own, bf16[48,896]{1,0:T(8,128)(2,1)S(1)} %collective-permute-done.4.low, bf16[48,896]{1,0:T(8,128)(2,1)S(1)} %collective-permute-done.5.high), custom_call_target="tpu_custom_call" | custom-call | flops 1000 | bytes 1740800 | tf_op jit(solution)/shard_map/pallas_call | solution.py:387
  25.7 0.0 collective-permute-done.6.rest_0_
  25.7 0.0 collective-permute-done.7.rest_1_
  25.7 0.0 collective-permute-done.8.rest_2_
  25.7 1.9 %shard_map.77.rest_0_ = bf16[96,1664]{1,0:T(8,128)(2,1)S(1)} custom-call(f32[48,3072]{1,0:T(8,128)S(1)} %get-tuple-element.36.mine, bf16[48,3200]{1,0:T(8,128)(2,1)S(1)} %collective-permute-done.6.rest_0_, bf16[48,3200]{1,0:T(8,128)(2,1)S(1)} %collective-permute-done.7.rest_1_, bf16[48,3200]{1,0:T(8,128)(2,1)S(1)} %collective-permute-done.8.rest_2_), custom_call_target="tpu_custom_call" | custom-call | flops 17694720 | bytes 1830912 | tf_op jit(solution)/shard_map/pallas_call | solution.py:387
  27.7 2.7 %collective-permute-start.11 = (bf16[96,1664]{1,0:T(8,128)(2,1)S(1)}, bf16[96,1664]{1,0:T(8,128)(2,1)S(1)}, u32[]{:S(2)}, u32[]{:S(2)}) collective-permute-start(bf16[96,1664]{1,0:T(8,128)(2,1)S(1)} %shard_map.77.rest_0_), channel_id=1, source_target_pairs={{0,2},{1,3},{2,0},{3,1},{4,6},{5,7},{6,4},{7,5},{8,10},{9,11},{10,... | collective-permute-start | bytes 958472 | tf_op jit(solution)/shard_map/ppermute | solution.py:470
  30.3 1.4 %collective-permute-start.12 = (bf16[96,1664]{1,0:T(8,128)(2,1)S(1)}, bf16[96,1664]{1,0:T(8,128)(2,1)S(1)}, u32[]{:S(2)}, u32[]{:S(2)}) collective-permute-start(bf16[96,1664]{1,0:T(8,128)(2,1)S(1)} %shard_map.77.rest_0_), channel_id=1, source_target_pairs={{0,1},{1,0},{2,3},{3,2},{4,5},{5,4},{6,7},{7,6},{8,9},{9,8},{10,11... | collective-permute-start | bytes 958472 | tf_op jit(solution)/shard_map/ppermute | solution.py:470
  31.8 1.3 %collective-permute-start.9 = (bf16[32,7552]{1,0:T(8,128)(2,1)}, bf16[32,7552]{1,0:T(8,128)(2,1)S(1)}, u32[]{:S(2)}, u32[]{:S(2)}) collective-permute-start(bf16[32,7552]{1,0:T(8,128)(2,1)} %get-tuple-element.42), channel_id=1, source_target_pairs={{0,4},{4,8},{8,12},{12,16},{16,20},{20,24},{24,28},{1,5},{5,9},{9,... | collective-permute-start | bytes 1449992 | tf_op jit(solution)/shard_map/ppermute | solution.py:485
  33.1 1.3 %collective-permute-start.10 = (bf16[32,7552]{1,0:T(8,128)(2,1)}, bf16[32,7552]{1,0:T(8,128)(2,1)S(1)}, u32[]{:S(2)}, u32[]{:S(2)}) collective-permute-start(bf16[32,7552]{1,0:T(8,128)(2,1)} %get-tuple-element.43), channel_id=1, source_target_pairs={{4,0},{8,4},{12,8},{16,12},{20,16},{24,20},{28,24},{5,1},{9,5},{13... | collective-permute-start | bytes 1449992 | tf_op jit(solution)/shard_map/ppermute | solution.py:486
  34.4 8.0 %collective-permute-done.11.rest_1_ = bf16[96,1664]{1,0:T(8,128)(2,1)S(1)} collective-permute-done((bf16[96,1664]{1,0:T(8,128)(2,1)S(1)}, bf16[96,1664]{1,0:T(8,128)(2,1)S(1)}, u32[]{:S(2)}, u32[]{:S(2)}) %collective-permute-start.11) | collective-permute-done | bytes 319520 | tf_op jit(solution)/shard_map/ppermute | solution.py:470
  42.4 0.2 collective-permute-done.12.rest_2_
  42.6 0.7 %collective-permute-start.13 = (bf16[96,1664]{1,0:T(8,128)(2,1)S(1)}, bf16[96,1664]{1,0:T(8,128)(2,1)S(1)}, u32[]{:S(2)}, u32[]{:S(2)}) collective-permute-start(bf16[96,1664]{1,0:T(8,128)(2,1)S(1)} %shard_map.77.rest_0_), channel_id=1, source_target_pairs={{1,2},{2,1},{5,6},{6,5},{9,10},{10,9},{13,14},{14,13},{17,18},{18,... | collective-permute-start | bytes 958472 | tf_op jit(solution)/shard_map/ppermute | solution.py:477
  43.3 1.3 %collective-permute-start.14 = (bf16[96,1664]{1,0:T(8,128)(2,1)S(1)}, bf16[96,1664]{1,0:T(8,128)(2,1)}, u32[]{:S(2)}, u32[]{:S(2)}) collective-permute-start(bf16[96,1664]{1,0:T(8,128)(2,1)S(1)} %collective-permute-done.11.rest_1_), channel_id=1, source_target_pairs={{1,0},{2,3},{5,4},{6,7},{9,8},{10,11},{13,12},{14,15},{17,16},{18,... | collective-permute-start | bytes 958472 | tf_op jit(solution)/shard_map/ppermute | solution.py:478
  44.6 0.0 copy-done.6
  44.6 0.1 copy.8.depth_factor
  44.7 0.0 copy-done.4
  44.7 1.6 %shard_map.79.earlier = f32[96,1536]{1,0:T(8,128)S(1)} custom-call(bf16[96,384]{1,0:T(8,128)(2,1)S(1)} %copy-done.4, bf16[96,1664]{1,0:T(8,128)(2,1)S(1)} %shard_map.77.rest_0_, bf16[96,1664]{1,0:T(8,128)(2,1)S(1)} %collective-permute-done.11.rest_1_, bf16[96,1664]{1,0:T(8,128)(2,1)S(1)} %collective-permute-done.12.rest_2_), custom_call_target="tpu_custom_call" | custom-call | flops 226492416 | bytes 1622016 | tf_op jit(solution)/shard_map/pallas_call | solution.py:387
  46.3 0.0 collective-permute-done.9.left
  46.3 0.0 collective-permute-done.10.right
  46.3 5.3 %shard_map.78.waves = f32[48,48,128]{2,1,0:T(8,128)S(1)} custom-call(f32[16,6144]{1,0:T(8,128)S(1)} %copy-done, f32[16,6144]{1,0:T(8,128)S(1)} %copy-done.1, bf16[16,6144]{1,0:T(8,128)(2,1)S(1)} %copy-done.3, bf16[32,7552]{1,0:T(8,128)(2,1)S(1)} %collective-permute-done.9.left, bf16[32,7552]{1,0:T(8,128)(2,1)S(1)} %collective-permute-done.10.right, ...), custom_call_target="tpu_custom_call" | custom-call | flops 44236800 | bytes 3301376 | tf_op jit(solution)/shard_map/pallas_call | solution.py:387
  51.6 0.0 collective-permute-done.13.rest_0_
  51.6 2.3 %collective-permute-done.14.rest_1_ = bf16[96,1664]{1,0:T(8,128)(2,1)} collective-permute-done((bf16[96,1664]{1,0:T(8,128)(2,1)S(1)}, bf16[96,1664]{1,0:T(8,128)(2,1)}, u32[]{:S(2)}, u32[]{:S(2)}) %collective-permute-start.14) | collective-permute-done | bytes 319520 | tf_op jit(solution)/shard_map/ppermute | solution.py:478
  54.0 3.2 %shard_map.80 = f32[16,6144]{1,0:T(8,128)} custom-call(bf16[96,384]{1,0:T(8,128)(2,1)S(1)} %copy-done.4, bf16[64,32]{1,0:T(8,128)(2,1)S(1)} %copy.8.depth_factor, f32[48,48,128]{2,1,0:T(8,128)S(1)} %shard_map.78.waves, f32[96,1536]{1,0:T(8,128)S(1)} %shard_map.79.earlier, bf16[96,1664]{1,0:T(8,128)(2,1)S(1)} %collective-permute-done.13.rest_0_, ...), custom_call_target="tpu_custom_call" | custom-call | flops 56623104 | bytes 2879488 | tf_op jit(solution)/shard_map/pallas_call | solution.py:387
  (5 shorter events, 0.0 us)
Async XLA Ops:
  0.0 14.4 %copy-start = (f32[16,6144]{1,0:T(8,128)S(1)}, f32[16,6144]{1,0:T(8,128)}, u32[]{:S(2)}) copy-start(f32[16,6144]{1,0:T(8,128)} %pressure.2) | copy-start | bytes 1179652
  0.0 14.4 %copy-start.1 = (f32[16,6144]{1,0:T(8,128)S(1)}, f32[16,6144]{1,0:T(8,128)}, u32[]{:S(2)}) copy-start(f32[16,6144]{1,0:T(8,128)} %previous.3) | copy-start | bytes 1179652
  0.0 9.3 %collective-permute-start = (bf16[3,48,3072]{2,1,0:T(8,128)(2,1)}, bf16[3,48,3072]{2,1,0:T(8,128)(2,1)S(1)}, u32[]{:S(2)}, u32[]{:S(2)}) collective-permute-start(bf16[3,48,3072]{2,1,0:T(8,128)(2,1)} %core.1), channel_id=1, source_target_pairs={{0,4},{4,0},{8,12},{12,8},{16,20},{20,16},{24,28},{28,24},{1,5},{5... | collective-permute-start | bytes 2654216 | tf_op jit(solution)/shard_map/ppermute | solution.py:415
  0.5 6.1 %collective-permute-start.1 = (bf16[16,384]{1,0:T(8,128)(2,1)}, bf16[16,384]{1,0:T(8,128)(2,1)S(1)}, u32[]{:S(2)}, u32[]{:S(2)}) collective-permute-start(bf16[16,384]{1,0:T(8,128)(2,1)} %factor.1), channel_id=1, source_target_pairs={{0,8},{4,12},{8,0},{12,4},{16,24},{20,28},{24,16},{28,20},{1,9},{5... | collective-permute-start | bytes 36872 | tf_op jit(solution)/shard_map/ppermute | solution.py:414
  3.0 3.9 %collective-permute-start.2 = (bf16[16,384]{1,0:T(8,128)(2,1)}, bf16[16,384]{1,0:T(8,128)(2,1)S(1)}, u32[]{:S(2)}, u32[]{:S(2)}) collective-permute-start(bf16[16,384]{1,0:T(8,128)(2,1)} %factor.1), channel_id=1, source_target_pairs={{0,16},{4,20},{8,24},{12,28},{16,0},{20,4},{24,8},{28,12},{1,17},{... | collective-permute-start | bytes 36872 | tf_op jit(solution)/shard_map/ppermute | solution.py:414
  4.5 4.8 %collective-permute-start.3 = (bf16[16,384]{1,0:T(8,128)(2,1)}, bf16[16,384]{1,0:T(8,128)(2,1)S(1)}, u32[]{:S(2)}, u32[]{:S(2)}) collective-permute-start(bf16[16,384]{1,0:T(8,128)(2,1)} %factor.1), channel_id=1, source_target_pairs={{0,24},{4,28},{8,16},{12,20},{16,8},{20,12},{24,0},{28,4},{1,25},{... | collective-permute-start | bytes 36872 | tf_op jit(solution)/shard_map/ppermute | solution.py:414
  4.6 1.2 %copy-start.2 = (bf16[3,48,3072]{2,1,0:T(8,128)(2,1)S(1)}, bf16[3,48,3072]{2,1,0:T(8,128)(2,1)}, u32[]{:S(2)}) copy-start(bf16[3,48,3072]{2,1,0:T(8,128)(2,1)} %core.1) | copy-start | bytes 2654212
  5.7 0.7 %copy-start.5 = (bf16[16,384]{1,0:T(8,128)(2,1)S(1)}, bf16[16,384]{1,0:T(8,128)(2,1)}, u32[]{:S(2)}) copy-start(bf16[16,384]{1,0:T(8,128)(2,1)} %factor.1) | copy-start | bytes 36868
  6.4 7.9 %copy-start.3 = (bf16[16,6144]{1,0:T(8,128)(2,1)S(1)}, bf16[16,6144]{1,0:T(8,128)(2,1)}, u32[]{:S(2)}) copy-start(bf16[16,6144]{1,0:T(8,128)(2,1)} %velocity.3) | copy-start | bytes 589828
  10.8 14.9 %collective-permute-start.6 = (bf16[48,3200]{1,0:T(8,128)(2,1)S(1)}, bf16[48,3200]{1,0:T(8,128)(2,1)S(1)}, u32[]{:S(2)}, u32[]{:S(2)}) collective-permute-start(bf16[48,3200]{1,0:T(8,128)(2,1)S(1)} %get-tuple-element.37), channel_id=1, source_target_pairs={{0,8},{4,12},{8,0},{12,4},{16,24},{20,28},{24,16},{28,20},{1,9},{5... | collective-permute-start | bytes 921608 | tf_op jit(solution)/shard_map/ppermute | solution.py:434
  11.4 14.3 %collective-permute-start.7 = (bf16[48,3200]{1,0:T(8,128)(2,1)S(1)}, bf16[48,3200]{1,0:T(8,128)(2,1)S(1)}, u32[]{:S(2)}, u32[]{:S(2)}) collective-permute-start(bf16[48,3200]{1,0:T(8,128)(2,1)S(1)} %get-tuple-element.38), channel_id=1, source_target_pairs={{0,16},{4,20},{8,24},{12,28},{16,0},{20,4},{24,8},{28,12},{1,17},{... | collective-permute-start | bytes 921608 | tf_op jit(solution)/shard_map/ppermute | solution.py:434
  11.5 14.2 %collective-permute-start.8 = (bf16[48,3200]{1,0:T(8,128)(2,1)S(1)}, bf16[48,3200]{1,0:T(8,128)(2,1)S(1)}, u32[]{:S(2)}, u32[]{:S(2)}) collective-permute-start(bf16[48,3200]{1,0:T(8,128)(2,1)S(1)} %get-tuple-element.39), channel_id=1, source_target_pairs={{0,24},{4,28},{8,16},{12,20},{16,8},{20,12},{24,0},{28,4},{1,25},{... | collective-permute-start | bytes 921608 | tf_op jit(solution)/shard_map/ppermute | solution.py:434
  14.8 5.6 %collective-permute-start.4 = (bf16[48,896]{1,0:T(8,128)(2,1)S(1)}, bf16[48,896]{1,0:T(8,128)(2,1)S(1)}, u32[]{:S(2)}, u32[]{:S(2)}) collective-permute-start(bf16[48,896]{1,0:T(8,128)(2,1)S(1)} %get-tuple-element.32), channel_id=1, source_target_pairs={{0,1},{1,2},{2,3},{4,5},{5,6},{6,7},{8,9},{9,10},{10,11},{12,13},{... | collective-permute-start | bytes 258056 | tf_op jit(solution)/shard_map/ppermute | solution.py:445
  18.3 6.4 %collective-permute-start.5 = (bf16[48,896]{1,0:T(8,128)(2,1)S(1)}, bf16[48,896]{1,0:T(8,128)(2,1)S(1)}, u32[]{:S(2)}, u32[]{:S(2)}) collective-permute-start(bf16[48,896]{1,0:T(8,128)(2,1)S(1)} %get-tuple-element.33), channel_id=1, source_target_pairs={{1,0},{2,1},{3,2},{5,4},{6,5},{7,6},{9,8},{10,9},{11,10},{13,12},{... | collective-permute-start | bytes 258056 | tf_op jit(solution)/shard_map/ppermute | solution.py:446
  24.7 19.9 %copy-start.6 = (bf16[64,32]{0,1:T(8,128)(2,1)S(1)}, bf16[64,32]{0,1:T(8,128)(2,1)}, u32[]{:S(2)}) copy-start(bf16[64,32]{0,1:T(8,128)(2,1)} %param.13) | copy-start | bytes 12292
  24.7 20.0 %copy-start.4 = (bf16[96,384]{1,0:T(8,128)(2,1)S(1)}, bf16[96,384]{1,0:T(8,128)(2,1)}, u32[]{:S(2)}) copy-start(bf16[96,384]{1,0:T(8,128)(2,1)} %second.3) | copy-start | bytes 221188
  27.7 14.7 %collective-permute-start.11 = (bf16[96,1664]{1,0:T(8,128)(2,1)S(1)}, bf16[96,1664]{1,0:T(8,128)(2,1)S(1)}, u32[]{:S(2)}, u32[]{:S(2)}) collective-permute-start(bf16[96,1664]{1,0:T(8,128)(2,1)S(1)} %shard_map.77.rest_0_), channel_id=1, source_target_pairs={{0,2},{1,3},{2,0},{3,1},{4,6},{5,7},{6,4},{7,5},{8,10},{9,11},{10,... | collective-permute-start | bytes 958472 | tf_op jit(solution)/shard_map/ppermute | solution.py:470
  30.3 12.3 %collective-permute-start.12 = (bf16[96,1664]{1,0:T(8,128)(2,1)S(1)}, bf16[96,1664]{1,0:T(8,128)(2,1)S(1)}, u32[]{:S(2)}, u32[]{:S(2)}) collective-permute-start(bf16[96,1664]{1,0:T(8,128)(2,1)S(1)} %shard_map.77.rest_0_), channel_id=1, source_target_pairs={{0,1},{1,0},{2,3},{3,2},{4,5},{5,4},{6,7},{7,6},{8,9},{9,8},{10,11... | collective-permute-start | bytes 958472 | tf_op jit(solution)/shard_map/ppermute | solution.py:470
  31.8 14.6 %collective-permute-start.9 = (bf16[32,7552]{1,0:T(8,128)(2,1)}, bf16[32,7552]{1,0:T(8,128)(2,1)S(1)}, u32[]{:S(2)}, u32[]{:S(2)}) collective-permute-start(bf16[32,7552]{1,0:T(8,128)(2,1)} %get-tuple-element.42), channel_id=1, source_target_pairs={{0,4},{4,8},{8,12},{12,16},{16,20},{20,24},{24,28},{1,5},{5,9},{9,... | collective-permute-start | bytes 1449992 | tf_op jit(solution)/shard_map/ppermute | solution.py:485
  33.1 13.3 %collective-permute-start.10 = (bf16[32,7552]{1,0:T(8,128)(2,1)}, bf16[32,7552]{1,0:T(8,128)(2,1)S(1)}, u32[]{:S(2)}, u32[]{:S(2)}) collective-permute-start(bf16[32,7552]{1,0:T(8,128)(2,1)} %get-tuple-element.43), channel_id=1, source_target_pairs={{4,0},{8,4},{12,8},{16,12},{20,16},{24,20},{28,24},{5,1},{9,5},{13... | collective-permute-start | bytes 1449992 | tf_op jit(solution)/shard_map/ppermute | solution.py:486
  42.6 9.0 %collective-permute-start.13 = (bf16[96,1664]{1,0:T(8,128)(2,1)S(1)}, bf16[96,1664]{1,0:T(8,128)(2,1)S(1)}, u32[]{:S(2)}, u32[]{:S(2)}) collective-permute-start(bf16[96,1664]{1,0:T(8,128)(2,1)S(1)} %shard_map.77.rest_0_), channel_id=1, source_target_pairs={{1,2},{2,1},{5,6},{6,5},{9,10},{10,9},{13,14},{14,13},{17,18},{18,... | collective-permute-start | bytes 958472 | tf_op jit(solution)/shard_map/ppermute | solution.py:477
  43.3 10.7 %collective-permute-start.14 = (bf16[96,1664]{1,0:T(8,128)(2,1)S(1)}, bf16[96,1664]{1,0:T(8,128)(2,1)}, u32[]{:S(2)}, u32[]{:S(2)}) collective-permute-start(bf16[96,1664]{1,0:T(8,128)(2,1)S(1)} %collective-permute-done.11.rest_1_), channel_id=1, source_target_pairs={{1,0},{2,3},{5,4},{6,7},{9,8},{10,11},{13,12},{14,15},{17,16},{18,... | collective-permute-start | bytes 958472 | tf_op jit(solution)/shard_map/ppermute | solution.py:478

commit v4 on v3

--- a/solution.py
+++ b/solution.py
@@ -76,13 +76,14 @@
     return [(start, 16) for start in range(0, rows, 16)] if rows % 16 == 0 else [(0, rows)]
 
 
-def project_kernel(chips, core, other, *rest):
-    factors, mine, sends, (partial,) = rest[:chips], rest[chips], rest[chips + 1 : -1], rest[-1:]
+def project_kernel(core, other, factors, mine, *rest):
+    sends, (partial,) = rest[:-1], rest[-1:]
+    chips = factors.shape[0]
     steps, rank, flat = core.shape
     lines = mine.shape[0]
     cells = lines // steps
     place = lax.axis_index("gx")
-    factor = jnp.concatenate([ref[...] for ref in factors], axis=0)
+    factor = jnp.concatenate([factors[jnp.bitwise_xor(place // 2, distance)] for distance in range(chips)], axis=0)
     offset = lax.broadcasted_iota(jnp.int32, (factor.shape[1], rank), 0) - lax.broadcasted_iota(
         jnp.int32, (factor.shape[1], rank), 1
     )
@@ -245,9 +246,8 @@
                 image[:, at * LANES : (at + 1) * LANES] = total
 
 
-def lift_kernel(core, factor, core_near, factor_near):
+def lift_kernel(core, core_near):
     core_near[...] = core[...]
-    factor_near[...] = factor[...]
 
 
 def pack_kernel(pressure, previous, velocity, own, up, down):
@@ -411,25 +411,23 @@
     lines_pad = (lines * depth // LANES + 7) // 8 * 8
 
     across = [[(i, 2 * ((i // 2) ^ distance) + i % 2) for i in range(count_x)] for distance in range(1, chips)]
-    factors = [lax.ppermute(first_factor, "gx", route) for route in across[::-1]][::-1]
     other = lax.ppermute(tucker_core, "gx", [(i, i + 1 - 2 * (i % 2)) for i in range(count_x)])
-    core_near, factor_near = call(
-        lift_kernel,
-        [shape_of(*array.shape, dtype=BF16) for array in (tucker_core, first_factor)],
-        [],
-        1000,
-        tucker_core,
-        first_factor,
-    )
+    factors = lax.all_to_all(
+        jnp.broadcast_to(first_factor, (chips, *first_factor.shape)),
+        "gx",
+        0,
+        0,
+        axis_index_groups=[list(range(side, count_x, 2)) for side in range(2)],
+    )
+    (core_near,) = call(lift_kernel, [shape_of(*tucker_core.shape, dtype=BF16)], [], 1000, tucker_core)
     mine, *sends = call(
-        functools.partial(project_kernel, chips),
+        project_kernel,
         [shape_of(lines, core_flat)] + [shape_of(lines, core_flat + LANES, dtype=BF16)] * (chips - 1),
         [pltpu.VMEM((chips - 1, lines, core_flat), F32)],
         4 * lines * chips * rank * core_flat,
         core_near,
         other,
-        factor_near,
-        *factors,
+        factors,
     )
     received = [lax.ppermute(send, "gx", route) for send, route in zip(sends, across)]
     pressure_later, _ = lax.optimization_barrier((pressure, mine))

time: 57.5 us -> 60.6 us (1.054)
  starting transfers between devices: 21.6 us -> 23 us
  waiting for transfers between devices: 18.5 us -> 19.4 us
  local copies, waits for them, and re-layouts: 1.99 us -> 2.62 us
    all_to_all x0 -> x1, starting transfers between devices: none -> 4.71 us  [body(): lax.all_to_all(jnp.broadcast_to(first_factor, (chips, *first_factor.shape...]
    ppermute x3 -> x0, starting transfers between devices: 4.11 us -> none  [body(): lax.ppermute(first_factor, 'gx', route)]
    all_to_all x0 -> x1, waiting for transfers between devices: none -> 3.54 us  [body(): lax.all_to_all(jnp.broadcast_to(first_factor, (chips, *first_factor.shape...]
    ppermute x3 -> x0, waiting for transfers between devices: 2.82 us -> none  [body(): lax.ppermute(first_factor, 'gx', route)]
    broadcast_in_dim x0 -> x1, local copies, waits for them, and re-layouts: none -> 1.33 us  [body(): jnp.broadcast_to(first_factor, (chips, *first_factor.shape))]
    ppermute x1, starting transfers between devices: 0.67 us -> 1.38 us  [body(): lax.ppermute(codes_later, 'gy', [(1, 2), (2, 1)])]
    unnamed x15 -> x13, local copies, waits for them, and re-layouts: 1.99 us -> 1.29 us
  transfers between devices with their start and end apart: 15 -> 13, of which waited for: 7 -> 7; matrix products, arithmetic and copies ran while one was open for 0% -> 2% of each run, Pallas kernels for 15% -> 14%
where the time goes in v4:
time: 60.6 us; the launch traced here: 60.2 us
  starting transfers between devices  23 us (38%)
  waiting for transfers between devices  19.4 us (32%)
  Pallas kernels  15.1 us (25%)
  local copies, waits for them, and re-layouts  2.62 us (4%)
    pallas_call x8, Pallas kernels, call(): pl.pallas_call(kernel, out_shape=outs, scratch_shapes=scratch, cost_estim...  15.1 us
    ppermute x2, waiting for transfers between devices, far(): lax.ppermute(codes, 'gy', [(i, i ^ distance) for i in range(count_y)])  8.59 us
    all_to_all x1, starting transfers between devices, body(): lax.all_to_all(jnp.broadcast_to(first_factor, (chips, *first_factor.shape...  4.71 us
    ppermute x1, waiting for transfers between devices, body(): high = lax.ppermute(down, 'gy', [(i + 1, i) for i in range(count_y - 1)])  4.3 us
    ppermute x2, starting transfers between devices, far(): lax.ppermute(codes, 'gy', [(i, i ^ distance) for i in range(count_y)])  4.25 us
    ppermute x3, starting transfers between devices, body(): lax.ppermute(send, 'gx', route)  3.55 us
    all_to_all x1, waiting for transfers between devices, body(): lax.all_to_all(jnp.broadcast_to(first_factor, (chips, *first_factor.shape...  3.54 us
    ppermute x1, starting transfers between devices, body(): low = lax.ppermute(up, 'gy', [(i, i + 1) for i in range(count_y - 1)])  3.48 us
  transfers between devices with their start and end apart: 13, of which 7 were waited for; matrix products, arithmetic and copies ran while one was open for 2% of the time, Pallas kernels for 14%

profile of v4, /device:TPU:0, one launch (start us, length us, event | category | flops | bytes accessed | tf_op | source)
XLA Modules:
  0.0 60.2 jit_solution(8449919079350936779)
XLA Ops:
  0.0 0.5 collective-permute-start
  0.5 1.3 %broadcast_in_dim.3 = bf16[4,16,384]{2,1,0:T(8,128)(2,1)} broadcast(bf16[16,384]{1,0:T(8,128)(2,1)} %param.11), dimensions={1,2} | broadcast | bytes 61440 | tf_op jit(solution)/shard_map/broadcast_in_dim | solution.py:416
  1.8 4.7 %all-to-all-start = ((bf16[4,16,384]{2,1,0:T(8,128)(2,1)}), bf16[4,16,384]{2,1,0:T(8,128)(2,1)S(1)}, u32[]{:S(2)}, u32[]{:S(2)}) async-start(bf16[4,16,384]{2,1,0:T(8,128)(2,1)} %broadcast_in_dim.3), calls=%async_computation | async-start | bytes 98304 | tf_op jit(solution)/shard_map/all_to_all | solution.py:415
  6.5 0.0 copy-start.2
  6.5 1.2 %copy-done.2 = bf16[3,48,3072]{2,1,0:T(8,128)(2,1)S(1)} copy-done((bf16[3,48,3072]{2,1,0:T(8,128)(2,1)S(1)}, bf16[3,48,3072]{2,1,0:T(8,128)(2,1)}, u32[]{:S(2)}) %copy-start.2) | copy-done | bytes 884760
  7.7 0.1 shard_map.73.core
  7.7 0.0 copy-start
  7.7 0.0 copy-start.1
  7.8 0.0 copy-start.3
  7.8 3.5 %all-to-all-done.factors = bf16[4,16,384]{2,1,0:T(8,128)(2,1)S(1)} async-done(((bf16[4,16,384]{2,1,0:T(8,128)(2,1)}), bf16[4,16,384]{2,1,0:T(8,128)(2,1)S(1)}, u32[]{:S(2)}, u32[]{:S(2)}) %all-to-all-start) | async-done | bytes 49184 | tf_op jit(solution)/shard_map/all_to_all | solution.py:415
  11.3 0.0 collective-permute-done.other
  11.3 1.4 %shard_map.74 = (f32[48,3072]{1,0:T(8,128)S(1)}, bf16[48,3200]{1,0:T(8,128)(2,1)S(1)}, bf16[48,3200]{1,0:T(8,128)(2,1)S(1)}, bf16[48,3200]{1,0:T(8,128)(2,1)S(1)}) custom-call(bf16[3,48,3072]{2,1,0:T(8,128)(2,1)S(1)} %shard_map.73.core, bf16[3,48,3072]{2,1,0:T(8,128)(2,1)S(1)} %collective-permute-done.other, bf16[4,16,384]{2,1,0:T(8,128)(2,1)S(1)} %all-to-all-done.factors), custom_call_target="tpu_custom_call" | custom-call | flops 113246208 | bytes 3330048 | tf_op jit(solution)/shard_map/pallas_call | solution.py:387
  12.8 0.8 %collective-permute-start.3 = (bf16[48,3200]{1,0:T(8,128)(2,1)S(1)}, bf16[48,3200]{1,0:T(8,128)(2,1)S(1)}, u32[]{:S(2)}, u32[]{:S(2)}) collective-permute-start(bf16[48,3200]{1,0:T(8,128)(2,1)S(1)} %get-tuple-element.33), channel_id=1, source_target_pairs={{0,8},{4,12},{8,0},{12,4},{16,24},{20,28},{24,16},{28,20},{1,9},{5... | collective-permute-start | bytes 921608 | tf_op jit(solution)/shard_map/ppermute | solution.py:432
  13.5 0.4 collective-permute-start.4
  13.9 2.4 %collective-permute-start.5 = (bf16[48,3200]{1,0:T(8,128)(2,1)S(1)}, bf16[48,3200]{1,0:T(8,128)(2,1)S(1)}, u32[]{:S(2)}, u32[]{:S(2)}) collective-permute-start(bf16[48,3200]{1,0:T(8,128)(2,1)S(1)} %get-tuple-element.35), channel_id=1, source_target_pairs={{0,24},{4,28},{8,16},{12,20},{16,8},{20,12},{24,0},{28,4},{1,25},{... | collective-permute-start | bytes 921608 | tf_op jit(solution)/shard_map/ppermute | solution.py:432
  16.3 0.0 copy-done
  16.3 0.0 copy-done.1
  16.3 0.0 copy-done.3
  16.3 0.5 shard_map.75
  16.8 3.5 %collective-permute-start.1 = (bf16[48,896]{1,0:T(8,128)(2,1)S(1)}, bf16[48,896]{1,0:T(8,128)(2,1)S(1)}, u32[]{:S(2)}, u32[]{:S(2)}) collective-permute-start(bf16[48,896]{1,0:T(8,128)(2,1)S(1)} %get-tuple-element.28), channel_id=1, source_target_pairs={{0,1},{1,2},{2,3},{4,5},{5,6},{6,7},{8,9},{9,10},{10,11},{12,13},{... | collective-permute-start | bytes 258056 | tf_op jit(solution)/shard_map/ppermute | solution.py:443
  20.3 1.3 %collective-permute-start.2 = (bf16[48,896]{1,0:T(8,128)(2,1)S(1)}, bf16[48,896]{1,0:T(8,128)(2,1)S(1)}, u32[]{:S(2)}, u32[]{:S(2)}) collective-permute-start(bf16[48,896]{1,0:T(8,128)(2,1)S(1)} %get-tuple-element.29), channel_id=1, source_target_pairs={{1,0},{2,1},{3,2},{5,4},{6,5},{7,6},{9,8},{10,9},{11,10},{13,12},{... | collective-permute-start | bytes 258056 | tf_op jit(solution)/shard_map/ppermute | solution.py:444
  21.6 0.8 %collective-permute-done.1.low = bf16[48,896]{1,0:T(8,128)(2,1)S(1)} collective-permute-done((bf16[48,896]{1,0:T(8,128)(2,1)S(1)}, bf16[48,896]{1,0:T(8,128)(2,1)S(1)}, u32[]{:S(2)}, u32[]{:S(2)}) %collective-permute-start.1) | collective-permute-done | bytes 86048 | tf_op jit(solution)/shard_map/ppermute | solution.py:443
  22.4 4.3 %collective-permute-done.2.high = bf16[48,896]{1,0:T(8,128)(2,1)S(1)} collective-permute-done((bf16[48,896]{1,0:T(8,128)(2,1)S(1)}, bf16[48,896]{1,0:T(8,128)(2,1)S(1)}, u32[]{:S(2)}, u32[]{:S(2)}) %collective-permute-start.2) | collective-permute-done | bytes 86048 | tf_op jit(solution)/shard_map/ppermute | solution.py:444
  26.7 0.0 copy-start.5
  26.7 0.0 copy-start.4
  26.7 1.0 %shard_map.76 = (bf16[32,7552]{1,0:T(8,128)(2,1)}, bf16[32,7552]{1,0:T(8,128)(2,1)}) custom-call(bf16[48,6272]{1,0:T(8,128)(2,1)S(1)} %get-tuple-element.27.own, bf16[48,896]{1,0:T(8,128)(2,1)S(1)} %collective-permute-done.1.low, bf16[48,896]{1,0:T(8,128)(2,1)S(1)} %collective-permute-done.2.high), custom_call_target="tpu_custom_call" | custom-call | flops 1000 | bytes 1740800 | tf_op jit(solution)/shard_map/pallas_call | solution.py:387
  27.7 0.0 collective-permute-done.3.rest_0_
  27.7 0.4 collective-permute-done.4.rest_1_
  28.1 0.0 collective-permute-done.5.rest_2_
  28.1 1.9 %shard_map.77.rest_0_ = bf16[96,1664]{1,0:T(8,128)(2,1)S(1)} custom-call(f32[48,3072]{1,0:T(8,128)S(1)} %get-tuple-element.32.mine, bf16[48,3200]{1,0:T(8,128)(2,1)S(1)} %collective-permute-done.3.rest_0_, bf16[48,3200]{1,0:T(8,128)(2,1)S(1)} %collective-permute-done.4.rest_1_, bf16[48,3200]{1,0:T(8,128)(2,1)S(1)} %collective-permute-done.5.rest_2_), custom_call_target="tpu_custom_call" | custom-call | flops 17694720 | bytes 1830912 | tf_op jit(solution)/shard_map/pallas_call | solution.py:387
  30.0 2.7 %collective-permute-start.8 = (bf16[96,1664]{1,0:T(8,128)(2,1)S(1)}, bf16[96,1664]{1,0:T(8,128)(2,1)S(1)}, u32[]{:S(2)}, u32[]{:S(2)}) collective-permute-start(bf16[96,1664]{1,0:T(8,128)(2,1)S(1)} %shard_map.77.rest_0_), channel_id=1, source_target_pairs={{0,2},{1,3},{2,0},{3,1},{4,6},{5,7},{6,4},{7,5},{8,10},{9,11},{10,... | collective-permute-start | bytes 958472 | tf_op jit(solution)/shard_map/ppermute | solution.py:468
  32.7 1.6 %collective-permute-start.9 = (bf16[96,1664]{1,0:T(8,128)(2,1)S(1)}, bf16[96,1664]{1,0:T(8,128)(2,1)S(1)}, u32[]{:S(2)}, u32[]{:S(2)}) collective-permute-start(bf16[96,1664]{1,0:T(8,128)(2,1)S(1)} %shard_map.77.rest_0_), channel_id=1, source_target_pairs={{0,1},{1,0},{2,3},{3,2},{4,5},{5,4},{6,7},{7,6},{8,9},{9,8},{10,11... | collective-permute-start | bytes 958472 | tf_op jit(solution)/shard_map/ppermute | solution.py:468
  34.2 1.3 %collective-permute-start.6 = (bf16[32,7552]{1,0:T(8,128)(2,1)}, bf16[32,7552]{1,0:T(8,128)(2,1)S(1)}, u32[]{:S(2)}, u32[]{:S(2)}) collective-permute-start(bf16[32,7552]{1,0:T(8,128)(2,1)} %get-tuple-element.38), channel_id=1, source_target_pairs={{0,4},{4,8},{8,12},{12,16},{16,20},{20,24},{24,28},{1,5},{5,9},{9,... | collective-permute-start | bytes 1449992 | tf_op jit(solution)/shard_map/ppermute | solution.py:483
  35.6 1.3 %collective-permute-start.7 = (bf16[32,7552]{1,0:T(8,128)(2,1)}, bf16[32,7552]{1,0:T(8,128)(2,1)S(1)}, u32[]{:S(2)}, u32[]{:S(2)}) collective-permute-start(bf16[32,7552]{1,0:T(8,128)(2,1)} %get-tuple-element.39), channel_id=1, source_target_pairs={{4,0},{8,4},{12,8},{16,12},{20,16},{24,20},{28,24},{5,1},{9,5},{13... | collective-permute-start | bytes 1449992 | tf_op jit(solution)/shard_map/ppermute | solution.py:484
  36.9 8.4 %collective-permute-done.8.rest_1_ = bf16[96,1664]{1,0:T(8,128)(2,1)S(1)} collective-permute-done((bf16[96,1664]{1,0:T(8,128)(2,1)S(1)}, bf16[96,1664]{1,0:T(8,128)(2,1)S(1)}, u32[]{:S(2)}, u32[]{:S(2)}) %collective-permute-start.8) | collective-permute-done | bytes 319520 | tf_op jit(solution)/shard_map/ppermute | solution.py:468
  45.3 0.2 collective-permute-done.9.rest_2_
  45.5 1.4 %collective-permute-start.10 = (bf16[96,1664]{1,0:T(8,128)(2,1)S(1)}, bf16[96,1664]{1,0:T(8,128)(2,1)}, u32[]{:S(2)}, u32[]{:S(2)}) collective-permute-start(bf16[96,1664]{1,0:T(8,128)(2,1)S(1)} %shard_map.77.rest_0_), channel_id=1, source_target_pairs={{1,2},{2,1},{5,6},{6,5},{9,10},{10,9},{13,14},{14,13},{17,18},{18,... | collective-permute-start | bytes 958472 | tf_op jit(solution)/shard_map/ppermute | solution.py:475
  46.8 1.3 %collective-permute-start.11 = (bf16[96,1664]{1,0:T(8,128)(2,1)S(1)}, bf16[96,1664]{1,0:T(8,128)(2,1)}, u32[]{:S(2)}, u32[]{:S(2)}) collective-permute-start(bf16[96,1664]{1,0:T(8,128)(2,1)S(1)} %collective-permute-done.8.rest_1_), channel_id=1, source_target_pairs={{1,0},{2,3},{5,4},{6,7},{9,8},{10,11},{13,12},{14,15},{17,16},{18,... | collective-permute-start | bytes 958472 | tf_op jit(solution)/shard_map/ppermute | solution.py:476
  48.1 0.0 copy-done.5
  48.1 0.1 copy.8.depth_factor
  48.2 0.0 copy-done.4
  48.2 1.6 %shard_map.79.earlier = f32[96,1536]{1,0:T(8,128)S(1)} custom-call(bf16[96,384]{1,0:T(8,128)(2,1)S(1)} %copy-done.4, bf16[96,1664]{1,0:T(8,128)(2,1)S(1)} %shard_map.77.rest_0_, bf16[96,1664]{1,0:T(8,128)(2,1)S(1)} %collective-permute-done.8.rest_1_, bf16[96,1664]{1,0:T(8,128)(2,1)S(1)} %collective-permute-done.9.rest_2_), custom_call_target="tpu_custom_call" | custom-call | flops 226492416 | bytes 1622016 | tf_op jit(solution)/shard_map/pallas_call | solution.py:387
  49.9 0.0 collective-permute-done.6.left
  49.9 0.0 collective-permute-done.7.right
  49.9 5.3 %shard_map.78.waves = f32[48,48,128]{2,1,0:T(8,128)S(1)} custom-call(f32[16,6144]{1,0:T(8,128)S(1)} %copy-done, f32[16,6144]{1,0:T(8,128)S(1)} %copy-done.1, bf16[16,6144]{1,0:T(8,128)(2,1)S(1)} %copy-done.3, bf16[32,7552]{1,0:T(8,128)(2,1)S(1)} %collective-permute-done.6.left, bf16[32,7552]{1,0:T(8,128)(2,1)S(1)} %collective-permute-done.7.right, ...), custom_call_target="tpu_custom_call" | custom-call | flops 44236800 | bytes 3301376 | tf_op jit(solution)/shard_map/pallas_call | solution.py:387
  55.2 0.0 collective-permute-done.10.rest_0_
  55.2 1.8 %collective-permute-done.11.rest_1_ = bf16[96,1664]{1,0:T(8,128)(2,1)} collective-permute-done((bf16[96,1664]{1,0:T(8,128)(2,1)S(1)}, bf16[96,1664]{1,0:T(8,128)(2,1)}, u32[]{:S(2)}, u32[]{:S(2)}) %collective-permute-start.11) | collective-permute-done | bytes 319520 | tf_op jit(solution)/shard_map/ppermute | solution.py:476
  57.0 3.3 %shard_map.80 = f32[16,6144]{1,0:T(8,128)} custom-call(bf16[96,384]{1,0:T(8,128)(2,1)S(1)} %copy-done.4, bf16[64,32]{1,0:T(8,128)(2,1)S(1)} %copy.8.depth_factor, f32[48,48,128]{2,1,0:T(8,128)S(1)} %shard_map.78.waves, f32[96,1536]{1,0:T(8,128)S(1)} %shard_map.79.earlier, bf16[96,1664]{1,0:T(8,128)(2,1)} %collective-permute-done.10.rest_0_, ...), custom_call_target="tpu_custom_call" | custom-call | flops 56623104 | bytes 2879488 | tf_op jit(solution)/shard_map/pallas_call | solution.py:387
Async XLA Ops:
  0.0 11.3 %collective-permute-start = (bf16[3,48,3072]{2,1,0:T(8,128)(2,1)}, bf16[3,48,3072]{2,1,0:T(8,128)(2,1)S(1)}, u32[]{:S(2)}, u32[]{:S(2)}) collective-permute-start(bf16[3,48,3072]{2,1,0:T(8,128)(2,1)} %core.1), channel_id=1, source_target_pairs={{0,4},{4,0},{8,12},{12,8},{16,20},{20,16},{24,28},{28,24},{1,5},{5... | collective-permute-start | bytes 2654216 | tf_op jit(solution)/shard_map/ppermute | solution.py:414
  1.8 9.5 %all-to-all-start = ((bf16[4,16,384]{2,1,0:T(8,128)(2,1)}), bf16[4,16,384]{2,1,0:T(8,128)(2,1)S(1)}, u32[]{:S(2)}, u32[]{:S(2)}) async-start(bf16[4,16,384]{2,1,0:T(8,128)(2,1)} %broadcast_in_dim.3), calls=%async_computation | async-start | bytes 98304 | tf_op jit(solution)/shard_map/all_to_all | solution.py:415
  6.5 1.2 %copy-start.2 = (bf16[3,48,3072]{2,1,0:T(8,128)(2,1)S(1)}, bf16[3,48,3072]{2,1,0:T(8,128)(2,1)}, u32[]{:S(2)}) copy-start(bf16[3,48,3072]{2,1,0:T(8,128)(2,1)} %core.1) | copy-start | bytes 2654212
  7.7 8.6 %copy-start = (f32[16,6144]{1,0:T(8,128)S(1)}, f32[16,6144]{1,0:T(8,128)}, u32[]{:S(2)}) copy-start(f32[16,6144]{1,0:T(8,128)} %pressure.2) | copy-start | bytes 1179652
  7.7 8.6 %copy-start.1 = (f32[16,6144]{1,0:T(8,128)S(1)}, f32[16,6144]{1,0:T(8,128)}, u32[]{:S(2)}) copy-start(f32[16,6144]{1,0:T(8,128)} %previous.3) | copy-start | bytes 1179652
  7.8 8.6 %copy-start.3 = (bf16[16,6144]{1,0:T(8,128)(2,1)S(1)}, bf16[16,6144]{1,0:T(8,128)(2,1)}, u32[]{:S(2)}) copy-start(bf16[16,6144]{1,0:T(8,128)(2,1)} %velocity.3) | copy-start | bytes 589828
  12.8 14.9 %collective-permute-start.3 = (bf16[48,3200]{1,0:T(8,128)(2,1)S(1)}, bf16[48,3200]{1,0:T(8,128)(2,1)S(1)}, u32[]{:S(2)}, u32[]{:S(2)}) collective-permute-start(bf16[48,3200]{1,0:T(8,128)(2,1)S(1)} %get-tuple-element.33), channel_id=1, source_target_pairs={{0,8},{4,12},{8,0},{12,4},{16,24},{20,28},{24,16},{28,20},{1,9},{5... | collective-permute-start | bytes 921608 | tf_op jit(solution)/shard_map/ppermute | solution.py:432
  13.5 14.6 %collective-permute-start.4 = (bf16[48,3200]{1,0:T(8,128)(2,1)S(1)}, bf16[48,3200]{1,0:T(8,128)(2,1)S(1)}, u32[]{:S(2)}, u32[]{:S(2)}) collective-permute-start(bf16[48,3200]{1,0:T(8,128)(2,1)S(1)} %get-tuple-element.34), channel_id=1, source_target_pairs={{0,16},{4,20},{8,24},{12,28},{16,0},{20,4},{24,8},{28,12},{1,17},{... | collective-permute-start | bytes 921608 | tf_op jit(solution)/shard_map/ppermute | solution.py:432
  13.9 14.1 %collective-permute-start.5 = (bf16[48,3200]{1,0:T(8,128)(2,1)S(1)}, bf16[48,3200]{1,0:T(8,128)(2,1)S(1)}, u32[]{:S(2)}, u32[]{:S(2)}) collective-permute-start(bf16[48,3200]{1,0:T(8,128)(2,1)S(1)} %get-tuple-element.35), channel_id=1, source_target_pairs={{0,24},{4,28},{8,16},{12,20},{16,8},{20,12},{24,0},{28,4},{1,25},{... | collective-permute-start | bytes 921608 | tf_op jit(solution)/shard_map/ppermute | solution.py:432
  16.8 5.6 %collective-permute-start.1 = (bf16[48,896]{1,0:T(8,128)(2,1)S(1)}, bf16[48,896]{1,0:T(8,128)(2,1)S(1)}, u32[]{:S(2)}, u32[]{:S(2)}) collective-permute-start(bf16[48,896]{1,0:T(8,128)(2,1)S(1)} %get-tuple-element.28), channel_id=1, source_target_pairs={{0,1},{1,2},{2,3},{4,5},{5,6},{6,7},{8,9},{9,10},{10,11},{12,13},{... | collective-permute-start | bytes 258056 | tf_op jit(solution)/shard_map/ppermute | solution.py:443
  20.3 6.4 %collective-permute-start.2 = (bf16[48,896]{1,0:T(8,128)(2,1)S(1)}, bf16[48,896]{1,0:T(8,128)(2,1)S(1)}, u32[]{:S(2)}, u32[]{:S(2)}) collective-permute-start(bf16[48,896]{1,0:T(8,128)(2,1)S(1)} %get-tuple-element.29), channel_id=1, source_target_pairs={{1,0},{2,1},{3,2},{5,4},{6,5},{7,6},{9,8},{10,9},{11,10},{13,12},{... | collective-permute-start | bytes 258056 | tf_op jit(solution)/shard_map/ppermute | solution.py:444
  26.7 21.5 %copy-start.5 = (bf16[64,32]{0,1:T(8,128)(2,1)S(1)}, bf16[64,32]{0,1:T(8,128)(2,1)}, u32[]{:S(2)}) copy-start(bf16[64,32]{0,1:T(8,128)(2,1)} %param.13) | copy-start | bytes 12292
  26.7 21.6 %copy-start.4 = (bf16[96,384]{1,0:T(8,128)(2,1)S(1)}, bf16[96,384]{1,0:T(8,128)(2,1)}, u32[]{:S(2)}) copy-start(bf16[96,384]{1,0:T(8,128)(2,1)} %second.3) | copy-start | bytes 221188
  30.0 15.3 %collective-permute-start.8 = (bf16[96,1664]{1,0:T(8,128)(2,1)S(1)}, bf16[96,1664]{1,0:T(8,128)(2,1)S(1)}, u32[]{:S(2)}, u32[]{:S(2)}) collective-permute-start(bf16[96,1664]{1,0:T(8,128)(2,1)S(1)} %shard_map.77.rest_0_), channel_id=1, source_target_pairs={{0,2},{1,3},{2,0},{3,1},{4,6},{5,7},{6,4},{7,5},{8,10},{9,11},{10,... | collective-permute-start | bytes 958472 | tf_op jit(solution)/shard_map/ppermute | solution.py:468
  32.7 12.8 %collective-permute-start.9 = (bf16[96,1664]{1,0:T(8,128)(2,1)S(1)}, bf16[96,1664]{1,0:T(8,128)(2,1)S(1)}, u32[]{:S(2)}, u32[]{:S(2)}) collective-permute-start(bf16[96,1664]{1,0:T(8,128)(2,1)S(1)} %shard_map.77.rest_0_), channel_id=1, source_target_pairs={{0,1},{1,0},{2,3},{3,2},{4,5},{5,4},{6,7},{7,6},{8,9},{9,8},{10,11... | collective-permute-start | bytes 958472 | tf_op jit(solution)/shard_map/ppermute | solution.py:468
  34.2 15.6 %collective-permute-start.6 = (bf16[32,7552]{1,0:T(8,128)(2,1)}, bf16[32,7552]{1,0:T(8,128)(2,1)S(1)}, u32[]{:S(2)}, u32[]{:S(2)}) collective-permute-start(bf16[32,7552]{1,0:T(8,128)(2,1)} %get-tuple-element.38), channel_id=1, source_target_pairs={{0,4},{4,8},{8,12},{12,16},{16,20},{20,24},{24,28},{1,5},{5,9},{9,... | collective-permute-start | bytes 1449992 | tf_op jit(solution)/shard_map/ppermute | solution.py:483
  35.6 14.3 %collective-permute-start.7 = (bf16[32,7552]{1,0:T(8,128)(2,1)}, bf16[32,7552]{1,0:T(8,128)(2,1)S(1)}, u32[]{:S(2)}, u32[]{:S(2)}) collective-permute-start(bf16[32,7552]{1,0:T(8,128)(2,1)} %get-tuple-element.39), channel_id=1, source_target_pairs={{4,0},{8,4},{12,8},{16,12},{20,16},{24,20},{28,24},{5,1},{9,5},{13... | collective-permute-start | bytes 1449992 | tf_op jit(solution)/shard_map/ppermute | solution.py:484
  45.5 9.7 %collective-permute-start.10 = (bf16[96,1664]{1,0:T(8,128)(2,1)S(1)}, bf16[96,1664]{1,0:T(8,128)(2,1)}, u32[]{:S(2)}, u32[]{:S(2)}) collective-permute-start(bf16[96,1664]{1,0:T(8,128)(2,1)S(1)} %shard_map.77.rest_0_), channel_id=1, source_target_pairs={{1,2},{2,1},{5,6},{6,5},{9,10},{10,9},{13,14},{14,13},{17,18},{18,... | collective-permute-start | bytes 958472 | tf_op jit(solution)/shard_map/ppermute | solution.py:475
  46.8 10.1 %collective-permute-start.11 = (bf16[96,1664]{1,0:T(8,128)(2,1)S(1)}, bf16[96,1664]{1,0:T(8,128)(2,1)}, u32[]{:S(2)}, u32[]{:S(2)}) collective-permute-start(bf16[96,1664]{1,0:T(8,128)(2,1)S(1)} %collective-permute-done.8.rest_1_), channel_id=1, source_target_pairs={{1,0},{2,3},{5,4},{6,7},{9,8},{10,11},{13,12},{14,15},{17,16},{18,... | collective-permute-start | bytes 958472 | tf_op jit(solution)/shard_map/ppermute | solution.py:476

commit v5 on v3

--- a/solution.py
+++ b/solution.py
@@ -15,8 +15,8 @@
 VMEM_BYTES = 48 * 1024 * 1024
 
 
-def encode(values):
-    peak = jnp.max(jnp.abs(values), axis=1, keepdims=True)
+def encode(values, axis=1):
+    peak = jnp.max(jnp.abs(values), axis=axis, keepdims=True)
     scale = (jnp.maximum(peak, 1e-30) * (1.0 + 2.0**-7)).astype(BF16).astype(F32)
     ratio = values * (TOP / scale)
     power = ratio * ratio
@@ -82,7 +82,7 @@
     lines = mine.shape[0]
     cells = lines // steps
     place = lax.axis_index("gx")
-    factor = jnp.concatenate([ref[...] for ref in factors], axis=0)
+    factor = jnp.concatenate([ref[...] for ref in factors[::-1]], axis=0)
     offset = lax.broadcasted_iota(jnp.int32, (factor.shape[1], rank), 0) - lax.broadcasted_iota(
         jnp.int32, (factor.shape[1], rank), 1
     )
@@ -253,8 +253,10 @@
 def pack_kernel(pressure, previous, velocity, own, up, down):
     cells, flat = pressure.shape
     span = up.shape[1] - LANES
-    put_codes(own, 0, pressure[...], flat)
-    put_codes(own, cells, previous[...], flat)
+    for row, part in ((0, pressure), (cells, previous)):
+        codes, scale = encode(part[...], (0, 1))
+        own[row : row + cells, :flat] = codes
+        own[row : row + cells, flat:] = jnp.broadcast_to(scale, (cells, LANES)).astype(BF16)
     own[2 * cells :, :flat] = velocity[...]
     own[2 * cells :, flat:] = jnp.zeros((cells, LANES), BF16)
     up[:, :span] = own[:, flat - span : flat]
@@ -263,27 +265,47 @@
     down[:, span:] = own[:, flat:]
 
 
+def layout(cells, flat, near):
+    widths = (flat, flat // 2, flat // 4, near, near // 2, LANES)
+    starts = [sum(widths[:k]) for k in range(len(widths))]
+    return [slice(start, start + width) for start, width in zip(starts, widths)]
+
+
 def edge_kernel(own, low, high, ahead, behind):
     flat = own.shape[1] - LANES
     span = low.shape[1] - LANES
     near = span * 2 // 3
     cells = own.shape[0] // 3
-    half = cells // 2
-    scales = 2 * near + flat
-    spans = [
-        (low, slice(span - near, span), slice(0, near)),
-        (own, slice(0, flat), slice(near, near + flat)),
-        (high, slice(0, near), slice(near + flat, scales)),
-        (low, slice(span, span + LANES), slice(scales, scales + LANES)),
-        (own, slice(flat, flat + LANES), slice(scales + LANES, scales + 2 * LANES)),
-        (high, slice(span, span + LANES), slice(scales + 2 * LANES, scales + 3 * LANES)),
-    ]
-    for ref, rows in ((ahead, slice(half, cells)), (behind, slice(0, half))):
-        for part, lanes, into in spans:
-            ref[:cells, into] = part[:cells, lanes]
-            prior = part[cells : 2 * cells, lanes].astype(F32)[rows]
-            speed = part[2 * cells :, lanes].astype(F32)[rows]
-            ref[cells:, into] = jnp.concatenate([prior, speed], axis=0).astype(BF16)
+    half, quarter = cells // 2, cells // 4
+    places = layout(cells, flat, near)
+    lane = lax.broadcasted_iota(jnp.int32, (cells, LANES), 1) // 16
+    scales = jnp.zeros((cells, LANES), F32)
+    for k, (part, row) in enumerate(((own, 0), (own, cells), (low, 0), (high, 0), (low, cells), (high, cells))):
+        width = part.shape[1]
+        scales = jnp.where(lane == k, part[row : row + cells, width - LANES :].astype(F32), scales)
+    pressure = own[:cells, :flat].astype(F32)
+    previous = own[cells : 2 * cells, :flat].astype(F32)
+    speed = own[2 * cells :, :flat].astype(F32)
+    below, above = low[:, span - near : span].astype(F32), high[:, :near].astype(F32)
+    for ref, first, next_first in ((ahead, half, half - quarter), (behind, 0, half)):
+        rows = slice(first, first + half)
+        close = half if first > 0 else 0
+        tight = slice(cells - quarter, cells) if first > 0 else slice(0, quarter)
+        blocks = [
+            [previous[rows], speed[rows]],
+            [pressure[rows, : flat // 2], pressure[rows, flat // 2 :]],
+            [pressure[next_first : next_first + quarter, k * (flat // 4) : (k + 1) * (flat // 4)] for k in range(4)],
+            [below[close : close + half], above[close : close + half]],
+            [
+                below[cells + tight.start : cells + tight.stop, near // 2 :],
+                above[cells + tight.start : cells + tight.stop, : near // 2],
+                below[2 * cells + tight.start : 2 * cells + tight.stop, near // 2 :],
+                above[2 * cells + tight.start : 2 * cells + tight.stop, : near // 2],
+            ],
+            [scales],
+        ]
+        for place, block in zip(places, blocks):
+            ref[:, place] = jnp.concatenate(block, axis=0).astype(BF16)
 
 
 def wave_kernel(levels, pressure, previous, velocity, left, right, low, high, waves, first, second, third, prior, speed):
@@ -299,18 +321,53 @@
         first[edge + tile, cells : 2 * cells, :] = pressure[:, lane : lane + LANES]
         prior[inner + tile, half : half + cells, :] = previous[:, lane : lane + LANES]
         speed[inner + tile, half : half + cells, :] = velocity[:, lane : lane + LANES].astype(F32)
-    wide = own_tiles + 2 * inner
-    for part, top, side in ((left, 0, 0), (right, 2 * cells, half + cells)):
-        scales = [units(part, 0, 2 * cells, (wide + k) * LANES) for k in range(3)]
-        for tile in range(wide):
-            lanes = slice(tile * LANES, (tile + 1) * LANES)
-            unit = scales[0 if tile < inner else 1 if tile < inner + own_tiles else 2]
-            first[edge - inner + tile, top : top + cells, :] = decode(part[:cells, lanes], unit[:cells])
-            both = part[cells:, lanes].astype(F32)
-            prior[tile, side : side + half, :] = decode(both[:half], unit[cells : cells + half])
-            speed[tile, side : side + half, :] = both[half:]
-        for tile in list(range(edge - inner)) + list(range(edge + own_tiles + inner, 2 * edge + own_tiles)):
-            first[tile, top : top + cells, :] = jnp.zeros((cells, LANES), F32)
+    for tile in range(2 * edge + own_tiles):
+        if tile < edge or tile >= edge + own_tiles:
+            first[tile, :cells, :] = jnp.zeros((cells, LANES), F32)
+            first[tile, 2 * cells :, :] = jnp.zeros((cells, LANES), F32)
+    for tile in range(2 * inner + own_tiles):
+        if tile < inner or tile >= inner + own_tiles:
+            for ref in (prior, speed):
+                ref[tile, :half, :] = jnp.zeros((half, LANES), F32)
+                ref[tile, half + cells :, :] = jnp.zeros((half, LANES), F32)
+    quarter = cells // 4
+    places = layout(cells, flat, near)
+    for part, top, far, side, tight in (
+        (left, cells - half, half - quarter, 0, half - quarter),
+        (right, 2 * cells, 2 * cells + half, half + cells, half + cells),
+    ):
+        scales = part[:half, places[5]].astype(F32) * (1.0 / TOP)
+        unit = [jnp.broadcast_to(scales[:, 16 * k : 16 * k + 1], (half, LANES)) for k in range(6)]
+
+        def tile_of(place, tile):
+            start = places[place].start + tile * LANES
+            return part[:, start : start + LANES].astype(F32)
+
+        for tile in range(own_tiles):
+            both = tile_of(0, tile)
+            prior[inner + tile, side : side + half, :] = decode(both[:half], unit[1])
+            speed[inner + tile, side : side + half, :] = both[half:]
+        for tile in range(own_tiles // 2):
+            both = tile_of(1, tile)
+            first[edge + tile, top : top + half, :] = decode(both[:half], unit[0])
+            first[edge + own_tiles // 2 + tile, top : top + half, :] = decode(both[half:], unit[0])
+        for tile in range(own_tiles // 4):
+            both = decode(tile_of(2, tile), jnp.concatenate([unit[0]] * 2, axis=0))
+            for k in range(4):
+                into = edge + k * (own_tiles // 4) + tile
+                first[into, far : far + quarter, :] = both[k * quarter : (k + 1) * quarter]
+        for tile in range(inner):
+            both = tile_of(3, tile)
+            first[edge - inner + tile, top : top + half, :] = decode(both[:half], unit[2])
+            first[edge + own_tiles + tile, top : top + half, :] = decode(both[half:], unit[3])
+        for tile in range(inner // 2):
+            both = tile_of(4, tile)
+            ends = (inner // 2 + tile, inner + own_tiles + tile)
+            values = decode(both[:half], jnp.concatenate([unit[4][:quarter], unit[5][:quarter]], axis=0))
+            for k, end in enumerate(ends):
+                rows = slice(k * quarter, (k + 1) * quarter)
+                prior[end, tight : tight + quarter, :] = values[rows]
+                speed[end, tight : tight + quarter, :] = both[half:][rows]
     for part, start, cut, begin in ((low, 0, edge - inner, 0), (high, edge + own_tiles, 0, inner + own_tiles)):
         unit = units(part, 0, 3 * cells, span)
         for tile in range(edge):
@@ -411,7 +468,7 @@
     lines_pad = (lines * depth // LANES + 7) // 8 * 8
 
     across = [[(i, 2 * ((i // 2) ^ distance) + i % 2) for i in range(count_x)] for distance in range(1, chips)]
-    factors = [lax.ppermute(first_factor, "gx", route) for route in across[::-1]][::-1]
+    factors = [lax.ppermute(first_factor, "gx", route) for route in across[::-1]]
     other = lax.ppermute(tucker_core, "gx", [(i, i + 1 - 2 * (i % 2)) for i in range(count_x)])
     core_near, factor_near = call(
         lift_kernel,
@@ -428,8 +485,8 @@
         4 * lines * chips * rank * core_flat,
         core_near,
         other,
+        *factors,
         factor_near,
-        *factors,
     )
     received = [lax.ppermute(send, "gx", route) for send, route in zip(sends, across)]
     pressure_later, _ = lax.optimization_barrier((pressure, mine))
@@ -447,7 +504,7 @@
 
     ahead, behind = call(
         edge_kernel,
-        [shape_of(2 * cells, flat + 2 * near + 3 * LANES, dtype=BF16)] * 2,
+        [shape_of(cells, layout(cells, flat, near)[-1].stop, dtype=BF16)] * 2,
         [],
         1000,
         own,

time: 57.5 us -> 56.5 us (0.983)
  waiting for transfers between devices: 18.5 us -> 15.9 us
  starting transfers between devices: 21.6 us -> 23.5 us
  Pallas kernels: 15 us -> 13.8 us
  local copies, waits for them, and re-layouts: 1.99 us -> 2.87 us
    ppermute x1, starting transfers between devices: 1.31 us -> 3.05 us  [body(): left = lax.ppermute(ahead, 'gx', [(i, i + 1) for i in range(count_x - 1)])]
    ppermute x2, waiting for transfers between devices: 8.22 us -> 6.8 us  [far(): lax.ppermute(codes, 'gy', [(i, i ^ distance) for i in range(count_y)])]
    pallas_call x8, Pallas kernels: 15 us -> 13.8 us  [call(): pl.pallas_call(kernel, out_shape=outs, scratch_shapes=scratch, cost_estim...]
    ppermute x3, waiting for transfers between devices: 2.82 us -> 1.81 us  [body(): lax.ppermute(first_factor, 'gx', route)]
    unnamed x15, local copies, waits for them, and re-layouts: 1.99 us -> 2.87 us
    ppermute x1, waiting for transfers between devices: 2.33 us -> 1.54 us  [body(): lax.ppermute(blocks[1], 'gy', [(1, 0), (2, 3)])]
    ppermute x3, waiting for transfers between devices: 0.01 us -> 0.65 us  [body(): lax.ppermute(send, 'gx', route)]
  transfers between devices with their start and end apart: 15 -> 15, of which waited for: 7 -> 8; matrix products, arithmetic and copies ran while one was open for 0% -> 0% of each run, Pallas kernels for 15% -> 15%
where the time goes in v5:
time: 56.5 us; the launch traced here: 56.1 us
  starting transfers between devices  23.5 us (42%)
  waiting for transfers between devices  15.9 us (28%)
  Pallas kernels  13.8 us (24%)
  local copies, waits for them, and re-layouts  2.87 us (5%)
    pallas_call x8, Pallas kernels, call(): pl.pallas_call(kernel, out_shape=outs, scratch_shapes=scratch, cost_estim...  13.8 us
    ppermute x2, waiting for transfers between devices, far(): lax.ppermute(codes, 'gy', [(i, i ^ distance) for i in range(count_y)])  6.8 us
    ppermute x1, waiting for transfers between devices, body(): high = lax.ppermute(down, 'gy', [(i + 1, i) for i in range(count_y - 1)])  4.3 us
    ppermute x2, starting transfers between devices, far(): lax.ppermute(codes, 'gy', [(i, i ^ distance) for i in range(count_y)])  4.22 us
    ppermute x3, starting transfers between devices, body(): lax.ppermute(first_factor, 'gx', route)  4.17 us
    ppermute x3, starting transfers between devices, body(): lax.ppermute(send, 'gx', route)  3.55 us
    ppermute x1, starting transfers between devices, body(): low = lax.ppermute(up, 'gy', [(i, i + 1) for i in range(count_y - 1)])  3.48 us
    ppermute x1, starting transfers between devices, body(): left = lax.ppermute(ahead, 'gx', [(i, i + 1) for i in range(count_x - 1)])  3.05 us
  transfers between devices with their start and end apart: 15, of which 8 were waited for; matrix products, arithmetic and copies ran while one was open for 0% of the time, Pallas kernels for 15%

profile of v5, /device:TPU:0, one launch (start us, length us, event | category | flops | bytes accessed | tf_op | source)
XLA Modules:
  0.0 56.1 jit_solution(3783161592614220609)
XLA Ops:
  0.0 0.0 copy-start
  0.0 0.0 copy-start.1
  0.0 0.5 collective-permute-start
  0.5 3.5 %collective-permute-start.1 = (bf16[16,384]{1,0:T(8,128)(2,1)}, bf16[16,384]{1,0:T(8,128)(2,1)S(1)}, u32[]{:S(2)}, u32[]{:S(2)}) collective-permute-start(bf16[16,384]{1,0:T(8,128)(2,1)} %factor.1), channel_id=1, source_target_pairs={{0,24},{4,28},{8,16},{12,20},{16,8},{20,12},{24,0},{28,4},{1,25},{... | collective-permute-start | bytes 36872 | tf_op jit(solution)/shard_map/ppermute | solution.py:471
  4.0 0.5 collective-permute-start.2
  4.5 0.1 collective-permute-start.3
  4.6 1.2 %copy-done.2 = bf16[3,48,3072]{2,1,0:T(8,128)(2,1)S(1)} copy-done((bf16[3,48,3072]{2,1,0:T(8,128)(2,1)S(1)}, bf16[3,48,3072]{2,1,0:T(8,128)(2,1)}, u32[]{:S(2)}) %copy-start.2) | copy-done | bytes 884760
  5.8 0.7 %copy-done.5 = bf16[16,384]{1,0:T(8,128)(2,1)S(1)} copy-done((bf16[16,384]{1,0:T(8,128)(2,1)S(1)}, bf16[16,384]{1,0:T(8,128)(2,1)}, u32[]{:S(2)}) %copy-start.5) | copy-done | bytes 12312
  6.5 0.1 shard_map.73
  6.6 0.0 collective-permute-done.1.rest_0_
  6.6 1.3 %collective-permute-done.2.rest_1_ = bf16[16,384]{1,0:T(8,128)(2,1)S(1)} collective-permute-done((bf16[16,384]{1,0:T(8,128)(2,1)}, bf16[16,384]{1,0:T(8,128)(2,1)S(1)}, u32[]{:S(2)}, u32[]{:S(2)}) %collective-permute-start.2) | collective-permute-done | bytes 12320 | tf_op jit(solution)/shard_map/ppermute | solution.py:471
  7.9 0.5 collective-permute-done.3.rest_2_
  8.4 0.0 collective-permute-done.other
  8.4 1.4 %shard_map.74 = (f32[48,3072]{1,0:T(8,128)S(1)}, bf16[48,3200]{1,0:T(8,128)(2,1)S(1)}, bf16[48,3200]{1,0:T(8,128)(2,1)S(1)}, bf16[48,3200]{1,0:T(8,128)(2,1)S(1)}) custom-call(bf16[3,48,3072]{2,1,0:T(8,128)(2,1)S(1)} %get-tuple-element.27.core, bf16[3,48,3072]{2,1,0:T(8,128)(2,1)S(1)} %collective-permute-done.other, ...), custom_call_target="tpu_custom_call" | custom-call | flops 113246208 | bytes 3330048 | tf_op jit(solution)/shard_map/pallas_call | solution.py:444
  9.8 0.2 collective-permute-start.6
  10.1 1.9 %collective-permute-start.7 = (bf16[48,3200]{1,0:T(8,128)(2,1)S(1)}, bf16[48,3200]{1,0:T(8,128)(2,1)S(1)}, u32[]{:S(2)}, u32[]{:S(2)}) collective-permute-start(bf16[48,3200]{1,0:T(8,128)(2,1)S(1)} %get-tuple-element.38), channel_id=1, source_target_pairs={{0,16},{4,20},{8,24},{12,28},{16,0},{20,4},{24,8},{28,12},{1,17},{... | collective-permute-start | bytes 921608 | tf_op jit(solution)/shard_map/ppermute | solution.py:491
  12.0 1.4 %collective-permute-start.8 = (bf16[48,3200]{1,0:T(8,128)(2,1)S(1)}, bf16[48,3200]{1,0:T(8,128)(2,1)S(1)}, u32[]{:S(2)}, u32[]{:S(2)}) collective-permute-start(bf16[48,3200]{1,0:T(8,128)(2,1)S(1)} %get-tuple-element.39), channel_id=1, source_target_pairs={{0,24},{4,28},{8,16},{12,20},{16,8},{20,12},{24,0},{28,4},{1,25},{... | collective-permute-start | bytes 921608 | tf_op jit(solution)/shard_map/ppermute | solution.py:491
  13.4 0.0 copy-done
  13.4 0.0 copy-done.1
  13.4 0.0 copy-done.3
  13.4 0.5 shard_map.75
  13.9 3.5 %collective-permute-start.4 = (bf16[48,896]{1,0:T(8,128)(2,1)S(1)}, bf16[48,896]{1,0:T(8,128)(2,1)S(1)}, u32[]{:S(2)}, u32[]{:S(2)}) collective-permute-start(bf16[48,896]{1,0:T(8,128)(2,1)S(1)} %get-tuple-element.32), channel_id=1, source_target_pairs={{0,1},{1,2},{2,3},{4,5},{5,6},{6,7},{8,9},{9,10},{10,11},{12,13},{... | collective-permute-start | bytes 258056 | tf_op jit(solution)/shard_map/ppermute | solution.py:502
  17.4 1.3 %collective-permute-start.5 = (bf16[48,896]{1,0:T(8,128)(2,1)S(1)}, bf16[48,896]{1,0:T(8,128)(2,1)S(1)}, u32[]{:S(2)}, u32[]{:S(2)}) collective-permute-start(bf16[48,896]{1,0:T(8,128)(2,1)S(1)} %get-tuple-element.33), channel_id=1, source_target_pairs={{1,0},{2,1},{3,2},{5,4},{6,5},{7,6},{9,8},{10,9},{11,10},{13,12},{... | collective-permute-start | bytes 258056 | tf_op jit(solution)/shard_map/ppermute | solution.py:503
  18.7 0.8 %collective-permute-done.4.low = bf16[48,896]{1,0:T(8,128)(2,1)S(1)} collective-permute-done((bf16[48,896]{1,0:T(8,128)(2,1)S(1)}, bf16[48,896]{1,0:T(8,128)(2,1)S(1)}, u32[]{:S(2)}, u32[]{:S(2)}) %collective-permute-start.4) | collective-permute-done | bytes 86048 | tf_op jit(solution)/shard_map/ppermute | solution.py:502
  19.5 4.3 %collective-permute-done.5.high = bf16[48,896]{1,0:T(8,128)(2,1)S(1)} collective-permute-done((bf16[48,896]{1,0:T(8,128)(2,1)S(1)}, bf16[48,896]{1,0:T(8,128)(2,1)S(1)}, u32[]{:S(2)}, u32[]{:S(2)}) %collective-permute-start.5) | collective-permute-done | bytes 86048 | tf_op jit(solution)/shard_map/ppermute | solution.py:503
  23.8 0.9 %shard_map.76 = (bf16[16,11648]{1,0:T(8,128)(2,1)}, bf16[16,11648]{1,0:T(8,128)(2,1)}) custom-call(bf16[48,6272]{1,0:T(8,128)(2,1)S(1)} %get-tuple-element.31.own, bf16[48,896]{1,0:T(8,128)(2,1)S(1)} %collective-permute-done.4.low, bf16[48,896]{1,0:T(8,128)(2,1)S(1)} %collective-permute-done.5.high), custom_call_target="tpu_custom_call" | custom-call | flops 1000 | bytes 1519616 | tf_op jit(solution)/shard_map/pallas_call | solution.py:444
  24.7 0.0 collective-permute-done.6.rest_0_
  24.7 0.0 collective-permute-done.7.rest_1_
  24.7 0.6 %collective-permute-done.8.rest_2_ = bf16[48,3200]{1,0:T(8,128)(2,1)S(1)} collective-permute-done((bf16[48,3200]{1,0:T(8,128)(2,1)S(1)}, bf16[48,3200]{1,0:T(8,128)(2,1)S(1)}, u32[]{:S(2)}, u32[]{:S(2)}) %collective-permute-start.8) | collective-permute-done | bytes 307232 | tf_op jit(solution)/shard_map/ppermute | solution.py:491
  25.4 1.9 %shard_map.77.rest_0_ = bf16[96,1664]{1,0:T(8,128)(2,1)S(1)} custom-call(f32[48,3072]{1,0:T(8,128)S(1)} %get-tuple-element.36.mine, bf16[48,3200]{1,0:T(8,128)(2,1)S(1)} %collective-permute-done.6.rest_0_, bf16[48,3200]{1,0:T(8,128)(2,1)S(1)} %collective-permute-done.7.rest_1_, bf16[48,3200]{1,0:T(8,128)(2,1)S(1)} %collective-permute-done.8.rest_2_), custom_call_target="tpu_custom_call" | custom-call | flops 17694720 | bytes 1830912 | tf_op jit(solution)/shard_map/pallas_call | solution.py:444
  27.3 2.6 %collective-permute-start.11 = (bf16[96,1664]{1,0:T(8,128)(2,1)S(1)}, bf16[96,1664]{1,0:T(8,128)(2,1)S(1)}, u32[]{:S(2)}, u32[]{:S(2)}) collective-permute-start(bf16[96,1664]{1,0:T(8,128)(2,1)S(1)} %shard_map.77.rest_0_), channel_id=1, source_target_pairs={{0,2},{1,3},{2,0},{3,1},{4,6},{5,7},{6,4},{7,5},{8,10},{9,11},{10,... | collective-permute-start | bytes 958472 | tf_op jit(solution)/shard_map/ppermute | solution.py:527
  29.9 1.6 %collective-permute-start.12 = (bf16[96,1664]{1,0:T(8,128)(2,1)S(1)}, bf16[96,1664]{1,0:T(8,128)(2,1)S(1)}, u32[]{:S(2)}, u32[]{:S(2)}) collective-permute-start(bf16[96,1664]{1,0:T(8,128)(2,1)S(1)} %shard_map.77.rest_0_), channel_id=1, source_target_pairs={{0,1},{1,0},{2,3},{3,2},{4,5},{5,4},{6,7},{7,6},{8,9},{9,8},{10,11... | collective-permute-start | bytes 958472 | tf_op jit(solution)/shard_map/ppermute | solution.py:527
  31.5 1.3 %collective-permute-start.10 = (bf16[16,11648]{1,0:T(8,128)(2,1)}, bf16[16,11648]{1,0:T(8,128)(2,1)S(1)}, u32[]{:S(2)}, u32[]{:S(2)}) collective-permute-start(bf16[16,11648]{1,0:T(8,128)(2,1)} %get-tuple-element.43), channel_id=1, source_target_pairs={{4,0},{8,4},{12,8},{16,12},{20,16},{24,20},{28,24},{5,1},{9,5},{13... | collective-permute-start | bytes 1118216 | tf_op jit(solution)/shard_map/ppermute | solution.py:543
  32.8 3.1 %collective-permute-start.9 = (bf16[16,11648]{1,0:T(8,128)(2,1)}, bf16[16,11648]{1,0:T(8,128)(2,1)S(1)}, u32[]{:S(2)}, u32[]{:S(2)}) collective-permute-start(bf16[16,11648]{1,0:T(8,128)(2,1)} %get-tuple-element.42), channel_id=1, source_target_pairs={{0,4},{4,8},{8,12},{12,16},{16,20},{20,24},{24,28},{1,5},{5,9},{9,... | collective-permute-start | bytes 1118216 | tf_op jit(solution)/shard_map/ppermute | solution.py:542
  35.9 6.6 %collective-permute-done.11.rest_1_ = bf16[96,1664]{1,0:T(8,128)(2,1)S(1)} collective-permute-done((bf16[96,1664]{1,0:T(8,128)(2,1)S(1)}, bf16[96,1664]{1,0:T(8,128)(2,1)S(1)}, u32[]{:S(2)}, u32[]{:S(2)}) %collective-permute-start.11) | collective-permute-done | bytes 319520 | tf_op jit(solution)/shard_map/ppermute | solution.py:527
  42.5 0.2 collective-permute-done.12.rest_2_
  42.7 0.7 %collective-permute-start.13 = (bf16[96,1664]{1,0:T(8,128)(2,1)S(1)}, bf16[96,1664]{1,0:T(8,128)(2,1)S(1)}, u32[]{:S(2)}, u32[]{:S(2)}) collective-permute-start(bf16[96,1664]{1,0:T(8,128)(2,1)S(1)} %shard_map.77.rest_0_), channel_id=1, source_target_pairs={{1,2},{2,1},{5,6},{6,5},{9,10},{10,9},{13,14},{14,13},{17,18},{18,... | collective-permute-start | bytes 958472 | tf_op jit(solution)/shard_map/ppermute | solution.py:534
  43.3 1.3 %collective-permute-start.14 = (bf16[96,1664]{1,0:T(8,128)(2,1)S(1)}, bf16[96,1664]{1,0:T(8,128)(2,1)S(1)}, u32[]{:S(2)}, u32[]{:S(2)}) collective-permute-start(bf16[96,1664]{1,0:T(8,128)(2,1)S(1)} %collective-permute-done.11.rest_1_), channel_id=1, source_target_pairs={{1,0},{2,3},{5,4},{6,7},{9,8},{10,11},{13,12},{14,15},{17,16},{18,... | collective-permute-start | bytes 958472 | tf_op jit(solution)/shard_map/ppermute | solution.py:535
  44.6 0.0 copy-done.6
  44.6 0.1 copy.8.depth_factor
  44.8 0.9 %copy-done.4 = bf16[96,384]{1,0:T(8,128)(2,1)S(1)} copy-done((bf16[96,384]{1,0:T(8,128)(2,1)S(1)}, bf16[96,384]{1,0:T(8,128)(2,1)}, u32[]{:S(2)}) %copy-start.4) | copy-done | bytes 73752
  45.6 1.6 %shard_map.79.earlier = f32[96,1536]{1,0:T(8,128)S(1)} custom-call(bf16[96,384]{1,0:T(8,128)(2,1)S(1)} %copy-done.4, bf16[96,1664]{1,0:T(8,128)(2,1)S(1)} %shard_map.77.rest_0_, bf16[96,1664]{1,0:T(8,128)(2,1)S(1)} %collective-permute-done.11.rest_1_, bf16[96,1664]{1,0:T(8,128)(2,1)S(1)} %collective-permute-done.12.rest_2_), custom_call_target="tpu_custom_call" | custom-call | flops 226492416 | bytes 1622016 | tf_op jit(solution)/shard_map/pallas_call | solution.py:444
  47.3 0.0 collective-permute-done.10.right
  47.3 0.0 collective-permute-done.9.left
  47.3 5.1 %shard_map.78.waves = f32[48,48,128]{2,1,0:T(8,128)S(1)} custom-call(f32[16,6144]{1,0:T(8,128)S(1)} %copy-done, f32[16,6144]{1,0:T(8,128)S(1)} %copy-done.1, bf16[16,6144]{1,0:T(8,128)(2,1)S(1)} %copy-done.3, bf16[16,11648]{1,0:T(8,128)(2,1)S(1)} %collective-permute-done.9.left, bf16[16,11648]{1,0:T(8,128)(2,1)S(1)} %collective-permute-done.10.right, ...), custom_call_target="tpu_custom_call" | custom-call | flops 44236800 | bytes 3080192 | tf_op jit(solution)/shard_map/pallas_call | solution.py:444
  52.4 0.0 collective-permute-done.13.rest_0_
  52.4 1.5 %collective-permute-done.14.rest_1_ = bf16[96,1664]{1,0:T(8,128)(2,1)S(1)} collective-permute-done((bf16[96,1664]{1,0:T(8,128)(2,1)S(1)}, bf16[96,1664]{1,0:T(8,128)(2,1)S(1)}, u32[]{:S(2)}, u32[]{:S(2)}) %collective-permute-start.14) | collective-permute-done | bytes 319520 | tf_op jit(solution)/shard_map/ppermute | solution.py:535
  53.9 2.2 %shard_map.80 = f32[16,6144]{1,0:T(8,128)} custom-call(bf16[96,384]{1,0:T(8,128)(2,1)S(1)} %copy-done.4, bf16[64,32]{1,0:T(8,128)(2,1)S(1)} %copy.8.depth_factor, f32[48,48,128]{2,1,0:T(8,128)S(1)} %shard_map.78.waves, f32[96,1536]{1,0:T(8,128)S(1)} %shard_map.79.earlier, bf16[96,1664]{1,0:T(8,128)(2,1)S(1)} %collective-permute-done.13.rest_0_, ...), custom_call_target="tpu_custom_call" | custom-call | flops 56623104 | bytes 2879488 | tf_op jit(solution)/shard_map/pallas_call | solution.py:444
  (5 shorter events, 0.0 us)
Async XLA Ops:
  0.0 13.4 %copy-start = (f32[16,6144]{1,0:T(8,128)S(1)}, f32[16,6144]{1,0:T(8,128)}, u32[]{:S(2)}) copy-start(f32[16,6144]{1,0:T(8,128)} %pressure.2) | copy-start | bytes 1179652
  0.0 13.4 %copy-start.1 = (f32[16,6144]{1,0:T(8,128)S(1)}, f32[16,6144]{1,0:T(8,128)}, u32[]{:S(2)}) copy-start(f32[16,6144]{1,0:T(8,128)} %previous.3) | copy-start | bytes 1179652
  0.0 8.4 %collective-permute-start = (bf16[3,48,3072]{2,1,0:T(8,128)(2,1)}, bf16[3,48,3072]{2,1,0:T(8,128)(2,1)S(1)}, u32[]{:S(2)}, u32[]{:S(2)}) collective-permute-start(bf16[3,48,3072]{2,1,0:T(8,128)(2,1)} %core.1), channel_id=1, source_target_pairs={{0,4},{4,0},{8,12},{12,8},{16,20},{20,16},{24,28},{28,24},{1,5},{5... | collective-permute-start | bytes 2654216 | tf_op jit(solution)/shard_map/ppermute | solution.py:472
  0.5 6.1 %collective-permute-start.1 = (bf16[16,384]{1,0:T(8,128)(2,1)}, bf16[16,384]{1,0:T(8,128)(2,1)S(1)}, u32[]{:S(2)}, u32[]{:S(2)}) collective-permute-start(bf16[16,384]{1,0:T(8,128)(2,1)} %factor.1), channel_id=1, source_target_pairs={{0,24},{4,28},{8,16},{12,20},{16,8},{20,12},{24,0},{28,4},{1,25},{... | collective-permute-start | bytes 36872 | tf_op jit(solution)/shard_map/ppermute | solution.py:471
  4.0 3.9 %collective-permute-start.2 = (bf16[16,384]{1,0:T(8,128)(2,1)}, bf16[16,384]{1,0:T(8,128)(2,1)S(1)}, u32[]{:S(2)}, u32[]{:S(2)}) collective-permute-start(bf16[16,384]{1,0:T(8,128)(2,1)} %factor.1), channel_id=1, source_target_pairs={{0,16},{4,20},{8,24},{12,28},{16,0},{20,4},{24,8},{28,12},{1,17},{... | collective-permute-start | bytes 36872 | tf_op jit(solution)/shard_map/ppermute | solution.py:471
  4.5 3.9 %collective-permute-start.3 = (bf16[16,384]{1,0:T(8,128)(2,1)}, bf16[16,384]{1,0:T(8,128)(2,1)S(1)}, u32[]{:S(2)}, u32[]{:S(2)}) collective-permute-start(bf16[16,384]{1,0:T(8,128)(2,1)} %factor.1), channel_id=1, source_target_pairs={{0,8},{4,12},{8,0},{12,4},{16,24},{20,28},{24,16},{28,20},{1,9},{5... | collective-permute-start | bytes 36872 | tf_op jit(solution)/shard_map/ppermute | solution.py:471
  4.6 1.2 %copy-start.2 = (bf16[3,48,3072]{2,1,0:T(8,128)(2,1)S(1)}, bf16[3,48,3072]{2,1,0:T(8,128)(2,1)}, u32[]{:S(2)}) copy-start(bf16[3,48,3072]{2,1,0:T(8,128)(2,1)} %core.1) | copy-start | bytes 2654212
  5.8 0.7 %copy-start.5 = (bf16[16,384]{1,0:T(8,128)(2,1)S(1)}, bf16[16,384]{1,0:T(8,128)(2,1)}, u32[]{:S(2)}) copy-start(bf16[16,384]{1,0:T(8,128)(2,1)} %factor.1) | copy-start | bytes 36868
  6.5 6.9 %copy-start.3 = (bf16[16,6144]{1,0:T(8,128)(2,1)S(1)}, bf16[16,6144]{1,0:T(8,128)(2,1)}, u32[]{:S(2)}) copy-start(bf16[16,6144]{1,0:T(8,128)(2,1)} %velocity.3) | copy-start | bytes 589828
  9.8 14.9 %collective-permute-start.6 = (bf16[48,3200]{1,0:T(8,128)(2,1)S(1)}, bf16[48,3200]{1,0:T(8,128)(2,1)S(1)}, u32[]{:S(2)}, u32[]{:S(2)}) collective-permute-start(bf16[48,3200]{1,0:T(8,128)(2,1)S(1)} %get-tuple-element.37), channel_id=1, source_target_pairs={{0,8},{4,12},{8,0},{12,4},{16,24},{20,28},{24,16},{28,20},{1,9},{5... | collective-permute-start | bytes 921608 | tf_op jit(solution)/shard_map/ppermute | solution.py:491
  10.1 14.7 %collective-permute-start.7 = (bf16[48,3200]{1,0:T(8,128)(2,1)S(1)}, bf16[48,3200]{1,0:T(8,128)(2,1)S(1)}, u32[]{:S(2)}, u32[]{:S(2)}) collective-permute-start(bf16[48,3200]{1,0:T(8,128)(2,1)S(1)} %get-tuple-element.38), channel_id=1, source_target_pairs={{0,16},{4,20},{8,24},{12,28},{16,0},{20,4},{24,8},{28,12},{1,17},{... | collective-permute-start | bytes 921608 | tf_op jit(solution)/shard_map/ppermute | solution.py:491
  12.0 13.4 %collective-permute-start.8 = (bf16[48,3200]{1,0:T(8,128)(2,1)S(1)}, bf16[48,3200]{1,0:T(8,128)(2,1)S(1)}, u32[]{:S(2)}, u32[]{:S(2)}) collective-permute-start(bf16[48,3200]{1,0:T(8,128)(2,1)S(1)} %get-tuple-element.39), channel_id=1, source_target_pairs={{0,24},{4,28},{8,16},{12,20},{16,8},{20,12},{24,0},{28,4},{1,25},{... | collective-permute-start | bytes 921608 | tf_op jit(solution)/shard_map/ppermute | solution.py:491
  13.9 5.6 %collective-permute-start.4 = (bf16[48,896]{1,0:T(8,128)(2,1)S(1)}, bf16[48,896]{1,0:T(8,128)(2,1)S(1)}, u32[]{:S(2)}, u32[]{:S(2)}) collective-permute-start(bf16[48,896]{1,0:T(8,128)(2,1)S(1)} %get-tuple-element.32), channel_id=1, source_target_pairs={{0,1},{1,2},{2,3},{4,5},{5,6},{6,7},{8,9},{9,10},{10,11},{12,13},{... | collective-permute-start | bytes 258056 | tf_op jit(solution)/shard_map/ppermute | solution.py:502
  17.4 6.4 %collective-permute-start.5 = (bf16[48,896]{1,0:T(8,128)(2,1)S(1)}, bf16[48,896]{1,0:T(8,128)(2,1)S(1)}, u32[]{:S(2)}, u32[]{:S(2)}) collective-permute-start(bf16[48,896]{1,0:T(8,128)(2,1)S(1)} %get-tuple-element.33), channel_id=1, source_target_pairs={{1,0},{2,1},{3,2},{5,4},{6,5},{7,6},{9,8},{10,9},{11,10},{13,12},{... | collective-permute-start | bytes 258056 | tf_op jit(solution)/shard_map/ppermute | solution.py:503
  23.8 20.9 %copy-start.6 = (bf16[64,32]{0,1:T(8,128)(2,1)S(1)}, bf16[64,32]{0,1:T(8,128)(2,1)}, u32[]{:S(2)}) copy-start(bf16[64,32]{0,1:T(8,128)(2,1)} %param.13) | copy-start | bytes 12292
  27.3 15.2 %collective-permute-start.11 = (bf16[96,1664]{1,0:T(8,128)(2,1)S(1)}, bf16[96,1664]{1,0:T(8,128)(2,1)S(1)}, u32[]{:S(2)}, u32[]{:S(2)}) collective-permute-start(bf16[96,1664]{1,0:T(8,128)(2,1)S(1)} %shard_map.77.rest_0_), channel_id=1, source_target_pairs={{0,2},{1,3},{2,0},{3,1},{4,6},{5,7},{6,4},{7,5},{8,10},{9,11},{10,... | collective-permute-start | bytes 958472 | tf_op jit(solution)/shard_map/ppermute | solution.py:527
  29.9 12.7 %collective-permute-start.12 = (bf16[96,1664]{1,0:T(8,128)(2,1)S(1)}, bf16[96,1664]{1,0:T(8,128)(2,1)S(1)}, u32[]{:S(2)}, u32[]{:S(2)}) collective-permute-start(bf16[96,1664]{1,0:T(8,128)(2,1)S(1)} %shard_map.77.rest_0_), channel_id=1, source_target_pairs={{0,1},{1,0},{2,3},{3,2},{4,5},{5,4},{6,7},{7,6},{8,9},{9,8},{10,11... | collective-permute-start | bytes 958472 | tf_op jit(solution)/shard_map/ppermute | solution.py:527
  31.5 15.8 %collective-permute-start.10 = (bf16[16,11648]{1,0:T(8,128)(2,1)}, bf16[16,11648]{1,0:T(8,128)(2,1)S(1)}, u32[]{:S(2)}, u32[]{:S(2)}) collective-permute-start(bf16[16,11648]{1,0:T(8,128)(2,1)} %get-tuple-element.43), channel_id=1, source_target_pairs={{4,0},{8,4},{12,8},{16,12},{20,16},{24,20},{28,24},{5,1},{9,5},{13... | collective-permute-start | bytes 1118216 | tf_op jit(solution)/shard_map/ppermute | solution.py:543
  32.8 14.5 %collective-permute-start.9 = (bf16[16,11648]{1,0:T(8,128)(2,1)}, bf16[16,11648]{1,0:T(8,128)(2,1)S(1)}, u32[]{:S(2)}, u32[]{:S(2)}) collective-permute-start(bf16[16,11648]{1,0:T(8,128)(2,1)} %get-tuple-element.42), channel_id=1, source_target_pairs={{0,4},{4,8},{8,12},{12,16},{16,20},{20,24},{24,28},{1,5},{5,9},{9,... | collective-permute-start | bytes 1118216 | tf_op jit(solution)/shard_map/ppermute | solution.py:542
  42.7 9.7 %collective-permute-start.13 = (bf16[96,1664]{1,0:T(8,128)(2,1)S(1)}, bf16[96,1664]{1,0:T(8,128)(2,1)S(1)}, u32[]{:S(2)}, u32[]{:S(2)}) collective-permute-start(bf16[96,1664]{1,0:T(8,128)(2,1)S(1)} %shard_map.77.rest_0_), channel_id=1, source_target_pairs={{1,2},{2,1},{5,6},{6,5},{9,10},{10,9},{13,14},{14,13},{17,18},{18,... | collective-permute-start | bytes 958472 | tf_op jit(solution)/shard_map/ppermute | solution.py:534
  43.3 10.6 %collective-permute-start.14 = (bf16[96,1664]{1,0:T(8,128)(2,1)S(1)}, bf16[96,1664]{1,0:T(8,128)(2,1)S(1)}, u32[]{:S(2)}, u32[]{:S(2)}) collective-permute-start(bf16[96,1664]{1,0:T(8,128)(2,1)S(1)} %collective-permute-done.11.rest_1_), channel_id=1, source_target_pairs={{1,0},{2,3},{5,4},{6,7},{9,8},{10,11},{13,12},{14,15},{17,16},{18,... | collective-permute-start | bytes 958472 | tf_op jit(solution)/shard_map/ppermute | solution.py:535
  44.7 0.9 %copy-start.4 = (bf16[96,384]{1,0:T(8,128)(2,1)S(1)}, bf16[96,384]{1,0:T(8,128)(2,1)}, u32[]{:S(2)}) copy-start(bf16[96,384]{1,0:T(8,128)(2,1)} %second.3) | copy-start | bytes 221188

commit v6 on v5

--- a/solution.py
+++ b/solution.py
@@ -250,7 +250,8 @@
     factor_near[...] = factor[...]
 
 
-def pack_kernel(pressure, previous, velocity, own, up, down):
+def pack_kernel(pressure, previous, velocity, second, own, up, down, second_near):
+    second_near[...] = second[...]
     cells, flat = pressure.shape
     span = up.shape[1] - LANES
     for row, part in ((0, pressure), (cells, previous)):
@@ -424,15 +425,10 @@
     for step in range(steps):
         now, before, shift, tile_shift, later = chain[step]
         top, rows = (cells - half, 2 * cells) if later is not None else (cells, cells)
-        margin = inner if later is not None else 0
-
-        def loop(block, carry):
-            for group in range(2):
-                tile = edge - margin + 2 * count * block + group * count
-                advance(now, before, shift, tile_shift, later, step * cells, top, rows, tile)
-            return carry
-
-        lax.fori_loop(0, (own_tiles + 2 * margin) // (2 * count), loop, 0)
+        margin = (steps - 1 - step) * (edge // steps)
+
+        for tile in range(edge - margin, edge + own_tiles + margin, count):
+            advance(now, before, shift, tile_shift, later, step * cells, top, rows, tile)
         if later is not None:
             for tile in range(own_tiles):
                 waves[tile, step * cells : (step + 1) * cells, :] = later[edge + tile, cells : 2 * cells, :]
@@ -490,14 +486,17 @@
     )
     received = [lax.ppermute(send, "gx", route) for send, route in zip(sends, across)]
     pressure_later, _ = lax.optimization_barrier((pressure, mine))
-    own, up, down = call(
+    own, up, down, second_near = call(
         pack_kernel,
-        [shape_of(3 * cells, flat + LANES, dtype=BF16)] + [shape_of(3 * cells, span + LANES, dtype=BF16)] * 2,
+        [shape_of(3 * cells, flat + LANES, dtype=BF16)]
+        + [shape_of(3 * cells, span + LANES, dtype=BF16)] * 2
+        + [shape_of(*second_factor.shape, dtype=BF16)],
         [],
         10 * cells * flat,
         pressure_later,
         previous,
         velocity,
+        second_factor,
     )
     low = lax.ppermute(up, "gy", [(i, i + 1) for i in range(count_y - 1)])
     high = lax.ppermute(down, "gy", [(i + 1, i) for i in range(count_y - 1)])
@@ -561,7 +560,7 @@
         [shape_of(cells_y, lines * depth)],
         [pltpu.VMEM((2 * (count_y - 1), local_second, lines * depth), BF16)],
         4 * cells_y * count_y * local_second * lines * depth,
-        second_factor,
+        second_near,
         *blocks,
     )
     (image,) = call(
@@ -573,7 +572,7 @@
             pltpu.VMEM((cells_y * lines_pad, LANES), F32),
         ],
         4 * cells_y * local_second * lines * depth,
-        second_factor,
+        second_near,
         depth_factor,
         waves,
         mixed,

time: 56.5 us -> 56.5 us (level)
  waiting for transfers between devices: 15.9 us -> 19.4 us
  Pallas kernels: 13.8 us -> 12 us
  starting transfers between devices: 23.5 us -> 21.7 us
    ppermute x1, waiting for transfers between devices: 1.54 us -> 3.34 us  [body(): lax.ppermute(blocks[1], 'gy', [(1, 0), (2, 3)])]
    pallas_call x8, Pallas kernels: 13.8 us -> 12 us  [call(): pl.pallas_call(kernel, out_shape=outs, scratch_shapes=scratch, cost_estim...]
    ppermute x1, starting transfers between devices: 3.05 us -> 1.3 us  [body(): left = lax.ppermute(ahead, 'gx', [(i, i + 1) for i in range(count_x - 1)])]
    ppermute x2, waiting for transfers between devices: 6.8 us -> 8.52 us  [far(): lax.ppermute(codes, 'gy', [(i, i ^ distance) for i in range(count_y)])]
    unnamed x15 -> x19, local copies, waits for them, and re-layouts: 2.87 us -> 2.88 us
  transfers between devices with their start and end apart: 15 -> 15, of which waited for: 8 -> 8; matrix products, arithmetic and copies ran while one was open for 0% -> 0% of each run, Pallas kernels for 15% -> 11%
where the time goes in v6:
time: 56.5 us; the launch traced here: 56.1 us
  starting transfers between devices  21.7 us (38%)
  waiting for transfers between devices  19.4 us (34%)
  Pallas kernels  12 us (21%)
  local copies, waits for them, and re-layouts  2.88 us (5%)
    pallas_call x8, Pallas kernels, call(): pl.pallas_call(kernel, out_shape=outs, scratch_shapes=scratch, cost_estim...  12 us
    ppermute x2, waiting for transfers between devices, far(): lax.ppermute(codes, 'gy', [(i, i ^ distance) for i in range(count_y)])  8.52 us
    ppermute x1, waiting for transfers between devices, body(): high = lax.ppermute(down, 'gy', [(i + 1, i) for i in range(count_y - 1)])  4.3 us
    ppermute x2, starting transfers between devices, far(): lax.ppermute(codes, 'gy', [(i, i ^ distance) for i in range(count_y)])  4.23 us
    ppermute x3, starting transfers between devices, body(): lax.ppermute(first_factor, 'gx', route)  4.17 us
    ppermute x3, starting transfers between devices, body(): lax.ppermute(send, 'gx', route)  3.55 us
    ppermute x1, starting transfers between devices, body(): low = lax.ppermute(up, 'gy', [(i, i + 1) for i in range(count_y - 1)])  3.48 us
    ppermute x1, waiting for transfers between devices, body(): lax.ppermute(blocks[1], 'gy', [(1, 0), (2, 3)])  3.34 us
  transfers between devices with their start and end apart: 15, of which 8 were waited for; matrix products, arithmetic and copies ran while one was open for 0% of the time, Pallas kernels for 11%

profile of v6, /device:TPU:0, one launch (start us, length us, event | category | flops | bytes accessed | tf_op | source)
XLA Modules:
  0.0 56.1 jit_solution(7298865664385999560)
XLA Ops:
  0.0 0.5 collective-permute-start
  0.5 3.5 %collective-permute-start.1 = (bf16[16,384]{1,0:T(8,128)(2,1)}, bf16[16,384]{1,0:T(8,128)(2,1)S(1)}, u32[]{:S(2)}, u32[]{:S(2)}) collective-permute-start(bf16[16,384]{1,0:T(8,128)(2,1)} %factor.1), channel_id=1, source_target_pairs={{0,24},{4,28},{8,16},{12,20},{16,8},{20,12},{24,0},{28,4},{1,25},{... | collective-permute-start | bytes 36872 | tf_op jit(solution)/shard_map/ppermute | solution.py:467
  4.0 0.5 collective-permute-start.2
  4.5 0.1 collective-permute-start.3
  4.6 1.2 %copy-done.2 = bf16[3,48,3072]{2,1,0:T(8,128)(2,1)S(1)} copy-done((bf16[3,48,3072]{2,1,0:T(8,128)(2,1)S(1)}, bf16[3,48,3072]{2,1,0:T(8,128)(2,1)}, u32[]{:S(2)}) %copy-start.2) | copy-done | bytes 884760
  5.8 0.7 %copy-done.7 = bf16[16,384]{1,0:T(8,128)(2,1)S(1)} copy-done((bf16[16,384]{1,0:T(8,128)(2,1)S(1)}, bf16[16,384]{1,0:T(8,128)(2,1)}, u32[]{:S(2)}) %copy-start.7) | copy-done | bytes 12312
  6.5 0.1 shard_map.73
  6.6 0.0 collective-permute-done.1.rest_0_
  6.6 1.3 %collective-permute-done.2.rest_1_ = bf16[16,384]{1,0:T(8,128)(2,1)S(1)} collective-permute-done((bf16[16,384]{1,0:T(8,128)(2,1)}, bf16[16,384]{1,0:T(8,128)(2,1)S(1)}, u32[]{:S(2)}, u32[]{:S(2)}) %collective-permute-start.2) | collective-permute-done | bytes 12320 | tf_op jit(solution)/shard_map/ppermute | solution.py:467
  7.9 0.5 collective-permute-done.3.rest_2_
  8.4 0.0 collective-permute-done.other
  8.4 1.4 %shard_map.74 = (f32[48,3072]{1,0:T(8,128)S(1)}, bf16[48,3200]{1,0:T(8,128)(2,1)S(1)}, bf16[48,3200]{1,0:T(8,128)(2,1)S(1)}, bf16[48,3200]{1,0:T(8,128)(2,1)S(1)}) custom-call(bf16[3,48,3072]{2,1,0:T(8,128)(2,1)S(1)} %get-tuple-element.28.core, bf16[3,48,3072]{2,1,0:T(8,128)(2,1)S(1)} %collective-permute-done.other, ...), custom_call_target="tpu_custom_call" | custom-call | flops 113246208 | bytes 3330048 | tf_op jit(solution)/shard_map/pallas_call | solution.py:440
  9.8 0.2 collective-permute-start.6
  10.1 1.9 %collective-permute-start.7 = (bf16[48,3200]{1,0:T(8,128)(2,1)S(1)}, bf16[48,3200]{1,0:T(8,128)(2,1)S(1)}, u32[]{:S(2)}, u32[]{:S(2)}) collective-permute-start(bf16[48,3200]{1,0:T(8,128)(2,1)S(1)} %get-tuple-element.40), channel_id=1, source_target_pairs={{0,16},{4,20},{8,24},{12,28},{16,0},{20,4},{24,8},{28,12},{1,17},{... | collective-permute-start | bytes 921608 | tf_op jit(solution)/shard_map/ppermute | solution.py:487
  12.0 1.4 %collective-permute-start.8 = (bf16[48,3200]{1,0:T(8,128)(2,1)S(1)}, bf16[48,3200]{1,0:T(8,128)(2,1)S(1)}, u32[]{:S(2)}, u32[]{:S(2)}) collective-permute-start(bf16[48,3200]{1,0:T(8,128)(2,1)S(1)} %get-tuple-element.41), channel_id=1, source_target_pairs={{0,24},{4,28},{8,16},{12,20},{16,8},{20,12},{24,0},{28,4},{1,25},{... | collective-permute-start | bytes 921608 | tf_op jit(solution)/shard_map/ppermute | solution.py:487
  13.4 0.0 copy-done
  13.4 0.0 copy-done.1
  13.4 0.0 copy-done.3
  13.4 0.0 copy-done.6
  13.4 0.5 shard_map.75
  13.9 0.0 copy-start.4
  13.9 3.5 %collective-permute-start.4 = (bf16[48,896]{1,0:T(8,128)(2,1)S(1)}, bf16[48,896]{1,0:T(8,128)(2,1)S(1)}, u32[]{:S(2)}, u32[]{:S(2)}) collective-permute-start(bf16[48,896]{1,0:T(8,128)(2,1)S(1)} %get-tuple-element.34), channel_id=1, source_target_pairs={{0,1},{1,2},{2,3},{4,5},{5,6},{6,7},{8,9},{9,10},{10,11},{12,13},{... | collective-permute-start | bytes 258056 | tf_op jit(solution)/shard_map/ppermute | solution.py:501
  17.4 1.3 %collective-permute-start.5 = (bf16[48,896]{1,0:T(8,128)(2,1)S(1)}, bf16[48,896]{1,0:T(8,128)(2,1)S(1)}, u32[]{:S(2)}, u32[]{:S(2)}) collective-permute-start(bf16[48,896]{1,0:T(8,128)(2,1)S(1)} %get-tuple-element.35), channel_id=1, source_target_pairs={{1,0},{2,1},{3,2},{5,4},{6,5},{7,6},{9,8},{10,9},{11,10},{13,12},{... | collective-permute-start | bytes 258056 | tf_op jit(solution)/shard_map/ppermute | solution.py:502
  18.7 0.8 %collective-permute-done.4.low = bf16[48,896]{1,0:T(8,128)(2,1)S(1)} collective-permute-done((bf16[48,896]{1,0:T(8,128)(2,1)S(1)}, bf16[48,896]{1,0:T(8,128)(2,1)S(1)}, u32[]{:S(2)}, u32[]{:S(2)}) %collective-permute-start.4) | collective-permute-done | bytes 86048 | tf_op jit(solution)/shard_map/ppermute | solution.py:501
  19.5 4.3 %collective-permute-done.5.high = bf16[48,896]{1,0:T(8,128)(2,1)S(1)} collective-permute-done((bf16[48,896]{1,0:T(8,128)(2,1)S(1)}, bf16[48,896]{1,0:T(8,128)(2,1)S(1)}, u32[]{:S(2)}, u32[]{:S(2)}) %collective-permute-start.5) | collective-permute-done | bytes 86048 | tf_op jit(solution)/shard_map/ppermute | solution.py:502
  23.8 0.9 %shard_map.76 = (bf16[16,11648]{1,0:T(8,128)(2,1)}, bf16[16,11648]{1,0:T(8,128)(2,1)}) custom-call(bf16[48,6272]{1,0:T(8,128)(2,1)S(1)} %get-tuple-element.33.own, bf16[48,896]{1,0:T(8,128)(2,1)S(1)} %collective-permute-done.4.low, bf16[48,896]{1,0:T(8,128)(2,1)S(1)} %collective-permute-done.5.high), custom_call_target="tpu_custom_call" | custom-call | flops 1000 | bytes 1519616 | tf_op jit(solution)/shard_map/pallas_call | solution.py:440
  24.7 0.0 collective-permute-done.6.rest_0_
  24.7 0.0 collective-permute-done.7.rest_1_
  24.7 0.6 %collective-permute-done.8.rest_2_ = bf16[48,3200]{1,0:T(8,128)(2,1)S(1)} collective-permute-done((bf16[48,3200]{1,0:T(8,128)(2,1)S(1)}, bf16[48,3200]{1,0:T(8,128)(2,1)S(1)}, u32[]{:S(2)}, u32[]{:S(2)}) %collective-permute-start.8) | collective-permute-done | bytes 307232 | tf_op jit(solution)/shard_map/ppermute | solution.py:487
  25.4 1.9 %shard_map.77.rest_0_ = bf16[96,1664]{1,0:T(8,128)(2,1)S(1)} custom-call(f32[48,3072]{1,0:T(8,128)S(1)} %get-tuple-element.38.mine, bf16[48,3200]{1,0:T(8,128)(2,1)S(1)} %collective-permute-done.6.rest_0_, bf16[48,3200]{1,0:T(8,128)(2,1)S(1)} %collective-permute-done.7.rest_1_, bf16[48,3200]{1,0:T(8,128)(2,1)S(1)} %collective-permute-done.8.rest_2_), custom_call_target="tpu_custom_call" | custom-call | flops 17694720 | bytes 1830912 | tf_op jit(solution)/shard_map/pallas_call | solution.py:440
  27.3 0.0 copy-done.4
  27.3 2.7 %collective-permute-start.11 = (bf16[96,1664]{1,0:T(8,128)(2,1)S(1)}, bf16[96,1664]{1,0:T(8,128)(2,1)S(1)}, u32[]{:S(2)}, u32[]{:S(2)}) collective-permute-start(bf16[96,1664]{1,0:T(8,128)(2,1)S(1)} %shard_map.77.rest_0_), channel_id=1, source_target_pairs={{0,2},{1,3},{2,0},{3,1},{4,6},{5,7},{6,4},{7,5},{8,10},{9,11},{10,... | collective-permute-start | bytes 958472 | tf_op jit(solution)/shard_map/ppermute | solution.py:526
  29.9 1.6 %collective-permute-start.12 = (bf16[96,1664]{1,0:T(8,128)(2,1)S(1)}, bf16[96,1664]{1,0:T(8,128)(2,1)S(1)}, u32[]{:S(2)}, u32[]{:S(2)}) collective-permute-start(bf16[96,1664]{1,0:T(8,128)(2,1)S(1)} %shard_map.77.rest_0_), channel_id=1, source_target_pairs={{0,1},{1,0},{2,3},{3,2},{4,5},{5,4},{6,7},{7,6},{8,9},{9,8},{10,11... | collective-permute-start | bytes 958472 | tf_op jit(solution)/shard_map/ppermute | solution.py:526
  31.5 1.3 %collective-permute-start.9 = (bf16[16,11648]{1,0:T(8,128)(2,1)}, bf16[16,11648]{1,0:T(8,128)(2,1)S(1)}, u32[]{:S(2)}, u32[]{:S(2)}) collective-permute-start(bf16[16,11648]{1,0:T(8,128)(2,1)} %get-tuple-element.44), channel_id=1, source_target_pairs={{0,4},{4,8},{8,12},{12,16},{16,20},{20,24},{24,28},{1,5},{5,9},{9,... | collective-permute-start | bytes 1118216 | tf_op jit(solution)/shard_map/ppermute | solution.py:541
  32.8 1.3 %collective-permute-start.10 = (bf16[16,11648]{1,0:T(8,128)(2,1)}, bf16[16,11648]{1,0:T(8,128)(2,1)S(1)}, u32[]{:S(2)}, u32[]{:S(2)}) collective-permute-start(bf16[16,11648]{1,0:T(8,128)(2,1)} %get-tuple-element.45), channel_id=1, source_target_pairs={{4,0},{8,4},{12,8},{16,12},{20,16},{24,20},{28,24},{5,1},{9,5},{13... | collective-permute-start | bytes 1118216 | tf_op jit(solution)/shard_map/ppermute | solution.py:542
  34.1 8.3 %collective-permute-done.11.rest_1_ = bf16[96,1664]{1,0:T(8,128)(2,1)S(1)} collective-permute-done((bf16[96,1664]{1,0:T(8,128)(2,1)S(1)}, bf16[96,1664]{1,0:T(8,128)(2,1)S(1)}, u32[]{:S(2)}, u32[]{:S(2)}) %collective-permute-start.11) | collective-permute-done | bytes 319520 | tf_op jit(solution)/shard_map/ppermute | solution.py:526
  42.5 0.2 collective-permute-done.12.rest_2_
  42.7 0.7 %collective-permute-start.13 = (bf16[96,1664]{1,0:T(8,128)(2,1)S(1)}, bf16[96,1664]{1,0:T(8,128)(2,1)S(1)}, u32[]{:S(2)}, u32[]{:S(2)}) collective-permute-start(bf16[96,1664]{1,0:T(8,128)(2,1)S(1)} %shard_map.77.rest_0_), channel_id=1, source_target_pairs={{1,2},{2,1},{5,6},{6,5},{9,10},{10,9},{13,14},{14,13},{17,18},{18,... | collective-permute-start | bytes 958472 | tf_op jit(solution)/shard_map/ppermute | solution.py:533
  43.3 1.3 %collective-permute-start.14 = (bf16[96,1664]{1,0:T(8,128)(2,1)S(1)}, bf16[96,1664]{1,0:T(8,128)(2,1)S(1)}, u32[]{:S(2)}, u32[]{:S(2)}) collective-permute-start(bf16[96,1664]{1,0:T(8,128)(2,1)S(1)} %collective-permute-done.11.rest_1_), channel_id=1, source_target_pairs={{1,0},{2,3},{5,4},{6,7},{9,8},{10,11},{13,12},{14,15},{17,16},{18,... | collective-permute-start | bytes 958472 | tf_op jit(solution)/shard_map/ppermute | solution.py:534
  44.6 0.1 copy.8.depth_factor
  44.7 0.9 %copy-done.5 = bf16[96,384]{1,0:T(8,128)(2,1)S(1)} copy-done((bf16[96,384]{1,0:T(8,128)(2,1)S(1)}, bf16[96,384]{1,0:T(8,128)(2,1)}, u32[]{:S(2)}) %copy-start.5) | copy-done | bytes 73752
  45.6 1.6 %shard_map.79.earlier = f32[96,1536]{1,0:T(8,128)S(1)} custom-call(bf16[96,384]{1,0:T(8,128)(2,1)S(1)} %copy-done.5, bf16[96,1664]{1,0:T(8,128)(2,1)S(1)} %shard_map.77.rest_0_, bf16[96,1664]{1,0:T(8,128)(2,1)S(1)} %collective-permute-done.11.rest_1_, bf16[96,1664]{1,0:T(8,128)(2,1)S(1)} %collective-permute-done.12.rest_2_), custom_call_target="tpu_custom_call" | custom-call | flops 226492416 | bytes 1622016 | tf_op jit(solution)/shard_map/pallas_call | solution.py:440
  47.2 0.0 collective-permute-done.9.left
  47.3 0.0 collective-permute-done.10.right
  47.3 3.3 %shard_map.78.waves = f32[48,48,128]{2,1,0:T(8,128)S(1)} custom-call(f32[16,6144]{1,0:T(8,128)S(1)} %copy-done, f32[16,6144]{1,0:T(8,128)S(1)} %copy-done.1, bf16[16,6144]{1,0:T(8,128)(2,1)S(1)} %copy-done.3, bf16[16,11648]{1,0:T(8,128)(2,1)S(1)} %collective-permute-done.9.left, bf16[16,11648]{1,0:T(8,128)(2,1)S(1)} %collective-permute-done.10.right, ...), custom_call_target="tpu_custom_call" | custom-call | flops 44236800 | bytes 3080192 | tf_op jit(solution)/shard_map/pallas_call | solution.py:440
  50.6 0.0 collective-permute-done.13.rest_0_
  50.6 3.3 %collective-permute-done.14.rest_1_ = bf16[96,1664]{1,0:T(8,128)(2,1)S(1)} collective-permute-done((bf16[96,1664]{1,0:T(8,128)(2,1)S(1)}, bf16[96,1664]{1,0:T(8,128)(2,1)S(1)}, u32[]{:S(2)}, u32[]{:S(2)}) %collective-permute-start.14) | collective-permute-done | bytes 319520 | tf_op jit(solution)/shard_map/ppermute | solution.py:534
  53.9 2.2 %shard_map.80 = f32[16,6144]{1,0:T(8,128)} custom-call(bf16[96,384]{1,0:T(8,128)(2,1)S(1)} %copy-done.5, bf16[64,32]{1,0:T(8,128)(2,1)S(1)} %copy.8.depth_factor, f32[48,48,128]{2,1,0:T(8,128)S(1)} %shard_map.78.waves, f32[96,1536]{1,0:T(8,128)S(1)} %shard_map.79.earlier, bf16[96,1664]{1,0:T(8,128)(2,1)S(1)} %collective-permute-done.13.rest_0_, ...), custom_call_target="tpu_custom_call" | custom-call | flops 56623104 | bytes 2879488 | tf_op jit(solution)/shard_map/pallas_call | solution.py:440
  (9 shorter events, 0.0 us)
Async XLA Ops:
  0.0 13.4 %copy-start = (f32[16,6144]{1,0:T(8,128)S(1)}, f32[16,6144]{1,0:T(8,128)}, u32[]{:S(2)}) copy-start(f32[16,6144]{1,0:T(8,128)} %pressure.2) | copy-start | bytes 1179652
  0.0 13.4 %copy-start.1 = (f32[16,6144]{1,0:T(8,128)S(1)}, f32[16,6144]{1,0:T(8,128)}, u32[]{:S(2)}) copy-start(f32[16,6144]{1,0:T(8,128)} %previous.3) | copy-start | bytes 1179652
  0.0 8.4 %collective-permute-start = (bf16[3,48,3072]{2,1,0:T(8,128)(2,1)}, bf16[3,48,3072]{2,1,0:T(8,128)(2,1)S(1)}, u32[]{:S(2)}, u32[]{:S(2)}) collective-permute-start(bf16[3,48,3072]{2,1,0:T(8,128)(2,1)} %core.1), channel_id=1, source_target_pairs={{0,4},{4,0},{8,12},{12,8},{16,20},{20,16},{24,28},{28,24},{1,5},{5... | collective-permute-start | bytes 2654216 | tf_op jit(solution)/shard_map/ppermute | solution.py:468
  0.5 6.1 %collective-permute-start.1 = (bf16[16,384]{1,0:T(8,128)(2,1)}, bf16[16,384]{1,0:T(8,128)(2,1)S(1)}, u32[]{:S(2)}, u32[]{:S(2)}) collective-permute-start(bf16[16,384]{1,0:T(8,128)(2,1)} %factor.1), channel_id=1, source_target_pairs={{0,24},{4,28},{8,16},{12,20},{16,8},{20,12},{24,0},{28,4},{1,25},{... | collective-permute-start | bytes 36872 | tf_op jit(solution)/shard_map/ppermute | solution.py:467
  4.0 3.9 %collective-permute-start.2 = (bf16[16,384]{1,0:T(8,128)(2,1)}, bf16[16,384]{1,0:T(8,128)(2,1)S(1)}, u32[]{:S(2)}, u32[]{:S(2)}) collective-permute-start(bf16[16,384]{1,0:T(8,128)(2,1)} %factor.1), channel_id=1, source_target_pairs={{0,16},{4,20},{8,24},{12,28},{16,0},{20,4},{24,8},{28,12},{1,17},{... | collective-permute-start | bytes 36872 | tf_op jit(solution)/shard_map/ppermute | solution.py:467
  4.5 3.9 %collective-permute-start.3 = (bf16[16,384]{1,0:T(8,128)(2,1)}, bf16[16,384]{1,0:T(8,128)(2,1)S(1)}, u32[]{:S(2)}, u32[]{:S(2)}) collective-permute-start(bf16[16,384]{1,0:T(8,128)(2,1)} %factor.1), channel_id=1, source_target_pairs={{0,8},{4,12},{8,0},{12,4},{16,24},{20,28},{24,16},{28,20},{1,9},{5... | collective-permute-start | bytes 36872 | tf_op jit(solution)/shard_map/ppermute | solution.py:467
  4.6 1.2 %copy-start.2 = (bf16[3,48,3072]{2,1,0:T(8,128)(2,1)S(1)}, bf16[3,48,3072]{2,1,0:T(8,128)(2,1)}, u32[]{:S(2)}) copy-start(bf16[3,48,3072]{2,1,0:T(8,128)(2,1)} %core.1) | copy-start | bytes 2654212
  5.8 0.7 %copy-start.7 = (bf16[16,384]{1,0:T(8,128)(2,1)S(1)}, bf16[16,384]{1,0:T(8,128)(2,1)}, u32[]{:S(2)}) copy-start(bf16[16,384]{1,0:T(8,128)(2,1)} %factor.1) | copy-start | bytes 36868
  6.5 6.9 %copy-start.3 = (bf16[16,6144]{1,0:T(8,128)(2,1)S(1)}, bf16[16,6144]{1,0:T(8,128)(2,1)}, u32[]{:S(2)}) copy-start(bf16[16,6144]{1,0:T(8,128)(2,1)} %velocity.3) | copy-start | bytes 589828
  6.5 6.9 %copy-start.6 = (bf16[96,384]{1,0:T(8,128)(2,1)S(1)}, bf16[96,384]{1,0:T(8,128)(2,1)}, u32[]{:S(2)}) copy-start(bf16[96,384]{1,0:T(8,128)(2,1)} %second.1) | copy-start | bytes 221188
  9.8 14.9 %collective-permute-start.6 = (bf16[48,3200]{1,0:T(8,128)(2,1)S(1)}, bf16[48,3200]{1,0:T(8,128)(2,1)S(1)}, u32[]{:S(2)}, u32[]{:S(2)}) collective-permute-start(bf16[48,3200]{1,0:T(8,128)(2,1)S(1)} %get-tuple-element.39), channel_id=1, source_target_pairs={{0,8},{4,12},{8,0},{12,4},{16,24},{20,28},{24,16},{28,20},{1,9},{5... | collective-permute-start | bytes 921608 | tf_op jit(solution)/shard_map/ppermute | solution.py:487
  10.1 14.7 %collective-permute-start.7 = (bf16[48,3200]{1,0:T(8,128)(2,1)S(1)}, bf16[48,3200]{1,0:T(8,128)(2,1)S(1)}, u32[]{:S(2)}, u32[]{:S(2)}) collective-permute-start(bf16[48,3200]{1,0:T(8,128)(2,1)S(1)} %get-tuple-element.40), channel_id=1, source_target_pairs={{0,16},{4,20},{8,24},{12,28},{16,0},{20,4},{24,8},{28,12},{1,17},{... | collective-permute-start | bytes 921608 | tf_op jit(solution)/shard_map/ppermute | solution.py:487
  12.0 13.4 %collective-permute-start.8 = (bf16[48,3200]{1,0:T(8,128)(2,1)S(1)}, bf16[48,3200]{1,0:T(8,128)(2,1)S(1)}, u32[]{:S(2)}, u32[]{:S(2)}) collective-permute-start(bf16[48,3200]{1,0:T(8,128)(2,1)S(1)} %get-tuple-element.41), channel_id=1, source_target_pairs={{0,24},{4,28},{8,16},{12,20},{16,8},{20,12},{24,0},{28,4},{1,25},{... | collective-permute-start | bytes 921608 | tf_op jit(solution)/shard_map/ppermute | solution.py:487
  13.9 13.4 %copy-start.4 = (bf16[96,384]{1,0:T(8,128)(2,1)}, bf16[96,384]{1,0:T(8,128)(2,1)S(1)}, u32[]{:S(2)}) copy-start(bf16[96,384]{1,0:T(8,128)(2,1)S(1)} %get-tuple-element.32.second) | copy-start | bytes 221188
  13.9 5.6 %collective-permute-start.4 = (bf16[48,896]{1,0:T(8,128)(2,1)S(1)}, bf16[48,896]{1,0:T(8,128)(2,1)S(1)}, u32[]{:S(2)}, u32[]{:S(2)}) collective-permute-start(bf16[48,896]{1,0:T(8,128)(2,1)S(1)} %get-tuple-element.34), channel_id=1, source_target_pairs={{0,1},{1,2},{2,3},{4,5},{5,6},{6,7},{8,9},{9,10},{10,11},{12,13},{... | collective-permute-start | bytes 258056 | tf_op jit(solution)/shard_map/ppermute | solution.py:501
  17.4 6.4 %collective-permute-start.5 = (bf16[48,896]{1,0:T(8,128)(2,1)S(1)}, bf16[48,896]{1,0:T(8,128)(2,1)S(1)}, u32[]{:S(2)}, u32[]{:S(2)}) collective-permute-start(bf16[48,896]{1,0:T(8,128)(2,1)S(1)} %get-tuple-element.35), channel_id=1, source_target_pairs={{1,0},{2,1},{3,2},{5,4},{6,5},{7,6},{9,8},{10,9},{11,10},{13,12},{... | collective-permute-start | bytes 258056 | tf_op jit(solution)/shard_map/ppermute | solution.py:502
  23.8 20.8 %copy-start.8 = (bf16[64,32]{0,1:T(8,128)(2,1)S(1)}, bf16[64,32]{0,1:T(8,128)(2,1)}, u32[]{:S(2)}) copy-start(bf16[64,32]{0,1:T(8,128)(2,1)} %param.13) | copy-start | bytes 12292
  27.3 15.2 %collective-permute-start.11 = (bf16[96,1664]{1,0:T(8,128)(2,1)S(1)}, bf16[96,1664]{1,0:T(8,128)(2,1)S(1)}, u32[]{:S(2)}, u32[]{:S(2)}) collective-permute-start(bf16[96,1664]{1,0:T(8,128)(2,1)S(1)} %shard_map.77.rest_0_), channel_id=1, source_target_pairs={{0,2},{1,3},{2,0},{3,1},{4,6},{5,7},{6,4},{7,5},{8,10},{9,11},{10,... | collective-permute-start | bytes 958472 | tf_op jit(solution)/shard_map/ppermute | solution.py:526
  29.9 12.7 %collective-permute-start.12 = (bf16[96,1664]{1,0:T(8,128)(2,1)S(1)}, bf16[96,1664]{1,0:T(8,128)(2,1)S(1)}, u32[]{:S(2)}, u32[]{:S(2)}) collective-permute-start(bf16[96,1664]{1,0:T(8,128)(2,1)S(1)} %shard_map.77.rest_0_), channel_id=1, source_target_pairs={{0,1},{1,0},{2,3},{3,2},{4,5},{5,4},{6,7},{7,6},{8,9},{9,8},{10,11... | collective-permute-start | bytes 958472 | tf_op jit(solution)/shard_map/ppermute | solution.py:526
  31.5 15.7 %collective-permute-start.9 = (bf16[16,11648]{1,0:T(8,128)(2,1)}, bf16[16,11648]{1,0:T(8,128)(2,1)S(1)}, u32[]{:S(2)}, u32[]{:S(2)}) collective-permute-start(bf16[16,11648]{1,0:T(8,128)(2,1)} %get-tuple-element.44), channel_id=1, source_target_pairs={{0,4},{4,8},{8,12},{12,16},{16,20},{20,24},{24,28},{1,5},{5,9},{9,... | collective-permute-start | bytes 1118216 | tf_op jit(solution)/shard_map/ppermute | solution.py:541
  32.8 14.4 %collective-permute-start.10 = (bf16[16,11648]{1,0:T(8,128)(2,1)}, bf16[16,11648]{1,0:T(8,128)(2,1)S(1)}, u32[]{:S(2)}, u32[]{:S(2)}) collective-permute-start(bf16[16,11648]{1,0:T(8,128)(2,1)} %get-tuple-element.45), channel_id=1, source_target_pairs={{4,0},{8,4},{12,8},{16,12},{20,16},{24,20},{28,24},{5,1},{9,5},{13... | collective-permute-start | bytes 1118216 | tf_op jit(solution)/shard_map/ppermute | solution.py:542
  42.7 7.9 %collective-permute-start.13 = (bf16[96,1664]{1,0:T(8,128)(2,1)S(1)}, bf16[96,1664]{1,0:T(8,128)(2,1)S(1)}, u32[]{:S(2)}, u32[]{:S(2)}) collective-permute-start(bf16[96,1664]{1,0:T(8,128)(2,1)S(1)} %shard_map.77.rest_0_), channel_id=1, source_target_pairs={{1,2},{2,1},{5,6},{6,5},{9,10},{10,9},{13,14},{14,13},{17,18},{18,... | collective-permute-start | bytes 958472 | tf_op jit(solution)/shard_map/ppermute | solution.py:533
  43.3 10.6 %collective-permute-start.14 = (bf16[96,1664]{1,0:T(8,128)(2,1)S(1)}, bf16[96,1664]{1,0:T(8,128)(2,1)S(1)}, u32[]{:S(2)}, u32[]{:S(2)}) collective-permute-start(bf16[96,1664]{1,0:T(8,128)(2,1)S(1)} %collective-permute-done.11.rest_1_), channel_id=1, source_target_pairs={{1,0},{2,3},{5,4},{6,7},{9,8},{10,11},{13,12},{14,15},{17,16},{18,... | collective-permute-start | bytes 958472 | tf_op jit(solution)/shard_map/ppermute | solution.py:534
  44.7 0.9 %copy-start.5 = (bf16[96,384]{1,0:T(8,128)(2,1)S(1)}, bf16[96,384]{1,0:T(8,128)(2,1)}, u32[]{:S(2)}) copy-start(bf16[96,384]{1,0:T(8,128)(2,1)} %copy-done.4) | copy-start | bytes 221188

commit v7 on v6

--- a/solution.py
+++ b/solution.py
@@ -15,15 +15,21 @@
 VMEM_BYTES = 48 * 1024 * 1024
 
 
-def encode(values, axis=1):
-    peak = jnp.max(jnp.abs(values), axis=axis, keepdims=True)
-    scale = (jnp.maximum(peak, 1e-30) * (1.0 + 2.0**-7)).astype(BF16).astype(F32)
-    ratio = values * (TOP / scale)
+def scale_of(peak):
+    return (jnp.maximum(peak, 1e-30) * (1.0 + 2.0**-7)).astype(BF16).astype(F32)
+
+
+def raise_power(ratio):
     power = ratio * ratio
     power = power * power
     power = power * power
     power = power * power
-    return jnp.where(ratio < 0.0, -power, power).astype(BF16), scale
+    return jnp.where(ratio < 0.0, -power, power).astype(BF16)
+
+
+def encode(values):
+    scale = scale_of(jnp.max(jnp.abs(values), axis=(0, 1), keepdims=True))
+    return raise_power(values * (TOP / scale)), scale
 
 
 def decode(codes, unit):
@@ -35,15 +41,39 @@
     return jnp.where(codes < 0.0, -size, jnp.where(codes > 0.0, size, 0.0))
 
 
-def put_codes(ref, row, values, flat):
-    rows = values.shape[0]
-    codes, scale = encode(values)
-    ref[row : row + rows, :flat] = codes
-    ref[row : row + rows, flat : flat + LANES] = jnp.broadcast_to(scale, (rows, LANES)).astype(BF16)
+def stride_of(rows):
+    return (rows + 15) // 16 * 16
+
+
+def message(rows, flat):
+    return shape_of(flat // LANES * stride_of(rows) + 16, LANES, dtype=BF16)
+
+
+def put_message(ref, source):
+    rows, flat = source.shape
+    stride = stride_of(rows)
+    peak = jnp.max(jnp.abs(source[...]), axis=0, keepdims=True)
+    scale = scale_of(jnp.max(peak, axis=1, keepdims=True))
+    factor = TOP / scale
+    for tile in range(flat // LANES):
+        for start, count in pieces(rows):
+            into = tile * stride + start
+            ref[into : into + count, :] = raise_power(
+                source[start : start + count, tile * LANES : (tile + 1) * LANES] * factor
+            )
+    ref[flat // LANES * stride :, :] = jnp.broadcast_to(scale, (16, LANES)).astype(BF16)
+
+
+def unit_of(ref):
+    return ref[ref.shape[0] - 16 :, :].astype(F32)[:8] * (1.0 / TOP)
 
 
 def units(ref, row, rows, lane):
     return ref[row : row + rows, lane : lane + LANES].astype(F32) * (1.0 / TOP)
+
+
+def pieces(rows):
+    return [(start, 16) for start in range(0, rows, 16)] if rows % 16 == 0 else [(0, rows)]
 
 
 def split(values):
@@ -70,10 +100,6 @@
     first, second = exchange(first, second, depth, even)
     third, fourth = exchange(third, fourth, depth, even)
     return first, second, third, fourth
-
-
-def pieces(rows):
-    return [(start, 16) for start in range(0, rows, 16)] if rows % 16 == 0 else [(0, rows)]
 
 
 def project_kernel(chips, core, other, *rest):
@@ -101,8 +127,7 @@
                     distance * cells : (distance + 1) * cells
                 ]
     for distance in range(1, chips):
-        for start, count in pieces(lines):
-            put_codes(sends[distance - 1], start, partial[distance - 1, start : start + count, :], flat)
+        put_message(sends[distance - 1], partial.at[distance - 1])
 
 
 def gather_kernel(depth, steps, mine, *rest):
@@ -112,13 +137,14 @@
     quads = LANES // depth
     groups = flat // LANES
     pad = spread.shape[0] // lines
+    scales = [unit_of(ref) for ref in received]
     for start, count in pieces(lines):
-        scales = [units(ref, start, count, flat) for ref in received]
         for group in range(groups):
             lanes = slice(group * LANES, (group + 1) * LANES)
             value = mine[start : start + count, lanes]
             for ref, unit in zip(received, scales):
-                value = value + decode(ref[start : start + count, lanes], unit)
+                into = group * stride_of(lines) + start
+                value = value + decode(ref[into : into + count, :], unit[:1])
             for row in range(0, count, 8):
                 spread[pl.ds((start + row) * pad + group, 8, stride=pad), :] = value[row : row + 8]
     rest_x = cells // quads
@@ -131,12 +157,11 @@
             ]
             for j, tile in enumerate(swap_groups(tiles, depth)):
                 turned[j * groups + top : j * groups + top + count, line * LANES : (line + 1) * LANES] = tile[:count]
-    for start, count in pieces(turned.shape[0]):
-        put_codes(codes, start, turned[start : start + count, :], turned.shape[1])
+    put_message(codes, turned)
 
 
 def contract_second(depth, second, blocks, total, earlier, terms):
-    rows, flat = blocks[0][1].shape[0], total.shape[1]
+    rows, flat = terms.shape[1], total.shape[1]
     quads = LANES // depth
     ranks = second.shape[1]
     place = lax.axis_index("gy")
@@ -150,16 +175,15 @@
         owner = jnp.bitwise_xor(place, distance)
         chosen = jnp.where(offset == owner * rows, 1.0, 0.0).astype(BF16)
         columns.append(dot(second[...], chosen).astype(BF16))
-        for start, count in pieces(rows):
-            unit = units(options[0], start, count, flat)
-            if len(options) > 1:
-                unit = jnp.where(inner, unit, units(options[1], start, count, flat))
-            for low in range(0, flat, LANES):
-                codes = options[0][start : start + count, low : low + LANES].astype(F32)
+        unit = unit_of(options[0])[:1]
+        if len(options) > 1:
+            unit = jnp.where(inner, unit, unit_of(options[1])[:1])
+        for low in range(0, flat, LANES):
+            for start, count in pieces(rows):
+                into = low // LANES * stride_of(rows) + start
+                codes = options[0][into : into + count, :].astype(F32)
                 if len(options) > 1:
-                    codes = jnp.where(
-                        inner, codes, options[1][start : start + count, low : low + LANES].astype(F32)
-                    )
+                    codes = jnp.where(inner, codes, options[1][into : into + count, :].astype(F32))
                 high, rest_of = split(decode(codes, unit))
                 terms[2 * at, start : start + count, low : low + LANES] = high
                 terms[2 * at + 1, start : start + count, low : low + LANES] = rest_of
@@ -255,7 +279,7 @@
     cells, flat = pressure.shape
     span = up.shape[1] - LANES
     for row, part in ((0, pressure), (cells, previous)):
-        codes, scale = encode(part[...], (0, 1))
+        codes, scale = encode(part[...])
         own[row : row + cells, :flat] = codes
         own[row : row + cells, flat:] = jnp.broadcast_to(scale, (cells, LANES)).astype(BF16)
     own[2 * cells :, :flat] = velocity[...]
@@ -476,7 +500,7 @@
     )
     mine, *sends = call(
         functools.partial(project_kernel, chips),
-        [shape_of(lines, core_flat)] + [shape_of(lines, core_flat + LANES, dtype=BF16)] * (chips - 1),
+        [shape_of(lines, core_flat)] + [message(lines, core_flat)] * (chips - 1),
         [pltpu.VMEM((chips - 1, lines, core_flat), F32)],
         4 * lines * chips * rank * core_flat,
         core_near,
@@ -514,7 +538,7 @@
     mine, ahead, behind = lax.optimization_barrier((mine, ahead, behind))
     (codes,) = call(
         functools.partial(gather_kernel, depth, steps),
-        [shape_of(local_second, lines * depth + LANES, dtype=BF16)],
+        [message(local_second, lines * depth)],
         [pltpu.VMEM((lines * groups_pad, LANES), F32), pltpu.VMEM((local_second, lines * depth), F32)],
         30 * chips * lines * core_flat,
         mine,

time: 56.5 us -> 54.7 us (0.968)
  local copies, waits for them, and re-layouts: 2.88 us -> 1.99 us
  waiting for transfers between devices: 19.4 us -> 18.7 us
    unnamed x19 -> x15, local copies, waits for them, and re-layouts: 2.88 us -> 1.99 us
    ppermute x2, waiting for transfers between devices: 8.52 us -> 7.65 us  [far(): lax.ppermute(codes, 'gy', [(i, i ^ distance) for i in range(count_y)])]
  transfers between devices with their start and end apart: 15 -> 15, of which waited for: 8 -> 8; matrix products, arithmetic and copies ran while one was open for 0% -> 0% of each run, Pallas kernels for 11% -> 12%
where the time goes in v7:
time: 54.7 us; the launch traced here: 54.4 us
  starting transfers between devices  21.7 us (40%)
  waiting for transfers between devices  18.7 us (34%)
  Pallas kernels  11.9 us (22%)
  local copies, waits for them, and re-layouts  1.99 us (4%)
    pallas_call x8, Pallas kernels, call(): pl.pallas_call(kernel, out_shape=outs, scratch_shapes=scratch, cost_estim...  11.9 us
    ppermute x2, waiting for transfers between devices, far(): lax.ppermute(codes, 'gy', [(i, i ^ distance) for i in range(count_y)])  7.65 us
    ppermute x1, waiting for transfers between devices, body(): high = lax.ppermute(down, 'gy', [(i + 1, i) for i in range(count_y - 1)])  4.3 us
    ppermute x2, starting transfers between devices, far(): lax.ppermute(codes, 'gy', [(i, i ^ distance) for i in range(count_y)])  4.23 us
    ppermute x3, starting transfers between devices, body(): lax.ppermute(first_factor, 'gx', route)  4.17 us
    ppermute x1, waiting for transfers between devices, body(): lax.ppermute(blocks[1], 'gy', [(1, 0), (2, 3)])  3.83 us
    ppermute x3, starting transfers between devices, body(): lax.ppermute(send, 'gx', route)  3.55 us
    ppermute x1, starting transfers between devices, body(): low = lax.ppermute(up, 'gy', [(i, i + 1) for i in range(count_y - 1)])  3.49 us
  transfers between devices with their start and end apart: 15, of which 8 were waited for; matrix products, arithmetic and copies ran while one was open for 0% of the time, Pallas kernels for 12%

profile of v7, /device:TPU:0, one launch (start us, length us, event | category | flops | bytes accessed | tf_op | source)
XLA Modules:
  0.0 54.4 jit_solution(14242917893916484358)
XLA Ops:
  0.0 0.0 copy-start
  0.0 0.0 copy-start.1
  0.0 0.5 collective-permute-start
  0.5 3.5 %collective-permute-start.1 = (bf16[16,384]{1,0:T(8,128)(2,1)}, bf16[16,384]{1,0:T(8,128)(2,1)S(1)}, u32[]{:S(2)}, u32[]{:S(2)}) collective-permute-start(bf16[16,384]{1,0:T(8,128)(2,1)} %factor.1), channel_id=1, source_target_pairs={{0,24},{4,28},{8,16},{12,20},{16,8},{20,12},{24,0},{28,4},{1,25},{... | collective-permute-start | bytes 36872 | tf_op jit(solution)/shard_map/ppermute | solution.py:491
  4.0 0.5 collective-permute-start.2
  4.5 0.1 collective-permute-start.3
  4.6 1.2 %copy-done.2 = bf16[3,48,3072]{2,1,0:T(8,128)(2,1)S(1)} copy-done((bf16[3,48,3072]{2,1,0:T(8,128)(2,1)S(1)}, bf16[3,48,3072]{2,1,0:T(8,128)(2,1)}, u32[]{:S(2)}) %copy-start.2) | copy-done | bytes 884760
  5.8 0.7 %copy-done.5 = bf16[16,384]{1,0:T(8,128)(2,1)S(1)} copy-done((bf16[16,384]{1,0:T(8,128)(2,1)S(1)}, bf16[16,384]{1,0:T(8,128)(2,1)}, u32[]{:S(2)}) %copy-start.5) | copy-done | bytes 12312
  6.5 0.1 shard_map.73
  6.6 0.0 collective-permute-done.1.rest_0_
  6.6 1.3 %collective-permute-done.2.rest_1_ = bf16[16,384]{1,0:T(8,128)(2,1)S(1)} collective-permute-done((bf16[16,384]{1,0:T(8,128)(2,1)}, bf16[16,384]{1,0:T(8,128)(2,1)S(1)}, u32[]{:S(2)}, u32[]{:S(2)}) %collective-permute-start.2) | collective-permute-done | bytes 12320 | tf_op jit(solution)/shard_map/ppermute | solution.py:491
  7.9 0.5 collective-permute-done.3.rest_2_
  8.4 0.0 collective-permute-done.other
  8.4 1.5 %shard_map.74 = (f32[48,3072]{1,0:T(8,128)S(1)}, bf16[1168,128]{1,0:T(8,128)(2,1)S(1)}, bf16[1168,128]{1,0:T(8,128)(2,1)S(1)}, bf16[1168,128]{1,0:T(8,128)(2,1)S(1)}) custom-call(bf16[3,48,3072]{2,1,0:T(8,128)(2,1)S(1)} %get-tuple-element.28.core, bf16[3,48,3072]{2,1,0:T(8,128)(2,1)S(1)} %collective-permute-done.other, ...), custom_call_target="tpu_custom_call" | custom-call | flops 113246208 | bytes 3305472 | tf_op jit(solution)/shard_map/pallas_call | solution.py:464
  9.9 0.2 collective-permute-start.6
  10.1 1.9 %collective-permute-start.7 = (bf16[1168,128]{1,0:T(8,128)(2,1)S(1)}, bf16[1168,128]{1,0:T(8,128)(2,1)S(1)}, u32[]{:S(2)}, u32[]{:S(2)}) collective-permute-start(bf16[1168,128]{1,0:T(8,128)(2,1)S(1)} %get-tuple-element.40), channel_id=1, source_target_pairs={{0,16},{4,20},{8,24},{12,28},{16,0},{20,4},{24,8},{28,12},{1,17},{... | collective-permute-start | bytes 897032 | tf_op jit(solution)/shard_map/ppermute | solution.py:511
  12.0 1.4 %collective-permute-start.8 = (bf16[1168,128]{1,0:T(8,128)(2,1)S(1)}, bf16[1168,128]{1,0:T(8,128)(2,1)S(1)}, u32[]{:S(2)}, u32[]{:S(2)}) collective-permute-start(bf16[1168,128]{1,0:T(8,128)(2,1)S(1)} %get-tuple-element.41), channel_id=1, source_target_pairs={{0,24},{4,28},{8,16},{12,20},{16,8},{20,12},{24,0},{28,4},{1,25},{... | collective-permute-start | bytes 897032 | tf_op jit(solution)/shard_map/ppermute | solution.py:511
  13.5 0.0 copy-done
  13.5 0.0 copy-done.1
  13.5 0.0 copy-done.3
  13.5 0.0 copy-done.4
  13.5 0.5 shard_map.75
  14.0 3.5 %collective-permute-start.4 = (bf16[48,896]{1,0:T(8,128)(2,1)S(1)}, bf16[48,896]{1,0:T(8,128)(2,1)S(1)}, u32[]{:S(2)}, u32[]{:S(2)}) collective-permute-start(bf16[48,896]{1,0:T(8,128)(2,1)S(1)} %get-tuple-element.34), channel_id=1, source_target_pairs={{0,1},{1,2},{2,3},{4,5},{5,6},{6,7},{8,9},{9,10},{10,11},{12,13},{... | collective-permute-start | bytes 258056 | tf_op jit(solution)/shard_map/ppermute | solution.py:525
  17.5 1.3 %collective-permute-start.5 = (bf16[48,896]{1,0:T(8,128)(2,1)S(1)}, bf16[48,896]{1,0:T(8,128)(2,1)S(1)}, u32[]{:S(2)}, u32[]{:S(2)}) collective-permute-start(bf16[48,896]{1,0:T(8,128)(2,1)S(1)} %get-tuple-element.35), channel_id=1, source_target_pairs={{1,0},{2,1},{3,2},{5,4},{6,5},{7,6},{9,8},{10,9},{11,10},{13,12},{... | collective-permute-start | bytes 258056 | tf_op jit(solution)/shard_map/ppermute | solution.py:526
  18.8 0.8 %collective-permute-done.4.low = bf16[48,896]{1,0:T(8,128)(2,1)S(1)} collective-permute-done((bf16[48,896]{1,0:T(8,128)(2,1)S(1)}, bf16[48,896]{1,0:T(8,128)(2,1)S(1)}, u32[]{:S(2)}, u32[]{:S(2)}) %collective-permute-start.4) | collective-permute-done | bytes 86048 | tf_op jit(solution)/shard_map/ppermute | solution.py:525
  19.6 4.3 %collective-permute-done.5.high = bf16[48,896]{1,0:T(8,128)(2,1)S(1)} collective-permute-done((bf16[48,896]{1,0:T(8,128)(2,1)S(1)}, bf16[48,896]{1,0:T(8,128)(2,1)S(1)}, u32[]{:S(2)}, u32[]{:S(2)}) %collective-permute-start.5) | collective-permute-done | bytes 86048 | tf_op jit(solution)/shard_map/ppermute | solution.py:526
  23.9 0.9 %shard_map.76 = (bf16[16,11648]{1,0:T(8,128)(2,1)}, bf16[16,11648]{1,0:T(8,128)(2,1)}) custom-call(bf16[48,6272]{1,0:T(8,128)(2,1)S(1)} %get-tuple-element.33.own, bf16[48,896]{1,0:T(8,128)(2,1)S(1)} %collective-permute-done.4.low, bf16[48,896]{1,0:T(8,128)(2,1)S(1)} %collective-permute-done.5.high), custom_call_target="tpu_custom_call" | custom-call | flops 1000 | bytes 1519616 | tf_op jit(solution)/shard_map/pallas_call | solution.py:464
  24.8 0.0 collective-permute-done.6.rest_0_
  24.8 0.0 collective-permute-done.7.rest_1_
  24.8 0.3 collective-permute-done.8.rest_2_
  25.1 1.8 %shard_map.77.rest_0_ = bf16[1168,128]{1,0:T(8,128)(2,1)S(1)} custom-call(f32[48,3072]{1,0:T(8,128)S(1)} %get-tuple-element.38.mine, bf16[1168,128]{1,0:T(8,128)(2,1)S(1)} %collective-permute-done.6.rest_0_, bf16[1168,128]{1,0:T(8,128)(2,1)S(1)} %collective-permute-done.7.rest_1_, bf16[1168,128]{1,0:T(8,128)(2,1)S(1)} %collective-permute-done.8.rest_2_), custom_call_target="tpu_custom_call" | custom-call | flops 17694720 | bytes 1785856 | tf_op jit(solution)/shard_map/pallas_call | solution.py:464
  26.9 2.7 %collective-permute-start.11 = (bf16[1168,128]{1,0:T(8,128)(2,1)S(1)}, bf16[1168,128]{1,0:T(8,128)(2,1)S(1)}, u32[]{:S(2)}, u32[]{:S(2)}) collective-permute-start(bf16[1168,128]{1,0:T(8,128)(2,1)S(1)} %shard_map.77.rest_0_), channel_id=1, source_target_pairs={{0,2},{1,3},{2,0},{3,1},{4,6},{5,7},{6,4},{7,5},{8,10},{9,11},{10,... | collective-permute-start | bytes 897032 | tf_op jit(solution)/shard_map/ppermute | solution.py:550
  29.6 1.6 %collective-permute-start.12 = (bf16[1168,128]{1,0:T(8,128)(2,1)S(1)}, bf16[1168,128]{1,0:T(8,128)(2,1)S(1)}, u32[]{:S(2)}, u32[]{:S(2)}) collective-permute-start(bf16[1168,128]{1,0:T(8,128)(2,1)S(1)} %shard_map.77.rest_0_), channel_id=1, source_target_pairs={{0,1},{1,0},{2,3},{3,2},{4,5},{5,4},{6,7},{7,6},{8,9},{9,8},{10,11... | collective-permute-start | bytes 897032 | tf_op jit(solution)/shard_map/ppermute | solution.py:550
  31.2 1.3 %collective-permute-start.9 = (bf16[16,11648]{1,0:T(8,128)(2,1)}, bf16[16,11648]{1,0:T(8,128)(2,1)S(1)}, u32[]{:S(2)}, u32[]{:S(2)}) collective-permute-start(bf16[16,11648]{1,0:T(8,128)(2,1)} %get-tuple-element.44), channel_id=1, source_target_pairs={{0,4},{4,8},{8,12},{12,16},{16,20},{20,24},{24,28},{1,5},{5,9},{9,... | collective-permute-start | bytes 1118216 | tf_op jit(solution)/shard_map/ppermute | solution.py:565
  32.5 1.3 %collective-permute-start.10 = (bf16[16,11648]{1,0:T(8,128)(2,1)}, bf16[16,11648]{1,0:T(8,128)(2,1)S(1)}, u32[]{:S(2)}, u32[]{:S(2)}) collective-permute-start(bf16[16,11648]{1,0:T(8,128)(2,1)} %get-tuple-element.45), channel_id=1, source_target_pairs={{4,0},{8,4},{12,8},{16,12},{20,16},{24,20},{28,24},{5,1},{9,5},{13... | collective-permute-start | bytes 1118216 | tf_op jit(solution)/shard_map/ppermute | solution.py:566
  33.8 7.4 %collective-permute-done.11.rest_1_ = bf16[1168,128]{1,0:T(8,128)(2,1)S(1)} collective-permute-done((bf16[1168,128]{1,0:T(8,128)(2,1)S(1)}, bf16[1168,128]{1,0:T(8,128)(2,1)S(1)}, u32[]{:S(2)}, u32[]{:S(2)}) %collective-permute-start.11) | collective-permute-done | bytes 299040 | tf_op jit(solution)/shard_map/ppermute | solution.py:550
  41.2 0.2 collective-permute-done.12.rest_2_
  41.4 0.7 %collective-permute-start.13 = (bf16[1168,128]{1,0:T(8,128)(2,1)S(1)}, bf16[1168,128]{1,0:T(8,128)(2,1)S(1)}, u32[]{:S(2)}, u32[]{:S(2)}) collective-permute-start(bf16[1168,128]{1,0:T(8,128)(2,1)S(1)} %shard_map.77.rest_0_), channel_id=1, source_target_pairs={{1,2},{2,1},{5,6},{6,5},{9,10},{10,9},{13,14},{14,13},{17,18},{18,... | collective-permute-start | bytes 897032 | tf_op jit(solution)/shard_map/ppermute | solution.py:557
  42.1 1.3 %collective-permute-start.14 = (bf16[1168,128]{1,0:T(8,128)(2,1)S(1)}, bf16[1168,128]{1,0:T(8,128)(2,1)S(1)}, u32[]{:S(2)}, u32[]{:S(2)}) collective-permute-start(bf16[1168,128]{1,0:T(8,128)(2,1)S(1)} %collective-permute-done.11.rest_1_), channel_id=1, source_target_pairs={{1,0},{2,3},{5,4},{6,7},{9,8},{10,11},{13,12},{14,15},{17,16},{18,... | collective-permute-start | bytes 897032 | tf_op jit(solution)/shard_map/ppermute | solution.py:558
  43.4 0.0 copy-done.6
  43.4 0.1 copy.8.depth_factor
  43.5 1.6 %shard_map.79.earlier = f32[96,1536]{1,0:T(8,128)S(1)} custom-call(bf16[96,384]{1,0:T(8,128)(2,1)S(1)} %get-tuple-element.32.second, bf16[1168,128]{1,0:T(8,128)(2,1)S(1)} %shard_map.77.rest_0_, bf16[1168,128]{1,0:T(8,128)(2,1)S(1)} %collective-permute-done.11.rest_1_, bf16[1168,128]{1,0:T(8,128)(2,1)S(1)} %collective-permute-done.12.rest_2_), custom_call_target="tpu_custom_call" | custom-call | flops 226492416 | bytes 1560576 | tf_op jit(solution)/shard_map/pallas_call | solution.py:464
  45.1 0.0 collective-permute-done.9.left
  45.1 0.0 collective-permute-done.10.right
  45.1 3.3 %shard_map.78.waves = f32[48,48,128]{2,1,0:T(8,128)S(1)} custom-call(f32[16,6144]{1,0:T(8,128)S(1)} %copy-done, f32[16,6144]{1,0:T(8,128)S(1)} %copy-done.1, bf16[16,6144]{1,0:T(8,128)(2,1)S(1)} %copy-done.3, bf16[16,11648]{1,0:T(8,128)(2,1)S(1)} %collective-permute-done.9.left, bf16[16,11648]{1,0:T(8,128)(2,1)S(1)} %collective-permute-done.10.right, ...), custom_call_target="tpu_custom_call" | custom-call | flops 44236800 | bytes 3080192 | tf_op jit(solution)/shard_map/pallas_call | solution.py:464
  48.4 0.0 collective-permute-done.13.rest_0_
  48.4 3.8 %collective-permute-done.14.rest_1_ = bf16[1168,128]{1,0:T(8,128)(2,1)S(1)} collective-permute-done((bf16[1168,128]{1,0:T(8,128)(2,1)S(1)}, bf16[1168,128]{1,0:T(8,128)(2,1)S(1)}, u32[]{:S(2)}, u32[]{:S(2)}) %collective-permute-start.14) | collective-permute-done | bytes 299040 | tf_op jit(solution)/shard_map/ppermute | solution.py:558
  52.2 2.2 %shard_map.80 = f32[16,6144]{1,0:T(8,128)} custom-call(bf16[96,384]{1,0:T(8,128)(2,1)S(1)} %get-tuple-element.32.second, bf16[64,32]{1,0:T(8,128)(2,1)S(1)} %copy.8.depth_factor, f32[48,48,128]{2,1,0:T(8,128)S(1)} %shard_map.78.waves, f32[96,1536]{1,0:T(8,128)S(1)} %shard_map.79.earlier, bf16[1168,128]{1,0:T(8,128)(2,1)S(1)} %collective-permute-done.13.rest_0_, ...), custom_call_target="tpu_custom_call" | custom-call | flops 56623104 | bytes 2838528 | tf_op jit(solution)/shard_map/pallas_call | solution.py:464
  (5 shorter events, 0.0 us)
Async XLA Ops:
  0.0 13.5 %copy-start = (f32[16,6144]{1,0:T(8,128)S(1)}, f32[16,6144]{1,0:T(8,128)}, u32[]{:S(2)}) copy-start(f32[16,6144]{1,0:T(8,128)} %pressure.2) | copy-start | bytes 1179652
  0.0 13.5 %copy-start.1 = (f32[16,6144]{1,0:T(8,128)S(1)}, f32[16,6144]{1,0:T(8,128)}, u32[]{:S(2)}) copy-start(f32[16,6144]{1,0:T(8,128)} %previous.3) | copy-start | bytes 1179652
  0.0 8.4 %collective-permute-start = (bf16[3,48,3072]{2,1,0:T(8,128)(2,1)}, bf16[3,48,3072]{2,1,0:T(8,128)(2,1)S(1)}, u32[]{:S(2)}, u32[]{:S(2)}) collective-permute-start(bf16[3,48,3072]{2,1,0:T(8,128)(2,1)} %core.1), channel_id=1, source_target_pairs={{0,4},{4,0},{8,12},{12,8},{16,20},{20,16},{24,28},{28,24},{1,5},{5... | collective-permute-start | bytes 2654216 | tf_op jit(solution)/shard_map/ppermute | solution.py:492
  0.5 6.1 %collective-permute-start.1 = (bf16[16,384]{1,0:T(8,128)(2,1)}, bf16[16,384]{1,0:T(8,128)(2,1)S(1)}, u32[]{:S(2)}, u32[]{:S(2)}) collective-permute-start(bf16[16,384]{1,0:T(8,128)(2,1)} %factor.1), channel_id=1, source_target_pairs={{0,24},{4,28},{8,16},{12,20},{16,8},{20,12},{24,0},{28,4},{1,25},{... | collective-permute-start | bytes 36872 | tf_op jit(solution)/shard_map/ppermute | solution.py:491
  4.0 3.9 %collective-permute-start.2 = (bf16[16,384]{1,0:T(8,128)(2,1)}, bf16[16,384]{1,0:T(8,128)(2,1)S(1)}, u32[]{:S(2)}, u32[]{:S(2)}) collective-permute-start(bf16[16,384]{1,0:T(8,128)(2,1)} %factor.1), channel_id=1, source_target_pairs={{0,16},{4,20},{8,24},{12,28},{16,0},{20,4},{24,8},{28,12},{1,17},{... | collective-permute-start | bytes 36872 | tf_op jit(solution)/shard_map/ppermute | solution.py:491
  4.5 3.9 %collective-permute-start.3 = (bf16[16,384]{1,0:T(8,128)(2,1)}, bf16[16,384]{1,0:T(8,128)(2,1)S(1)}, u32[]{:S(2)}, u32[]{:S(2)}) collective-permute-start(bf16[16,384]{1,0:T(8,128)(2,1)} %factor.1), channel_id=1, source_target_pairs={{0,8},{4,12},{8,0},{12,4},{16,24},{20,28},{24,16},{28,20},{1,9},{5... | collective-permute-start | bytes 36872 | tf_op jit(solution)/shard_map/ppermute | solution.py:491
  4.6 1.2 %copy-start.2 = (bf16[3,48,3072]{2,1,0:T(8,128)(2,1)S(1)}, bf16[3,48,3072]{2,1,0:T(8,128)(2,1)}, u32[]{:S(2)}) copy-start(bf16[3,48,3072]{2,1,0:T(8,128)(2,1)} %core.1) | copy-start | bytes 2654212
  5.8 0.7 %copy-start.5 = (bf16[16,384]{1,0:T(8,128)(2,1)S(1)}, bf16[16,384]{1,0:T(8,128)(2,1)}, u32[]{:S(2)}) copy-start(bf16[16,384]{1,0:T(8,128)(2,1)} %factor.1) | copy-start | bytes 36868
  6.5 7.0 %copy-start.3 = (bf16[16,6144]{1,0:T(8,128)(2,1)S(1)}, bf16[16,6144]{1,0:T(8,128)(2,1)}, u32[]{:S(2)}) copy-start(bf16[16,6144]{1,0:T(8,128)(2,1)} %velocity.3) | copy-start | bytes 589828
  6.5 7.0 %copy-start.4 = (bf16[96,384]{1,0:T(8,128)(2,1)S(1)}, bf16[96,384]{1,0:T(8,128)(2,1)}, u32[]{:S(2)}) copy-start(bf16[96,384]{1,0:T(8,128)(2,1)} %second.1) | copy-start | bytes 221188
  9.9 14.9 %collective-permute-start.6 = (bf16[1168,128]{1,0:T(8,128)(2,1)S(1)}, bf16[1168,128]{1,0:T(8,128)(2,1)S(1)}, u32[]{:S(2)}, u32[]{:S(2)}) collective-permute-start(bf16[1168,128]{1,0:T(8,128)(2,1)S(1)} %get-tuple-element.39), channel_id=1, source_target_pairs={{0,8},{4,12},{8,0},{12,4},{16,24},{20,28},{24,16},{28,20},{1,9},{5... | collective-permute-start | bytes 897032 | tf_op jit(solution)/shard_map/ppermute | solution.py:511
  10.1 14.7 %collective-permute-start.7 = (bf16[1168,128]{1,0:T(8,128)(2,1)S(1)}, bf16[1168,128]{1,0:T(8,128)(2,1)S(1)}, u32[]{:S(2)}, u32[]{:S(2)}) collective-permute-start(bf16[1168,128]{1,0:T(8,128)(2,1)S(1)} %get-tuple-element.40), channel_id=1, source_target_pairs={{0,16},{4,20},{8,24},{12,28},{16,0},{20,4},{24,8},{28,12},{1,17},{... | collective-permute-start | bytes 897032 | tf_op jit(solution)/shard_map/ppermute | solution.py:511
  12.0 13.0 %collective-permute-start.8 = (bf16[1168,128]{1,0:T(8,128)(2,1)S(1)}, bf16[1168,128]{1,0:T(8,128)(2,1)S(1)}, u32[]{:S(2)}, u32[]{:S(2)}) collective-permute-start(bf16[1168,128]{1,0:T(8,128)(2,1)S(1)} %get-tuple-element.41), channel_id=1, source_target_pairs={{0,24},{4,28},{8,16},{12,20},{16,8},{20,12},{24,0},{28,4},{1,25},{... | collective-permute-start | bytes 897032 | tf_op jit(solution)/shard_map/ppermute | solution.py:511
  14.0 5.6 %collective-permute-start.4 = (bf16[48,896]{1,0:T(8,128)(2,1)S(1)}, bf16[48,896]{1,0:T(8,128)(2,1)S(1)}, u32[]{:S(2)}, u32[]{:S(2)}) collective-permute-start(bf16[48,896]{1,0:T(8,128)(2,1)S(1)} %get-tuple-element.34), channel_id=1, source_target_pairs={{0,1},{1,2},{2,3},{4,5},{5,6},{6,7},{8,9},{9,10},{10,11},{12,13},{... | collective-permute-start | bytes 258056 | tf_op jit(solution)/shard_map/ppermute | solution.py:525
  17.5 6.4 %collective-permute-start.5 = (bf16[48,896]{1,0:T(8,128)(2,1)S(1)}, bf16[48,896]{1,0:T(8,128)(2,1)S(1)}, u32[]{:S(2)}, u32[]{:S(2)}) collective-permute-start(bf16[48,896]{1,0:T(8,128)(2,1)S(1)} %get-tuple-element.35), channel_id=1, source_target_pairs={{1,0},{2,1},{3,2},{5,4},{6,5},{7,6},{9,8},{10,9},{11,10},{13,12},{... | collective-permute-start | bytes 258056 | tf_op jit(solution)/shard_map/ppermute | solution.py:526
  23.9 19.5 %copy-start.6 = (bf16[64,32]{0,1:T(8,128)(2,1)S(1)}, bf16[64,32]{0,1:T(8,128)(2,1)}, u32[]{:S(2)}) copy-start(bf16[64,32]{0,1:T(8,128)(2,1)} %param.13) | copy-start | bytes 12292
  26.9 14.3 %collective-permute-start.11 = (bf16[1168,128]{1,0:T(8,128)(2,1)S(1)}, bf16[1168,128]{1,0:T(8,128)(2,1)S(1)}, u32[]{:S(2)}, u32[]{:S(2)}) collective-permute-start(bf16[1168,128]{1,0:T(8,128)(2,1)S(1)} %shard_map.77.rest_0_), channel_id=1, source_target_pairs={{0,2},{1,3},{2,0},{3,1},{4,6},{5,7},{6,4},{7,5},{8,10},{9,11},{10,... | collective-permute-start | bytes 897032 | tf_op jit(solution)/shard_map/ppermute | solution.py:550
  29.6 11.8 %collective-permute-start.12 = (bf16[1168,128]{1,0:T(8,128)(2,1)S(1)}, bf16[1168,128]{1,0:T(8,128)(2,1)S(1)}, u32[]{:S(2)}, u32[]{:S(2)}) collective-permute-start(bf16[1168,128]{1,0:T(8,128)(2,1)S(1)} %shard_map.77.rest_0_), channel_id=1, source_target_pairs={{0,1},{1,0},{2,3},{3,2},{4,5},{5,4},{6,7},{7,6},{8,9},{9,8},{10,11... | collective-permute-start | bytes 897032 | tf_op jit(solution)/shard_map/ppermute | solution.py:550
  31.2 13.9 %collective-permute-start.9 = (bf16[16,11648]{1,0:T(8,128)(2,1)}, bf16[16,11648]{1,0:T(8,128)(2,1)S(1)}, u32[]{:S(2)}, u32[]{:S(2)}) collective-permute-start(bf16[16,11648]{1,0:T(8,128)(2,1)} %get-tuple-element.44), channel_id=1, source_target_pairs={{0,4},{4,8},{8,12},{12,16},{16,20},{20,24},{24,28},{1,5},{5,9},{9,... | collective-permute-start | bytes 1118216 | tf_op jit(solution)/shard_map/ppermute | solution.py:565
  32.5 12.7 %collective-permute-start.10 = (bf16[16,11648]{1,0:T(8,128)(2,1)}, bf16[16,11648]{1,0:T(8,128)(2,1)S(1)}, u32[]{:S(2)}, u32[]{:S(2)}) collective-permute-start(bf16[16,11648]{1,0:T(8,128)(2,1)} %get-tuple-element.45), channel_id=1, source_target_pairs={{4,0},{8,4},{12,8},{16,12},{20,16},{24,20},{28,24},{5,1},{9,5},{13... | collective-permute-start | bytes 1118216 | tf_op jit(solution)/shard_map/ppermute | solution.py:566
  41.4 7.0 %collective-permute-start.13 = (bf16[1168,128]{1,0:T(8,128)(2,1)S(1)}, bf16[1168,128]{1,0:T(8,128)(2,1)S(1)}, u32[]{:S(2)}, u32[]{:S(2)}) collective-permute-start(bf16[1168,128]{1,0:T(8,128)(2,1)S(1)} %shard_map.77.rest_0_), channel_id=1, source_target_pairs={{1,2},{2,1},{5,6},{6,5},{9,10},{10,9},{13,14},{14,13},{17,18},{18,... | collective-permute-start | bytes 897032 | tf_op jit(solution)/shard_map/ppermute | solution.py:557
  42.1 10.2 %collective-permute-start.14 = (bf16[1168,128]{1,0:T(8,128)(2,1)S(1)}, bf16[1168,128]{1,0:T(8,128)(2,1)S(1)}, u32[]{:S(2)}, u32[]{:S(2)}) collective-permute-start(bf16[1168,128]{1,0:T(8,128)(2,1)S(1)} %collective-permute-done.11.rest_1_), channel_id=1, source_target_pairs={{1,0},{2,3},{5,4},{6,7},{9,8},{10,11},{13,12},{14,15},{17,16},{18,... | collective-permute-start | bytes 897032 | tf_op jit(solution)/shard_map/ppermute | solution.py:558

commit v8 on v7

--- a/solution.py
+++ b/solution.py
@@ -552,11 +552,9 @@
     if count_y == 4:
         distances = (0, 2, 1)
         blocks = [codes, far(2), far(1)]
-        codes_later, blocks = lax.optimization_barrier((codes, blocks))
-        last = [
-            lax.ppermute(codes_later, "gy", [(1, 2), (2, 1)]),
-            lax.ppermute(blocks[1], "gy", [(1, 0), (2, 3)]),
-        ]
+        place = lax.axis_index("gy")
+        passed = jnp.where((place == 1) | (place == 2), blocks[1], blocks[2])
+        last = [lax.ppermute(passed, "gy", [(0, 2), (3, 1), (1, 0), (2, 3)])]
     else:
         distances = tuple(range(count_y - 1))
         blocks = [codes] + [far(distance) for distance in distances[1:]]

time: 54.7 us -> 51.9 us (0.949)
  waiting for transfers between devices: 18.7 us -> 14.4 us
  starting transfers between devices: 21.7 us -> 22.9 us
    ppermute x2 -> x1, waiting for transfers between devices: 3.83 us -> 1.32 us  [body(): last = [lax.ppermute(passed, 'gy', [(0, 2), (3, 1), (1, 0), (2, 3)])]]
    ppermute x1, starting transfers between devices: 1.3 us -> 3.05 us  [body(): left = lax.ppermute(ahead, 'gx', [(i, i + 1) for i in range(count_x - 1)])]
    ppermute x2, waiting for transfers between devices: 7.65 us -> 5.91 us  [far(): lax.ppermute(codes, 'gy', [(i, i ^ distance) for i in range(count_y)])]
    ppermute x2 -> x1, starting transfers between devices: 1.96 us -> 1.37 us  [body(): last = [lax.ppermute(passed, 'gy', [(0, 2), (3, 1), (1, 0), (2, 3)])]]
  transfers between devices with their start and end apart: 15 -> 14, of which waited for: 8 -> 8; matrix products, arithmetic and copies ran while one was open for 0% -> 0% of each run, Pallas kernels for 12% -> 12%
where the time goes in v8:
time: 51.9 us; the launch traced here: 51.3 us
  starting transfers between devices  22.9 us (44%)
  waiting for transfers between devices  14.4 us (28%)
  Pallas kernels  11.9 us (23%)
  local copies, waits for them, and re-layouts  1.99 us (4%)
    pallas_call x8, Pallas kernels, call(): pl.pallas_call(kernel, out_shape=outs, scratch_shapes=scratch, cost_estim...  11.9 us
    ppermute x2, waiting for transfers between devices, far(): lax.ppermute(codes, 'gy', [(i, i ^ distance) for i in range(count_y)])  5.91 us
    ppermute x1, waiting for transfers between devices, body(): high = lax.ppermute(down, 'gy', [(i + 1, i) for i in range(count_y - 1)])  4.3 us
    ppermute x2, starting transfers between devices, far(): lax.ppermute(codes, 'gy', [(i, i ^ distance) for i in range(count_y)])  4.23 us
    ppermute x3, starting transfers between devices, body(): lax.ppermute(first_factor, 'gx', route)  4.17 us
    ppermute x3, starting transfers between devices, body(): lax.ppermute(send, 'gx', route)  3.55 us
    ppermute x1, starting transfers between devices, body(): low = lax.ppermute(up, 'gy', [(i, i + 1) for i in range(count_y - 1)])  3.49 us
    ppermute x1, starting transfers between devices, body(): left = lax.ppermute(ahead, 'gx', [(i, i + 1) for i in range(count_x - 1)])  3.05 us
  transfers between devices with their start and end apart: 14, of which 8 were waited for; matrix products, arithmetic and copies ran while one was open for 0% of the time, Pallas kernels for 12%

profile of v8, /device:TPU:0, one launch (start us, length us, event | category | flops | bytes accessed | tf_op | source)
XLA Modules:
  0.0 51.3 jit_solution(11647712669667384541)
XLA Ops:
  0.0 0.0 copy-start
  0.0 0.0 copy-start.1
  0.0 0.5 collective-permute-start
  0.5 3.5 %collective-permute-start.1 = (bf16[16,384]{1,0:T(8,128)(2,1)}, bf16[16,384]{1,0:T(8,128)(2,1)S(1)}, u32[]{:S(2)}, u32[]{:S(2)}) collective-permute-start(bf16[16,384]{1,0:T(8,128)(2,1)} %factor.1), channel_id=1, source_target_pairs={{0,24},{4,28},{8,16},{12,20},{16,8},{20,12},{24,0},{28,4},{1,25},{... | collective-permute-start | bytes 36872 | tf_op jit(solution)/shard_map/ppermute | solution.py:491
  4.0 0.5 collective-permute-start.2
  4.5 0.1 collective-permute-start.3
  4.6 0.0 copy-start.2
  4.6 1.2 %copy-done.2 = bf16[3,48,3072]{2,1,0:T(8,128)(2,1)S(1)} copy-done((bf16[3,48,3072]{2,1,0:T(8,128)(2,1)S(1)}, bf16[3,48,3072]{2,1,0:T(8,128)(2,1)}, u32[]{:S(2)}) %copy-start.2) | copy-done | bytes 884760
  5.8 0.0 copy-start.5
  5.8 0.7 %copy-done.5 = bf16[16,384]{1,0:T(8,128)(2,1)S(1)} copy-done((bf16[16,384]{1,0:T(8,128)(2,1)S(1)}, bf16[16,384]{1,0:T(8,128)(2,1)}, u32[]{:S(2)}) %copy-start.5) | copy-done | bytes 12312
  6.5 0.1 shard_map.73
  6.6 0.0 collective-permute-done.1.rest_0_
  6.6 1.3 %collective-permute-done.2.rest_1_ = bf16[16,384]{1,0:T(8,128)(2,1)S(1)} collective-permute-done((bf16[16,384]{1,0:T(8,128)(2,1)}, bf16[16,384]{1,0:T(8,128)(2,1)S(1)}, u32[]{:S(2)}, u32[]{:S(2)}) %collective-permute-start.2) | collective-permute-done | bytes 12320 | tf_op jit(solution)/shard_map/ppermute | solution.py:491
  7.9 0.5 collective-permute-done.3.rest_2_
  8.4 0.0 collective-permute-done.other
  8.4 1.5 %shard_map.74 = (f32[48,3072]{1,0:T(8,128)S(1)}, bf16[1168,128]{1,0:T(8,128)(2,1)S(1)}, bf16[1168,128]{1,0:T(8,128)(2,1)S(1)}, bf16[1168,128]{1,0:T(8,128)(2,1)S(1)}) custom-call(bf16[3,48,3072]{2,1,0:T(8,128)(2,1)S(1)} %get-tuple-element.24.core, bf16[3,48,3072]{2,1,0:T(8,128)(2,1)S(1)} %collective-permute-done.other, ...), custom_call_target="tpu_custom_call" | custom-call | flops 113246208 | bytes 3305472 | tf_op jit(solution)/shard_map/pallas_call | solution.py:464
  9.9 0.2 collective-permute-start.6
  10.1 1.9 %collective-permute-start.7 = (bf16[1168,128]{1,0:T(8,128)(2,1)S(1)}, bf16[1168,128]{1,0:T(8,128)(2,1)S(1)}, u32[]{:S(2)}, u32[]{:S(2)}) collective-permute-start(bf16[1168,128]{1,0:T(8,128)(2,1)S(1)} %get-tuple-element.36), channel_id=1, source_target_pairs={{0,16},{4,20},{8,24},{12,28},{16,0},{20,4},{24,8},{28,12},{1,17},{... | collective-permute-start | bytes 897032 | tf_op jit(solution)/shard_map/ppermute | solution.py:511
  12.0 1.4 %collective-permute-start.8 = (bf16[1168,128]{1,0:T(8,128)(2,1)S(1)}, bf16[1168,128]{1,0:T(8,128)(2,1)S(1)}, u32[]{:S(2)}, u32[]{:S(2)}) collective-permute-start(bf16[1168,128]{1,0:T(8,128)(2,1)S(1)} %get-tuple-element.37), channel_id=1, source_target_pairs={{0,24},{4,28},{8,16},{12,20},{16,8},{20,12},{24,0},{28,4},{1,25},{... | collective-permute-start | bytes 897032 | tf_op jit(solution)/shard_map/ppermute | solution.py:511
  13.5 0.0 copy-done
  13.5 0.0 copy-done.1
  13.5 0.0 copy-done.3
  13.5 0.0 copy-done.4
  13.5 0.5 shard_map.75
  14.0 3.5 %collective-permute-start.4 = (bf16[48,896]{1,0:T(8,128)(2,1)S(1)}, bf16[48,896]{1,0:T(8,128)(2,1)S(1)}, u32[]{:S(2)}, u32[]{:S(2)}) collective-permute-start(bf16[48,896]{1,0:T(8,128)(2,1)S(1)} %get-tuple-element.30), channel_id=1, source_target_pairs={{0,1},{1,2},{2,3},{4,5},{5,6},{6,7},{8,9},{9,10},{10,11},{12,13},{... | collective-permute-start | bytes 258056 | tf_op jit(solution)/shard_map/ppermute | solution.py:525
  17.5 1.3 %collective-permute-start.5 = (bf16[48,896]{1,0:T(8,128)(2,1)S(1)}, bf16[48,896]{1,0:T(8,128)(2,1)S(1)}, u32[]{:S(2)}, u32[]{:S(2)}) collective-permute-start(bf16[48,896]{1,0:T(8,128)(2,1)S(1)} %get-tuple-element.31), channel_id=1, source_target_pairs={{1,0},{2,1},{3,2},{5,4},{6,5},{7,6},{9,8},{10,9},{11,10},{13,12},{... | collective-permute-start | bytes 258056 | tf_op jit(solution)/shard_map/ppermute | solution.py:526
  18.8 0.8 %collective-permute-done.4.low = bf16[48,896]{1,0:T(8,128)(2,1)S(1)} collective-permute-done((bf16[48,896]{1,0:T(8,128)(2,1)S(1)}, bf16[48,896]{1,0:T(8,128)(2,1)S(1)}, u32[]{:S(2)}, u32[]{:S(2)}) %collective-permute-start.4) | collective-permute-done | bytes 86048 | tf_op jit(solution)/shard_map/ppermute | solution.py:525
  19.6 4.3 %collective-permute-done.5.high = bf16[48,896]{1,0:T(8,128)(2,1)S(1)} collective-permute-done((bf16[48,896]{1,0:T(8,128)(2,1)S(1)}, bf16[48,896]{1,0:T(8,128)(2,1)S(1)}, u32[]{:S(2)}, u32[]{:S(2)}) %collective-permute-start.5) | collective-permute-done | bytes 86048 | tf_op jit(solution)/shard_map/ppermute | solution.py:526
  23.9 0.9 %shard_map.76 = (bf16[16,11648]{1,0:T(8,128)(2,1)}, bf16[16,11648]{1,0:T(8,128)(2,1)}) custom-call(bf16[48,6272]{1,0:T(8,128)(2,1)S(1)} %get-tuple-element.29.own, bf16[48,896]{1,0:T(8,128)(2,1)S(1)} %collective-permute-done.4.low, bf16[48,896]{1,0:T(8,128)(2,1)S(1)} %collective-permute-done.5.high), custom_call_target="tpu_custom_call" | custom-call | flops 1000 | bytes 1519616 | tf_op jit(solution)/shard_map/pallas_call | solution.py:464
  24.8 0.0 collective-permute-done.6.rest_0_
  24.8 0.0 collective-permute-done.7.rest_1_
  24.8 0.3 collective-permute-done.8.rest_2_
  25.1 1.8 %shard_map.77.rest_0_ = bf16[1168,128]{1,0:T(8,128)(2,1)S(1)} custom-call(f32[48,3072]{1,0:T(8,128)S(1)} %get-tuple-element.34.mine, bf16[1168,128]{1,0:T(8,128)(2,1)S(1)} %collective-permute-done.6.rest_0_, bf16[1168,128]{1,0:T(8,128)(2,1)S(1)} %collective-permute-done.7.rest_1_, bf16[1168,128]{1,0:T(8,128)(2,1)S(1)} %collective-permute-done.8.rest_2_), custom_call_target="tpu_custom_call" | custom-call | flops 17694720 | bytes 1785856 | tf_op jit(solution)/shard_map/pallas_call | solution.py:464
  26.9 2.7 %collective-permute-start.11 = (bf16[1168,128]{1,0:T(8,128)(2,1)S(1)}, bf16[1168,128]{1,0:T(8,128)(2,1)S(1)}, u32[]{:S(2)}, u32[]{:S(2)}) collective-permute-start(bf16[1168,128]{1,0:T(8,128)(2,1)S(1)} %shard_map.77.rest_0_), channel_id=1, source_target_pairs={{0,2},{1,3},{2,0},{3,1},{4,6},{5,7},{6,4},{7,5},{8,10},{9,11},{10,... | collective-permute-start | bytes 897032 | tf_op jit(solution)/shard_map/ppermute | solution.py:550
  29.6 1.6 %collective-permute-start.12 = (bf16[1168,128]{1,0:T(8,128)(2,1)S(1)}, bf16[1168,128]{1,0:T(8,128)(2,1)S(1)}, u32[]{:S(2)}, u32[]{:S(2)}) collective-permute-start(bf16[1168,128]{1,0:T(8,128)(2,1)S(1)} %shard_map.77.rest_0_), channel_id=1, source_target_pairs={{0,1},{1,0},{2,3},{3,2},{4,5},{5,4},{6,7},{7,6},{8,9},{9,8},{10,11... | collective-permute-start | bytes 897032 | tf_op jit(solution)/shard_map/ppermute | solution.py:550
  31.1 1.3 %collective-permute-start.10 = (bf16[16,11648]{1,0:T(8,128)(2,1)}, bf16[16,11648]{1,0:T(8,128)(2,1)S(1)}, u32[]{:S(2)}, u32[]{:S(2)}) collective-permute-start(bf16[16,11648]{1,0:T(8,128)(2,1)} %get-tuple-element.41), channel_id=1, source_target_pairs={{4,0},{8,4},{12,8},{16,12},{20,16},{24,20},{28,24},{5,1},{9,5},{13... | collective-permute-start | bytes 1118216 | tf_op jit(solution)/shard_map/ppermute | solution.py:564
  32.4 3.1 %collective-permute-start.9 = (bf16[16,11648]{1,0:T(8,128)(2,1)}, bf16[16,11648]{1,0:T(8,128)(2,1)S(1)}, u32[]{:S(2)}, u32[]{:S(2)}) collective-permute-start(bf16[16,11648]{1,0:T(8,128)(2,1)} %get-tuple-element.40), channel_id=1, source_target_pairs={{0,4},{4,8},{8,12},{12,16},{16,20},{20,24},{24,28},{1,5},{5,9},{9,... | collective-permute-start | bytes 1118216 | tf_op jit(solution)/shard_map/ppermute | solution.py:563
  35.5 5.7 %collective-permute-done.11.rest_1_ = bf16[1168,128]{1,0:T(8,128)(2,1)S(1)} collective-permute-done((bf16[1168,128]{1,0:T(8,128)(2,1)S(1)}, bf16[1168,128]{1,0:T(8,128)(2,1)S(1)}, u32[]{:S(2)}, u32[]{:S(2)}) %collective-permute-start.11) | collective-permute-done | bytes 299040 | tf_op jit(solution)/shard_map/ppermute | solution.py:550
  41.2 0.2 collective-permute-done.12.rest_2_
  41.4 1.4 %collective-permute-start.13 = (bf16[1168,128]{1,0:T(8,128)(2,1)S(1)}, bf16[1168,128]{1,0:T(8,128)(2,1)S(1)}, u32[]{:S(2)}, u32[]{:S(2)}) collective-permute-start(bf16[1168,128]{1,0:T(8,128)(2,1)S(1)} %broadcast_select_fusion), channel_id=1, source_target_pairs={{0,2},{3,1},{1,0},{2,3},{4,6},{7,5},{5,4},{6,7},{8,10},{11,9},{9,8... | collective-permute-start | bytes 897032 | tf_op jit(solution)/shard_map/ppermute | solution.py:557
  42.8 0.0 copy-done.6
  42.8 0.1 copy.8.depth_factor
  42.9 1.6 %shard_map.79.earlier = f32[96,1536]{1,0:T(8,128)S(1)} custom-call(bf16[96,384]{1,0:T(8,128)(2,1)S(1)} %get-tuple-element.28.second, bf16[1168,128]{1,0:T(8,128)(2,1)S(1)} %shard_map.77.rest_0_, bf16[1168,128]{1,0:T(8,128)(2,1)S(1)} %collective-permute-done.11.rest_1_, bf16[1168,128]{1,0:T(8,128)(2,1)S(1)} %collective-permute-done.12.rest_2_), custom_call_target="tpu_custom_call" | custom-call | flops 226492416 | bytes 1560576 | tf_op jit(solution)/shard_map/pallas_call | solution.py:464
  44.5 0.0 collective-permute-done.10.right
  44.5 0.0 collective-permute-done.9.left
  44.5 3.3 %shard_map.78.waves = f32[48,48,128]{2,1,0:T(8,128)S(1)} custom-call(f32[16,6144]{1,0:T(8,128)S(1)} %copy-done, f32[16,6144]{1,0:T(8,128)S(1)} %copy-done.1, bf16[16,6144]{1,0:T(8,128)(2,1)S(1)} %copy-done.3, bf16[16,11648]{1,0:T(8,128)(2,1)S(1)} %collective-permute-done.9.left, bf16[16,11648]{1,0:T(8,128)(2,1)S(1)} %collective-permute-done.10.right, ...), custom_call_target="tpu_custom_call" | custom-call | flops 44236800 | bytes 3080192 | tf_op jit(solution)/shard_map/pallas_call | solution.py:464
  47.9 1.3 %collective-permute-done.13.rest_0_ = bf16[1168,128]{1,0:T(8,128)(2,1)S(1)} collective-permute-done((bf16[1168,128]{1,0:T(8,128)(2,1)S(1)}, bf16[1168,128]{1,0:T(8,128)(2,1)S(1)}, u32[]{:S(2)}, u32[]{:S(2)}) %collective-permute-start.13) | collective-permute-done | bytes 299040 | tf_op jit(solution)/shard_map/ppermute | solution.py:557
  49.2 2.2 %shard_map.80 = f32[16,6144]{1,0:T(8,128)} custom-call(bf16[96,384]{1,0:T(8,128)(2,1)S(1)} %get-tuple-element.28.second, bf16[64,32]{1,0:T(8,128)(2,1)S(1)} %copy.8.depth_factor, f32[48,48,128]{2,1,0:T(8,128)S(1)} %shard_map.78.waves, f32[96,1536]{1,0:T(8,128)S(1)} %shard_map.79.earlier, bf16[1168,128]{1,0:T(8,128)(2,1)S(1)} %collective-permute-done.13.rest_0_), custom_call_target="tpu_custom_call" | custom-call | flops 56623104 | bytes 2539520 | tf_op jit(solution)/shard_map/pallas_call | solution.py:464
  (4 shorter events, 0.0 us)
Async XLA Ops:
  0.0 13.5 %copy-start = (f32[16,6144]{1,0:T(8,128)S(1)}, f32[16,6144]{1,0:T(8,128)}, u32[]{:S(2)}) copy-start(f32[16,6144]{1,0:T(8,128)} %pressure.2) | copy-start | bytes 1179652
  0.0 13.5 %copy-start.1 = (f32[16,6144]{1,0:T(8,128)S(1)}, f32[16,6144]{1,0:T(8,128)}, u32[]{:S(2)}) copy-start(f32[16,6144]{1,0:T(8,128)} %previous.3) | copy-start | bytes 1179652
  0.0 8.4 %collective-permute-start = (bf16[3,48,3072]{2,1,0:T(8,128)(2,1)}, bf16[3,48,3072]{2,1,0:T(8,128)(2,1)S(1)}, u32[]{:S(2)}, u32[]{:S(2)}) collective-permute-start(bf16[3,48,3072]{2,1,0:T(8,128)(2,1)} %core.1), channel_id=1, source_target_pairs={{0,4},{4,0},{8,12},{12,8},{16,20},{20,16},{24,28},{28,24},{1,5},{5... | collective-permute-start | bytes 2654216 | tf_op jit(solution)/shard_map/ppermute | solution.py:492
  0.5 6.1 %collective-permute-start.1 = (bf16[16,384]{1,0:T(8,128)(2,1)}, bf16[16,384]{1,0:T(8,128)(2,1)S(1)}, u32[]{:S(2)}, u32[]{:S(2)}) collective-permute-start(bf16[16,384]{1,0:T(8,128)(2,1)} %factor.1), channel_id=1, source_target_pairs={{0,24},{4,28},{8,16},{12,20},{16,8},{20,12},{24,0},{28,4},{1,25},{... | collective-permute-start | bytes 36872 | tf_op jit(solution)/shard_map/ppermute | solution.py:491
  4.0 3.9 %collective-permute-start.2 = (bf16[16,384]{1,0:T(8,128)(2,1)}, bf16[16,384]{1,0:T(8,128)(2,1)S(1)}, u32[]{:S(2)}, u32[]{:S(2)}) collective-permute-start(bf16[16,384]{1,0:T(8,128)(2,1)} %factor.1), channel_id=1, source_target_pairs={{0,16},{4,20},{8,24},{12,28},{16,0},{20,4},{24,8},{28,12},{1,17},{... | collective-permute-start | bytes 36872 | tf_op jit(solution)/shard_map/ppermute | solution.py:491
  4.5 3.9 %collective-permute-start.3 = (bf16[16,384]{1,0:T(8,128)(2,1)}, bf16[16,384]{1,0:T(8,128)(2,1)S(1)}, u32[]{:S(2)}, u32[]{:S(2)}) collective-permute-start(bf16[16,384]{1,0:T(8,128)(2,1)} %factor.1), channel_id=1, source_target_pairs={{0,8},{4,12},{8,0},{12,4},{16,24},{20,28},{24,16},{28,20},{1,9},{5... | collective-permute-start | bytes 36872 | tf_op jit(solution)/shard_map/ppermute | solution.py:491
  4.6 1.2 %copy-start.2 = (bf16[3,48,3072]{2,1,0:T(8,128)(2,1)S(1)}, bf16[3,48,3072]{2,1,0:T(8,128)(2,1)}, u32[]{:S(2)}) copy-start(bf16[3,48,3072]{2,1,0:T(8,128)(2,1)} %core.1) | copy-start | bytes 2654212
  5.8 0.7 %copy-start.5 = (bf16[16,384]{1,0:T(8,128)(2,1)S(1)}, bf16[16,384]{1,0:T(8,128)(2,1)}, u32[]{:S(2)}) copy-start(bf16[16,384]{1,0:T(8,128)(2,1)} %factor.1) | copy-start | bytes 36868
  6.5 7.0 %copy-start.3 = (bf16[16,6144]{1,0:T(8,128)(2,1)S(1)}, bf16[16,6144]{1,0:T(8,128)(2,1)}, u32[]{:S(2)}) copy-start(bf16[16,6144]{1,0:T(8,128)(2,1)} %velocity.3) | copy-start | bytes 589828
  6.5 7.0 %copy-start.4 = (bf16[96,384]{1,0:T(8,128)(2,1)S(1)}, bf16[96,384]{1,0:T(8,128)(2,1)}, u32[]{:S(2)}) copy-start(bf16[96,384]{1,0:T(8,128)(2,1)} %second.1) | copy-start | bytes 221188
  9.9 14.9 %collective-permute-start.6 = (bf16[1168,128]{1,0:T(8,128)(2,1)S(1)}, bf16[1168,128]{1,0:T(8,128)(2,1)S(1)}, u32[]{:S(2)}, u32[]{:S(2)}) collective-permute-start(bf16[1168,128]{1,0:T(8,128)(2,1)S(1)} %get-tuple-element.35), channel_id=1, source_target_pairs={{0,8},{4,12},{8,0},{12,4},{16,24},{20,28},{24,16},{28,20},{1,9},{5... | collective-permute-start | bytes 897032 | tf_op jit(solution)/shard_map/ppermute | solution.py:511
  10.1 14.7 %collective-permute-start.7 = (bf16[1168,128]{1,0:T(8,128)(2,1)S(1)}, bf16[1168,128]{1,0:T(8,128)(2,1)S(1)}, u32[]{:S(2)}, u32[]{:S(2)}) collective-permute-start(bf16[1168,128]{1,0:T(8,128)(2,1)S(1)} %get-tuple-element.36), channel_id=1, source_target_pairs={{0,16},{4,20},{8,24},{12,28},{16,0},{20,4},{24,8},{28,12},{1,17},{... | collective-permute-start | bytes 897032 | tf_op jit(solution)/shard_map/ppermute | solution.py:511
  12.0 13.0 %collective-permute-start.8 = (bf16[1168,128]{1,0:T(8,128)(2,1)S(1)}, bf16[1168,128]{1,0:T(8,128)(2,1)S(1)}, u32[]{:S(2)}, u32[]{:S(2)}) collective-permute-start(bf16[1168,128]{1,0:T(8,128)(2,1)S(1)} %get-tuple-element.37), channel_id=1, source_target_pairs={{0,24},{4,28},{8,16},{12,20},{16,8},{20,12},{24,0},{28,4},{1,25},{... | collective-permute-start | bytes 897032 | tf_op jit(solution)/shard_map/ppermute | solution.py:511
  14.0 5.6 %collective-permute-start.4 = (bf16[48,896]{1,0:T(8,128)(2,1)S(1)}, bf16[48,896]{1,0:T(8,128)(2,1)S(1)}, u32[]{:S(2)}, u32[]{:S(2)}) collective-permute-start(bf16[48,896]{1,0:T(8,128)(2,1)S(1)} %get-tuple-element.30), channel_id=1, source_target_pairs={{0,1},{1,2},{2,3},{4,5},{5,6},{6,7},{8,9},{9,10},{10,11},{12,13},{... | collective-permute-start | bytes 258056 | tf_op jit(solution)/shard_map/ppermute | solution.py:525
  17.5 6.4 %collective-permute-start.5 = (bf16[48,896]{1,0:T(8,128)(2,1)S(1)}, bf16[48,896]{1,0:T(8,128)(2,1)S(1)}, u32[]{:S(2)}, u32[]{:S(2)}) collective-permute-start(bf16[48,896]{1,0:T(8,128)(2,1)S(1)} %get-tuple-element.31), channel_id=1, source_target_pairs={{1,0},{2,1},{3,2},{5,4},{6,5},{7,6},{9,8},{10,9},{11,10},{13,12},{... | collective-permute-start | bytes 258056 | tf_op jit(solution)/shard_map/ppermute | solution.py:526
  24.8 18.0 %copy-start.6 = (bf16[64,32]{0,1:T(8,128)(2,1)S(1)}, bf16[64,32]{0,1:T(8,128)(2,1)}, u32[]{:S(2)}) copy-start(bf16[64,32]{0,1:T(8,128)(2,1)} %param.13) | copy-start | bytes 12292
  26.9 14.3 %collective-permute-start.11 = (bf16[1168,128]{1,0:T(8,128)(2,1)S(1)}, bf16[1168,128]{1,0:T(8,128)(2,1)S(1)}, u32[]{:S(2)}, u32[]{:S(2)}) collective-permute-start(bf16[1168,128]{1,0:T(8,128)(2,1)S(1)} %shard_map.77.rest_0_), channel_id=1, source_target_pairs={{0,2},{1,3},{2,0},{3,1},{4,6},{5,7},{6,4},{7,5},{8,10},{9,11},{10,... | collective-permute-start | bytes 897032 | tf_op jit(solution)/shard_map/ppermute | solution.py:550
  29.6 11.8 %collective-permute-start.12 = (bf16[1168,128]{1,0:T(8,128)(2,1)S(1)}, bf16[1168,128]{1,0:T(8,128)(2,1)S(1)}, u32[]{:S(2)}, u32[]{:S(2)}) collective-permute-start(bf16[1168,128]{1,0:T(8,128)(2,1)S(1)} %shard_map.77.rest_0_), channel_id=1, source_target_pairs={{0,1},{1,0},{2,3},{3,2},{4,5},{5,4},{6,7},{7,6},{8,9},{9,8},{10,11... | collective-permute-start | bytes 897032 | tf_op jit(solution)/shard_map/ppermute | solution.py:550
  31.1 13.4 %collective-permute-start.10 = (bf16[16,11648]{1,0:T(8,128)(2,1)}, bf16[16,11648]{1,0:T(8,128)(2,1)S(1)}, u32[]{:S(2)}, u32[]{:S(2)}) collective-permute-start(bf16[16,11648]{1,0:T(8,128)(2,1)} %get-tuple-element.41), channel_id=1, source_target_pairs={{4,0},{8,4},{12,8},{16,12},{20,16},{24,20},{28,24},{5,1},{9,5},{13... | collective-permute-start | bytes 1118216 | tf_op jit(solution)/shard_map/ppermute | solution.py:564
  32.4 12.1 %collective-permute-start.9 = (bf16[16,11648]{1,0:T(8,128)(2,1)}, bf16[16,11648]{1,0:T(8,128)(2,1)S(1)}, u32[]{:S(2)}, u32[]{:S(2)}) collective-permute-start(bf16[16,11648]{1,0:T(8,128)(2,1)} %get-tuple-element.40), channel_id=1, source_target_pairs={{0,4},{4,8},{8,12},{12,16},{16,20},{20,24},{24,28},{1,5},{5,9},{9,... | collective-permute-start | bytes 1118216 | tf_op jit(solution)/shard_map/ppermute | solution.py:563
  41.4 7.7 %collective-permute-start.13 = (bf16[1168,128]{1,0:T(8,128)(2,1)S(1)}, bf16[1168,128]{1,0:T(8,128)(2,1)S(1)}, u32[]{:S(2)}, u32[]{:S(2)}) collective-permute-start(bf16[1168,128]{1,0:T(8,128)(2,1)S(1)} %broadcast_select_fusion), channel_id=1, source_target_pairs={{0,2},{3,1},{1,0},{2,3},{4,6},{7,5},{5,4},{6,7},{8,10},{11,9},{9,8... | collective-permute-start | bytes 897032 | tf_op jit(solution)/shard_map/ppermute | solution.py:557

commit v9 on v8

--- a/solution.py
+++ b/solution.py
@@ -128,6 +128,18 @@
                 ]
     for distance in range(1, chips):
         put_message(sends[distance - 1], partial.at[distance - 1])
+
+
+def presum_kernel(mine, part, total):
+    lines, flat = mine.shape
+    unit = unit_of(part)[:1]
+    for group in range(flat // LANES):
+        lanes = slice(group * LANES, (group + 1) * LANES)
+        for start, count in pieces(lines):
+            into = group * stride_of(lines) + start
+            total[start : start + count, lanes] = mine[start : start + count, lanes] + decode(
+                part[into : into + count, :], unit
+            )
 
 
 def gather_kernel(depth, steps, mine, *rest):
@@ -525,6 +537,8 @@
     low = lax.ppermute(up, "gy", [(i, i + 1) for i in range(count_y - 1)])
     high = lax.ppermute(down, "gy", [(i + 1, i) for i in range(count_y - 1)])
 
+    (mine,) = call(presum_kernel, [shape_of(lines, core_flat)], [], 1000, mine, received.pop(0))
+    mine, low, high = lax.optimization_barrier((mine, low, high))
     ahead, behind = call(
         edge_kernel,
         [shape_of(cells, layout(cells, flat, near)[-1].stop, dtype=BF16)] * 2,

time: 51.9 us -> 51.6 us (level)
    ppermute x3, waiting for transfers between devices: 0.27 us -> 1.5 us  [body(): lax.ppermute(send, 'gx', route)]
    ppermute x1, waiting for transfers between devices: 4.3 us -> 3.5 us  [body(): high = lax.ppermute(down, 'gy', [(i + 1, i) for i in range(count_y - 1)])]
    ppermute x1, waiting for transfers between devices: 0.78 us -> 0.01 us  [body(): low = lax.ppermute(up, 'gy', [(i, i + 1) for i in range(count_y - 1)])]
    pallas_call x8 -> x9, Pallas kernels: 11.9 us -> 11.9 us  [call(): pl.pallas_call(kernel, out_shape=outs, scratch_shapes=scratch, cost_estim...]
  transfers between devices with their start and end apart: 14 -> 14, of which waited for: 8 -> 8; matrix products, arithmetic and copies ran while one was open for 0% -> 0% of each run, Pallas kernels for 12% -> 13%
where the time goes in v9:
time: 51.6 us; the launch traced here: 51 us
  starting transfers between devices  22.9 us (44%)
  waiting for transfers between devices  14 us (27%)
  Pallas kernels  11.9 us (23%)
  local copies, waits for them, and re-layouts  1.99 us (4%)
    pallas_call x9, Pallas kernels, call(): pl.pallas_call(kernel, out_shape=outs, scratch_shapes=scratch, cost_estim...  11.9 us
    ppermute x2, waiting for transfers between devices, far(): lax.ppermute(codes, 'gy', [(i, i ^ distance) for i in range(count_y)])  5.91 us
    ppermute x2, starting transfers between devices, far(): lax.ppermute(codes, 'gy', [(i, i ^ distance) for i in range(count_y)])  4.23 us
    ppermute x3, starting transfers between devices, body(): lax.ppermute(first_factor, 'gx', route)  4.17 us
    ppermute x3, starting transfers between devices, body(): lax.ppermute(send, 'gx', route)  3.55 us
    ppermute x1, waiting for transfers between devices, body(): high = lax.ppermute(down, 'gy', [(i + 1, i) for i in range(count_y - 1)])  3.5 us
    ppermute x1, starting transfers between devices, body(): low = lax.ppermute(up, 'gy', [(i, i + 1) for i in range(count_y - 1)])  3.49 us
    ppermute x1, starting transfers between devices, body(): left = lax.ppermute(ahead, 'gx', [(i, i + 1) for i in range(count_x - 1)])  3.05 us
  transfers between devices with their start and end apart: 14, of which 8 were waited for; matrix products, arithmetic and copies ran while one was open for 0% of the time, Pallas kernels for 13%

profile of v9, /device:TPU:0, one launch (start us, length us, event | category | flops | bytes accessed | tf_op | source)
XLA Modules:
  0.0 51.0 jit_solution(673517951607571560)
XLA Ops:
  0.0 0.0 copy-start
  0.0 0.0 copy-start.1
  0.0 0.5 collective-permute-start
  0.5 3.5 %collective-permute-start.1 = (bf16[16,384]{1,0:T(8,128)(2,1)}, bf16[16,384]{1,0:T(8,128)(2,1)S(1)}, u32[]{:S(2)}, u32[]{:S(2)}) collective-permute-start(bf16[16,384]{1,0:T(8,128)(2,1)} %factor.1), channel_id=1, source_target_pairs={{0,24},{4,28},{8,16},{12,20},{16,8},{20,12},{24,0},{28,4},{1,25},{... | collective-permute-start | bytes 36872 | tf_op jit(solution)/shard_map/ppermute | solution.py:503
  4.0 0.5 collective-permute-start.2
  4.5 0.1 collective-permute-start.3
  4.6 0.0 copy-start.2
  4.6 1.2 %copy-done.2 = bf16[3,48,3072]{2,1,0:T(8,128)(2,1)S(1)} copy-done((bf16[3,48,3072]{2,1,0:T(8,128)(2,1)S(1)}, bf16[3,48,3072]{2,1,0:T(8,128)(2,1)}, u32[]{:S(2)}) %copy-start.2) | copy-done | bytes 884760
  5.8 0.7 %copy-done.5 = bf16[16,384]{1,0:T(8,128)(2,1)S(1)} copy-done((bf16[16,384]{1,0:T(8,128)(2,1)S(1)}, bf16[16,384]{1,0:T(8,128)(2,1)}, u32[]{:S(2)}) %copy-start.5) | copy-done | bytes 12312
  6.5 0.1 shard_map.73
  6.6 0.0 collective-permute-done.1.rest_0_
  6.6 1.3 %collective-permute-done.2.rest_1_ = bf16[16,384]{1,0:T(8,128)(2,1)S(1)} collective-permute-done((bf16[16,384]{1,0:T(8,128)(2,1)}, bf16[16,384]{1,0:T(8,128)(2,1)S(1)}, u32[]{:S(2)}, u32[]{:S(2)}) %collective-permute-start.2) | collective-permute-done | bytes 12320 | tf_op jit(solution)/shard_map/ppermute | solution.py:503
  7.9 0.5 collective-permute-done.3.rest_2_
  8.4 0.0 collective-permute-done.other
  8.4 1.5 %shard_map.74 = (f32[48,3072]{1,0:T(8,128)S(1)}, bf16[1168,128]{1,0:T(8,128)(2,1)S(1)}, bf16[1168,128]{1,0:T(8,128)(2,1)S(1)}, bf16[1168,128]{1,0:T(8,128)(2,1)S(1)}) custom-call(bf16[3,48,3072]{2,1,0:T(8,128)(2,1)S(1)} %get-tuple-element.27.core, bf16[3,48,3072]{2,1,0:T(8,128)(2,1)S(1)} %collective-permute-done.other, ...), custom_call_target="tpu_custom_call" | custom-call | flops 113246208 | bytes 3305472 | tf_op jit(solution)/shard_map/pallas_call | solution.py:476
  9.9 0.2 collective-permute-start.4
  10.1 1.9 %collective-permute-start.7 = (bf16[1168,128]{1,0:T(8,128)(2,1)S(1)}, bf16[1168,128]{1,0:T(8,128)(2,1)S(1)}, u32[]{:S(2)}, u32[]{:S(2)}) collective-permute-start(bf16[1168,128]{1,0:T(8,128)(2,1)S(1)} %get-tuple-element.42), channel_id=1, source_target_pairs={{0,16},{4,20},{8,24},{12,28},{16,0},{20,4},{24,8},{28,12},{1,17},{... | collective-permute-start | bytes 897032 | tf_op jit(solution)/shard_map/ppermute | solution.py:523
  12.0 1.4 %collective-permute-start.8 = (bf16[1168,128]{1,0:T(8,128)(2,1)S(1)}, bf16[1168,128]{1,0:T(8,128)(2,1)S(1)}, u32[]{:S(2)}, u32[]{:S(2)}) collective-permute-start(bf16[1168,128]{1,0:T(8,128)(2,1)S(1)} %get-tuple-element.43), channel_id=1, source_target_pairs={{0,24},{4,28},{8,16},{12,20},{16,8},{20,12},{24,0},{28,4},{1,25},{... | collective-permute-start | bytes 897032 | tf_op jit(solution)/shard_map/ppermute | solution.py:523
  13.5 0.0 copy-done
  13.5 0.0 copy-done.1
  13.5 0.0 copy-done.3
  13.5 0.0 copy-done.4
  13.5 0.5 %shard_map.75 = (bf16[48,6272]{1,0:T(8,128)(2,1)S(1)}, bf16[48,896]{1,0:T(8,128)(2,1)S(1)}, bf16[48,896]{1,0:T(8,128)(2,1)S(1)}, bf16[96,384]{1,0:T(8,128)(2,1)S(1)}) custom-call(f32[16,6144]{1,0:T(8,128)S(1)} %copy-done, f32[16,6144]{1,0:T(8,128)S(1)} %copy-done.1, bf16[16,6144]{1,0:T(8,128)(2,1)S(1)} %copy-done.3, bf16[96,384]{1,0:T(8,128)(2,1)S(1)} %copy-done.4), custom_call_target="tpu_custom_call" | custom-call | flops 983040 | bytes 1904640 | tf_op jit(solution)/shard_map/pallas_call | solution.py:476
  14.0 3.5 %collective-permute-start.5 = (bf16[48,896]{1,0:T(8,128)(2,1)S(1)}, bf16[48,896]{1,0:T(8,128)(2,1)S(1)}, u32[]{:S(2)}, u32[]{:S(2)}) collective-permute-start(bf16[48,896]{1,0:T(8,128)(2,1)S(1)} %get-tuple-element.33), channel_id=1, source_target_pairs={{0,1},{1,2},{2,3},{4,5},{5,6},{6,7},{8,9},{9,10},{10,11},{12,13},{... | collective-permute-start | bytes 258056 | tf_op jit(solution)/shard_map/ppermute | solution.py:537
  17.5 1.3 %collective-permute-start.6 = (bf16[48,896]{1,0:T(8,128)(2,1)S(1)}, bf16[48,896]{1,0:T(8,128)(2,1)S(1)}, u32[]{:S(2)}, u32[]{:S(2)}) collective-permute-start(bf16[48,896]{1,0:T(8,128)(2,1)S(1)} %get-tuple-element.34), channel_id=1, source_target_pairs={{1,0},{2,1},{3,2},{5,4},{6,5},{7,6},{9,8},{10,9},{11,10},{13,12},{... | collective-permute-start | bytes 258056 | tf_op jit(solution)/shard_map/ppermute | solution.py:538
  18.8 1.2 %collective-permute-done.4.part = bf16[1168,128]{1,0:T(8,128)(2,1)S(1)} collective-permute-done((bf16[1168,128]{1,0:T(8,128)(2,1)S(1)}, bf16[1168,128]{1,0:T(8,128)(2,1)S(1)}, u32[]{:S(2)}, u32[]{:S(2)}) %collective-permute-start.4) | collective-permute-done | bytes 299040 | tf_op jit(solution)/shard_map/ppermute | solution.py:523
  20.0 0.3 shard_map.76.mine
  20.4 0.0 collective-permute-done.5.low
  20.4 3.5 %collective-permute-done.6.high = bf16[48,896]{1,0:T(8,128)(2,1)S(1)} collective-permute-done((bf16[48,896]{1,0:T(8,128)(2,1)S(1)}, bf16[48,896]{1,0:T(8,128)(2,1)S(1)}, u32[]{:S(2)}, u32[]{:S(2)}) %collective-permute-start.6) | collective-permute-done | bytes 86048 | tf_op jit(solution)/shard_map/ppermute | solution.py:538
  23.9 0.9 %shard_map.77 = (bf16[16,11648]{1,0:T(8,128)(2,1)}, bf16[16,11648]{1,0:T(8,128)(2,1)}) custom-call(bf16[48,6272]{1,0:T(8,128)(2,1)S(1)} %get-tuple-element.36.own, bf16[48,896]{1,0:T(8,128)(2,1)S(1)} %collective-permute-done.5.low, bf16[48,896]{1,0:T(8,128)(2,1)S(1)} %collective-permute-done.6.high), custom_call_target="tpu_custom_call" | custom-call | flops 1000 | bytes 1519616 | tf_op jit(solution)/shard_map/pallas_call | solution.py:476
  24.8 0.0 collective-permute-done.7.rest_0_
  24.8 0.3 collective-permute-done.8.rest_1_
  25.1 1.5 %shard_map.78.rest_0_ = bf16[1168,128]{1,0:T(8,128)(2,1)S(1)} custom-call(f32[48,3072]{1,0:T(8,128)S(1)} %shard_map.76.mine, bf16[1168,128]{1,0:T(8,128)(2,1)S(1)} %collective-permute-done.7.rest_0_, bf16[1168,128]{1,0:T(8,128)(2,1)S(1)} %collective-permute-done.8.rest_1_), custom_call_target="tpu_custom_call" | custom-call | flops 17694720 | bytes 1486848 | tf_op jit(solution)/shard_map/pallas_call | solution.py:476
  26.6 2.7 %collective-permute-start.11 = (bf16[1168,128]{1,0:T(8,128)(2,1)S(1)}, bf16[1168,128]{1,0:T(8,128)(2,1)S(1)}, u32[]{:S(2)}, u32[]{:S(2)}) collective-permute-start(bf16[1168,128]{1,0:T(8,128)(2,1)S(1)} %shard_map.78.rest_0_), channel_id=1, source_target_pairs={{0,2},{1,3},{2,0},{3,1},{4,6},{5,7},{6,4},{7,5},{8,10},{9,11},{10,... | collective-permute-start | bytes 897032 | tf_op jit(solution)/shard_map/ppermute | solution.py:564
  29.3 1.6 %collective-permute-start.12 = (bf16[1168,128]{1,0:T(8,128)(2,1)S(1)}, bf16[1168,128]{1,0:T(8,128)(2,1)S(1)}, u32[]{:S(2)}, u32[]{:S(2)}) collective-permute-start(bf16[1168,128]{1,0:T(8,128)(2,1)S(1)} %shard_map.78.rest_0_), channel_id=1, source_target_pairs={{0,1},{1,0},{2,3},{3,2},{4,5},{5,4},{6,7},{7,6},{8,9},{9,8},{10,11... | collective-permute-start | bytes 897032 | tf_op jit(solution)/shard_map/ppermute | solution.py:564
  30.8 1.3 %collective-permute-start.10 = (bf16[16,11648]{1,0:T(8,128)(2,1)}, bf16[16,11648]{1,0:T(8,128)(2,1)S(1)}, u32[]{:S(2)}, u32[]{:S(2)}) collective-permute-start(bf16[16,11648]{1,0:T(8,128)(2,1)} %get-tuple-element.47), channel_id=1, source_target_pairs={{4,0},{8,4},{12,8},{16,12},{20,16},{24,20},{28,24},{5,1},{9,5},{13... | collective-permute-start | bytes 1118216 | tf_op jit(solution)/shard_map/ppermute | solution.py:578
  32.1 3.1 %collective-permute-start.9 = (bf16[16,11648]{1,0:T(8,128)(2,1)}, bf16[16,11648]{1,0:T(8,128)(2,1)S(1)}, u32[]{:S(2)}, u32[]{:S(2)}) collective-permute-start(bf16[16,11648]{1,0:T(8,128)(2,1)} %get-tuple-element.46), channel_id=1, source_target_pairs={{0,4},{4,8},{8,12},{12,16},{16,20},{20,24},{24,28},{1,5},{5,9},{9,... | collective-permute-start | bytes 1118216 | tf_op jit(solution)/shard_map/ppermute | solution.py:577
  35.2 5.7 %collective-permute-done.11.rest_1_ = bf16[1168,128]{1,0:T(8,128)(2,1)S(1)} collective-permute-done((bf16[1168,128]{1,0:T(8,128)(2,1)S(1)}, bf16[1168,128]{1,0:T(8,128)(2,1)S(1)}, u32[]{:S(2)}, u32[]{:S(2)}) %collective-permute-start.11) | collective-permute-done | bytes 299040 | tf_op jit(solution)/shard_map/ppermute | solution.py:564
  40.9 0.2 collective-permute-done.12.rest_2_
  41.1 1.4 %collective-permute-start.13 = (bf16[1168,128]{1,0:T(8,128)(2,1)S(1)}, bf16[1168,128]{1,0:T(8,128)(2,1)S(1)}, u32[]{:S(2)}, u32[]{:S(2)}) collective-permute-start(bf16[1168,128]{1,0:T(8,128)(2,1)S(1)} %broadcast_select_fusion), channel_id=1, source_target_pairs={{0,2},{3,1},{1,0},{2,3},{4,6},{7,5},{5,4},{6,7},{8,10},{11,9},{9,8... | collective-permute-start | bytes 897032 | tf_op jit(solution)/shard_map/ppermute | solution.py:571
  42.5 0.0 copy-done.6
  42.5 0.1 copy.8.depth_factor
  42.6 1.6 %shard_map.80.earlier = f32[96,1536]{1,0:T(8,128)S(1)} custom-call(bf16[96,384]{1,0:T(8,128)(2,1)S(1)} %get-tuple-element.31.second, bf16[1168,128]{1,0:T(8,128)(2,1)S(1)} %shard_map.78.rest_0_, bf16[1168,128]{1,0:T(8,128)(2,1)S(1)} %collective-permute-done.11.rest_1_, bf16[1168,128]{1,0:T(8,128)(2,1)S(1)} %collective-permute-done.12.rest_2_), custom_call_target="tpu_custom_call" | custom-call | flops 226492416 | bytes 1560576 | tf_op jit(solution)/shard_map/pallas_call | solution.py:476
  44.2 0.0 collective-permute-done.10.right
  44.2 0.0 collective-permute-done.9.left
  44.2 3.3 %shard_map.79.waves = f32[48,48,128]{2,1,0:T(8,128)S(1)} custom-call(f32[16,6144]{1,0:T(8,128)S(1)} %copy-done, f32[16,6144]{1,0:T(8,128)S(1)} %copy-done.1, bf16[16,6144]{1,0:T(8,128)(2,1)S(1)} %copy-done.3, bf16[16,11648]{1,0:T(8,128)(2,1)S(1)} %collective-permute-done.9.left, bf16[16,11648]{1,0:T(8,128)(2,1)S(1)} %collective-permute-done.10.right, ...), custom_call_target="tpu_custom_call" | custom-call | flops 44236800 | bytes 3080192 | tf_op jit(solution)/shard_map/pallas_call | solution.py:476
  47.5 1.3 %collective-permute-done.13.rest_0_ = bf16[1168,128]{1,0:T(8,128)(2,1)S(1)} collective-permute-done((bf16[1168,128]{1,0:T(8,128)(2,1)S(1)}, bf16[1168,128]{1,0:T(8,128)(2,1)S(1)}, u32[]{:S(2)}, u32[]{:S(2)}) %collective-permute-start.13) | collective-permute-done | bytes 299040 | tf_op jit(solution)/shard_map/ppermute | solution.py:571
  48.9 2.2 %shard_map.81 = f32[16,6144]{1,0:T(8,128)} custom-call(bf16[96,384]{1,0:T(8,128)(2,1)S(1)} %get-tuple-element.31.second, bf16[64,32]{1,0:T(8,128)(2,1)S(1)} %copy.8.depth_factor, f32[48,48,128]{2,1,0:T(8,128)S(1)} %shard_map.79.waves, f32[96,1536]{1,0:T(8,128)S(1)} %shard_map.80.earlier, bf16[1168,128]{1,0:T(8,128)(2,1)S(1)} %collective-permute-done.13.rest_0_), custom_call_target="tpu_custom_call" | custom-call | flops 56623104 | bytes 2539520 | tf_op jit(solution)/shard_map/pallas_call | solution.py:476
  (5 shorter events, 0.1 us)
Async XLA Ops:
  0.0 13.5 %copy-start = (f32[16,6144]{1,0:T(8,128)S(1)}, f32[16,6144]{1,0:T(8,128)}, u32[]{:S(2)}) copy-start(f32[16,6144]{1,0:T(8,128)} %pressure.2) | copy-start | bytes 1179652
  0.0 13.5 %copy-start.1 = (f32[16,6144]{1,0:T(8,128)S(1)}, f32[16,6144]{1,0:T(8,128)}, u32[]{:S(2)}) copy-start(f32[16,6144]{1,0:T(8,128)} %previous.3) | copy-start | bytes 1179652
  0.0 8.4 %collective-permute-start = (bf16[3,48,3072]{2,1,0:T(8,128)(2,1)}, bf16[3,48,3072]{2,1,0:T(8,128)(2,1)S(1)}, u32[]{:S(2)}, u32[]{:S(2)}) collective-permute-start(bf16[3,48,3072]{2,1,0:T(8,128)(2,1)} %core.1), channel_id=1, source_target_pairs={{0,4},{4,0},{8,12},{12,8},{16,20},{20,16},{24,28},{28,24},{1,5},{5... | collective-permute-start | bytes 2654216 | tf_op jit(solution)/shard_map/ppermute | solution.py:504
  0.5 6.1 %collective-permute-start.1 = (bf16[16,384]{1,0:T(8,128)(2,1)}, bf16[16,384]{1,0:T(8,128)(2,1)S(1)}, u32[]{:S(2)}, u32[]{:S(2)}) collective-permute-start(bf16[16,384]{1,0:T(8,128)(2,1)} %factor.1), channel_id=1, source_target_pairs={{0,24},{4,28},{8,16},{12,20},{16,8},{20,12},{24,0},{28,4},{1,25},{... | collective-permute-start | bytes 36872 | tf_op jit(solution)/shard_map/ppermute | solution.py:503
  4.0 3.9 %collective-permute-start.2 = (bf16[16,384]{1,0:T(8,128)(2,1)}, bf16[16,384]{1,0:T(8,128)(2,1)S(1)}, u32[]{:S(2)}, u32[]{:S(2)}) collective-permute-start(bf16[16,384]{1,0:T(8,128)(2,1)} %factor.1), channel_id=1, source_target_pairs={{0,16},{4,20},{8,24},{12,28},{16,0},{20,4},{24,8},{28,12},{1,17},{... | collective-permute-start | bytes 36872 | tf_op jit(solution)/shard_map/ppermute | solution.py:503
  4.5 3.9 %collective-permute-start.3 = (bf16[16,384]{1,0:T(8,128)(2,1)}, bf16[16,384]{1,0:T(8,128)(2,1)S(1)}, u32[]{:S(2)}, u32[]{:S(2)}) collective-permute-start(bf16[16,384]{1,0:T(8,128)(2,1)} %factor.1), channel_id=1, source_target_pairs={{0,8},{4,12},{8,0},{12,4},{16,24},{20,28},{24,16},{28,20},{1,9},{5... | collective-permute-start | bytes 36872 | tf_op jit(solution)/shard_map/ppermute | solution.py:503
  4.6 1.2 %copy-start.2 = (bf16[3,48,3072]{2,1,0:T(8,128)(2,1)S(1)}, bf16[3,48,3072]{2,1,0:T(8,128)(2,1)}, u32[]{:S(2)}) copy-start(bf16[3,48,3072]{2,1,0:T(8,128)(2,1)} %core.1) | copy-start | bytes 2654212
  5.8 0.7 %copy-start.5 = (bf16[16,384]{1,0:T(8,128)(2,1)S(1)}, bf16[16,384]{1,0:T(8,128)(2,1)}, u32[]{:S(2)}) copy-start(bf16[16,384]{1,0:T(8,128)(2,1)} %factor.1) | copy-start | bytes 36868
  6.5 7.0 %copy-start.3 = (bf16[16,6144]{1,0:T(8,128)(2,1)S(1)}, bf16[16,6144]{1,0:T(8,128)(2,1)}, u32[]{:S(2)}) copy-start(bf16[16,6144]{1,0:T(8,128)(2,1)} %velocity.3) | copy-start | bytes 589828
  6.5 7.0 %copy-start.4 = (bf16[96,384]{1,0:T(8,128)(2,1)S(1)}, bf16[96,384]{1,0:T(8,128)(2,1)}, u32[]{:S(2)}) copy-start(bf16[96,384]{1,0:T(8,128)(2,1)} %second.1) | copy-start | bytes 221188
  9.9 10.1 %collective-permute-start.4 = (bf16[1168,128]{1,0:T(8,128)(2,1)S(1)}, bf16[1168,128]{1,0:T(8,128)(2,1)S(1)}, u32[]{:S(2)}, u32[]{:S(2)}) collective-permute-start(bf16[1168,128]{1,0:T(8,128)(2,1)S(1)} %get-tuple-element.32), channel_id=1, source_target_pairs={{0,8},{4,12},{8,0},{12,4},{16,24},{20,28},{24,16},{28,20},{1,9},{5... | collective-permute-start | bytes 897032 | tf_op jit(solution)/shard_map/ppermute | solution.py:523
  10.1 14.7 %collective-permute-start.7 = (bf16[1168,128]{1,0:T(8,128)(2,1)S(1)}, bf16[1168,128]{1,0:T(8,128)(2,1)S(1)}, u32[]{:S(2)}, u32[]{:S(2)}) collective-permute-start(bf16[1168,128]{1,0:T(8,128)(2,1)S(1)} %get-tuple-element.42), channel_id=1, source_target_pairs={{0,16},{4,20},{8,24},{12,28},{16,0},{20,4},{24,8},{28,12},{1,17},{... | collective-permute-start | bytes 897032 | tf_op jit(solution)/shard_map/ppermute | solution.py:523
  12.0 13.0 %collective-permute-start.8 = (bf16[1168,128]{1,0:T(8,128)(2,1)S(1)}, bf16[1168,128]{1,0:T(8,128)(2,1)S(1)}, u32[]{:S(2)}, u32[]{:S(2)}) collective-permute-start(bf16[1168,128]{1,0:T(8,128)(2,1)S(1)} %get-tuple-element.43), channel_id=1, source_target_pairs={{0,24},{4,28},{8,16},{12,20},{16,8},{20,12},{24,0},{28,4},{1,25},{... | collective-permute-start | bytes 897032 | tf_op jit(solution)/shard_map/ppermute | solution.py:523
  14.0 6.4 %collective-permute-start.5 = (bf16[48,896]{1,0:T(8,128)(2,1)S(1)}, bf16[48,896]{1,0:T(8,128)(2,1)S(1)}, u32[]{:S(2)}, u32[]{:S(2)}) collective-permute-start(bf16[48,896]{1,0:T(8,128)(2,1)S(1)} %get-tuple-element.33), channel_id=1, source_target_pairs={{0,1},{1,2},{2,3},{4,5},{5,6},{6,7},{8,9},{9,10},{10,11},{12,13},{... | collective-permute-start | bytes 258056 | tf_op jit(solution)/shard_map/ppermute | solution.py:537
  17.5 6.4 %collective-permute-start.6 = (bf16[48,896]{1,0:T(8,128)(2,1)S(1)}, bf16[48,896]{1,0:T(8,128)(2,1)S(1)}, u32[]{:S(2)}, u32[]{:S(2)}) collective-permute-start(bf16[48,896]{1,0:T(8,128)(2,1)S(1)} %get-tuple-element.34), channel_id=1, source_target_pairs={{1,0},{2,1},{3,2},{5,4},{6,5},{7,6},{9,8},{10,9},{11,10},{13,12},{... | collective-permute-start | bytes 258056 | tf_op jit(solution)/shard_map/ppermute | solution.py:538
  24.8 17.7 %copy-start.6 = (bf16[64,32]{0,1:T(8,128)(2,1)S(1)}, bf16[64,32]{0,1:T(8,128)(2,1)}, u32[]{:S(2)}) copy-start(bf16[64,32]{0,1:T(8,128)(2,1)} %param.13) | copy-start | bytes 12292
  26.6 14.3 %collective-permute-start.11 = (bf16[1168,128]{1,0:T(8,128)(2,1)S(1)}, bf16[1168,128]{1,0:T(8,128)(2,1)S(1)}, u32[]{:S(2)}, u32[]{:S(2)}) collective-permute-start(bf16[1168,128]{1,0:T(8,128)(2,1)S(1)} %shard_map.78.rest_0_), channel_id=1, source_target_pairs={{0,2},{1,3},{2,0},{3,1},{4,6},{5,7},{6,4},{7,5},{8,10},{9,11},{10,... | collective-permute-start | bytes 897032 | tf_op jit(solution)/shard_map/ppermute | solution.py:564
  29.3 11.8 %collective-permute-start.12 = (bf16[1168,128]{1,0:T(8,128)(2,1)S(1)}, bf16[1168,128]{1,0:T(8,128)(2,1)S(1)}, u32[]{:S(2)}, u32[]{:S(2)}) collective-permute-start(bf16[1168,128]{1,0:T(8,128)(2,1)S(1)} %shard_map.78.rest_0_), channel_id=1, source_target_pairs={{0,1},{1,0},{2,3},{3,2},{4,5},{5,4},{6,7},{7,6},{8,9},{9,8},{10,11... | collective-permute-start | bytes 897032 | tf_op jit(solution)/shard_map/ppermute | solution.py:564
  30.8 13.4 %collective-permute-start.10 = (bf16[16,11648]{1,0:T(8,128)(2,1)}, bf16[16,11648]{1,0:T(8,128)(2,1)S(1)}, u32[]{:S(2)}, u32[]{:S(2)}) collective-permute-start(bf16[16,11648]{1,0:T(8,128)(2,1)} %get-tuple-element.47), channel_id=1, source_target_pairs={{4,0},{8,4},{12,8},{16,12},{20,16},{24,20},{28,24},{5,1},{9,5},{13... | collective-permute-start | bytes 1118216 | tf_op jit(solution)/shard_map/ppermute | solution.py:578
  32.1 12.1 %collective-permute-start.9 = (bf16[16,11648]{1,0:T(8,128)(2,1)}, bf16[16,11648]{1,0:T(8,128)(2,1)S(1)}, u32[]{:S(2)}, u32[]{:S(2)}) collective-permute-start(bf16[16,11648]{1,0:T(8,128)(2,1)} %get-tuple-element.46), channel_id=1, source_target_pairs={{0,4},{4,8},{8,12},{12,16},{16,20},{20,24},{24,28},{1,5},{5,9},{9,... | collective-permute-start | bytes 1118216 | tf_op jit(solution)/shard_map/ppermute | solution.py:577
  41.1 7.7 %collective-permute-start.13 = (bf16[1168,128]{1,0:T(8,128)(2,1)S(1)}, bf16[1168,128]{1,0:T(8,128)(2,1)S(1)}, u32[]{:S(2)}, u32[]{:S(2)}) collective-permute-start(bf16[1168,128]{1,0:T(8,128)(2,1)S(1)} %broadcast_select_fusion), channel_id=1, source_target_pairs={{0,2},{3,1},{1,0},{2,3},{4,6},{7,5},{5,4},{6,7},{8,10},{11,9},{9,8... | collective-permute-start | bytes 897032 | tf_op jit(solution)/shard_map/ppermute | solution.py:571
